TPU v7x, 512 devices: a whole 4x8x8 slice. The times are simulated.
512 devices in a mesh: region: 64 (over x, z, core), seg: 8 (over y).
Axes of the slice: x: 4, y: 8, z: 8, core: 2. Of those that a mesh axis runs over, the one named last changes fastest.
Arguments:
- image_start: bfloat16 [1024, 64, 128], P('region'), may hold values from 0 to 1
- tiles: bfloat16 [8, 64, 32, 128, 128], P('seg', 'region'), may hold values from -0.088378906 to 0.088378906
- tile_list: int32 [8, 64, 32, 3], P('seg', 'region'), may hold values from 0 to 63, as said below
- recv_map: int32 [8, 64, 64, 2], P('seg', 'region'), may hold values from 0 to 7
- sinogram: bfloat16 [8, 512, 64, 128], P('seg', 'region'), may hold values from -3 to 3
- weights: bfloat16 [8, 512, 64, 128], P('seg', 'region'), may hold values from 0.25 to 1
Outputs:
- image: bfloat16 [1024, 64, 128], P('region')
Inputs may be any that keep to these rules, and one draw needn't show every extreme that they name: `tile_list`: column 0 is a region index below 64, column 1 a slot below 2, column 2 a voxel tile below 16; each bound is reached on every device.
All inputs are finite; a program needn't handle non-finite values.
Results may differ from a plain program's by a relative error of at most 0.0036.
Values may be sent and summed in bfloat16 or wider, within the bound.
No kernel may reach another device: no remote copies, remote signals or barrier semaphores. Data moves between devices by JAX's collectives and lax.ppermute only.
A program may use at most 64 MiB of HBM per device.

v0:
```python
import jax
import jax.numpy as jnp
from jax import lax
from jax.sharding import PartitionSpec as P

CAP = 2
ITERS = 2


def per_device(image_start, tiles, tile_list, recv_map, sinogram, weights):
    tile_set = tiles[0, 0]
    entries = tile_list[0, 0]
    cols = entries[:, 2]
    dest = entries[:, 0] * CAP + entries[:, 1]
    regions = lax.axis_size("region")
    owned = recv_map[0, 0].reshape(-1)
    measured = sinogram[0].astype(jnp.float32)
    ray_wts = weights[0].astype(jnp.float32)
    ray_tiles = measured.shape[0]
    vox_tiles = image_start.shape[0]
    slices = image_start.shape[1]
    width = image_start.shape[2]
    image = image_start.astype(jnp.float32)
    for step in range(ITERS):
        current = image.astype(jnp.bfloat16)
        picked = jnp.take(current, cols, axis=0)
        partial_rays = jnp.einsum(
            "isk,ijk->isj", picked, tile_set, preferred_element_type=jnp.float32
        )
        outgoing = jax.ops.segment_sum(partial_rays, dest, num_segments=regions * CAP)
        outgoing = outgoing.astype(jnp.bfloat16).reshape(regions, CAP, slices, width)
        received = lax.all_to_all(outgoing, "region", split_axis=0, concat_axis=0, tiled=True)
        ray_flat = received.reshape(-1, received.shape[2], received.shape[3])
        forward_ray_sums = jax.ops.segment_sum(
            ray_flat.astype(jnp.float32), owned, num_segments=ray_tiles
        )
        residual_rays = (ray_wts * (measured - forward_ray_sums)).astype(jnp.bfloat16)
        answer = jnp.take(residual_rays, owned, axis=0).reshape(regions, CAP, slices, width)
        returned = lax.all_to_all(answer, "region", split_axis=0, concat_axis=0, tiled=True)
        flat = returned.reshape(-1, returned.shape[2], returned.shape[3])
        per_tile = jnp.take(flat, dest, axis=0)
        terms = jnp.einsum("isj,ijk->isk", per_tile, tile_set, preferred_element_type=jnp.float32)
        grad = jax.ops.segment_sum(terms, cols, num_segments=vox_tiles)
        total = lax.psum(grad, "seg")
        image = jnp.maximum(image + total, 0.0)
    return image.astype(jnp.bfloat16)


def solution(mesh):
    return jax.shard_map(
        per_device,
        mesh=mesh,
        in_specs=(
            P("region", None, None),
            P("seg", "region", None, None, None),
            P("seg", "region", None, None),
            P("seg", "region", None, None),
            P("seg", "region", None, None),
            P("seg", "region", None, None),
        ),
        out_specs=P("region", None, None),
        check_vma=False,
    )
```

profile of v0, /device:TPU:1, one launch (start us, length us, event | category | flops | bytes accessed | tf_op | source)
XLA Modules:
  0.0 476.4 jit_solution(3631720324909671951)
XLA Ops:
  6.5 0.8 copy.11
  7.3 0.5 compare_and_fusion.2
  7.9 1.6 gather_fusion
  9.5 0.8 fusion.6
  10.3 2.5 broadcast.23.clone
  12.8 4.8 %scatter_fusion = f32[128,64,128]{2,1,0:T(8,128)} fusion(f32[128,64,128]{2,1,0:T(8,128)} %broadcast.23.clone, s32[32]{0:T(128)S(1)} %get-tuple-element.13, f32[32,64,128]{2,1,0:T(8,128)S(1)} %fusion.6), kind=kCustom, calls=%fused_computation.6 | custom fusion | flops 262144 | bytes 3145856 | tf_op jit(solution)/shard_map/scatter-add | solution.py:30
  17.6 4.0 convert_element_type.51
  21.6 15.0 %all-to-all-start = ((bf16[64,2,64,128]{3,2,1,0:T(8,128)(2,1)}), bf16[64,2,64,128]{3,2,1,0:T(8,128)(2,1)S(1)}, u32[]{:S(2)}, u32[]{:S(2)}) async-start(bf16[64,2,64,128]{3,2,1,0:T(8,128)(2,1)} %bitcast.42), calls=%async_computation | async-start | bytes 4194304 | tf_op jit(solution)/shard_map/all_to_all | solution.py:32
  36.7 0.1 copy.8
  36.8 0.1 reshape.114
  36.9 0.6 compare_and_fusion.1
  37.5 50.4 %all-to-all-done = bf16[64,2,64,128]{3,2,1,0:T(8,128)(2,1)S(1)} async-done(((bf16[64,2,64,128]{3,2,1,0:T(8,128)(2,1)}), bf16[64,2,64,128]{3,2,1,0:T(8,128)(2,1)S(1)}, u32[]{:S(2)}, u32[]{:S(2)}) %all-to-all-start) | async-done | bytes 2097184 | tf_op jit(solution)/shard_map/all_to_all | solution.py:32
  87.9 2.5 bitcast_convert_fusion.1
  90.5 0.0 copy-start.6
  90.5 13.6 %scatter_fusion.1 = f32[8,64,128]{2,1,0:T(8,128)S(1)} fusion(f32[8,64,128]{2,1,0:T(8,128)S(1)} %broadcast.22.clone, s32[128]{0:T(128)S(1)} %reshape.114, f32[128,64,128]{2,1,0:T(8,128)} %bitcast_convert_fusion.1), kind=kCustom, calls=%fused_computation.7 | custom fusion | flops 1048576 | bytes 12583424 | tf_op jit(solution)/shard_map/scatter-add | solution.py:34
  104.1 0.1 fusion.17
  104.1 1.0 gather_fusion.1
  105.1 1.6 broadcast_select_fusion.1
  106.7 5.9 %all-to-all-start.1 = ((bf16[64,2,64,128]{3,2,1,0:T(8,128)(2,1)}), bf16[64,2,64,128]{3,2,1,0:T(8,128)(2,1)S(1)}, u32[]{:S(2)}, u32[]{:S(2)}) async-start(bf16[64,2,64,128]{3,2,1,0:T(8,128)(2,1)} %bitcast.7), calls=%async_computation.1 | async-start | bytes 4194304 | tf_op jit(solution)/shard_map/all_to_all | solution.py:39
  112.7 0.0 all-reduce.3.cloned.1.call-start
  112.8 51.1 %all-to-all-done.1 = bf16[64,2,64,128]{3,2,1,0:T(8,128)(2,1)S(1)} async-done(((bf16[64,2,64,128]{3,2,1,0:T(8,128)(2,1)}), bf16[64,2,64,128]{3,2,1,0:T(8,128)(2,1)S(1)}, u32[]{:S(2)}, u32[]{:S(2)}) %all-to-all-start.1) | async-done | bytes 2097184 | tf_op jit(solution)/shard_map/all_to_all | solution.py:39
  163.9 1.4 gather_fusion.2
  165.3 1.5 fusion.4
  166.9 2.1 scatter_fusion.2
  169.1 0.8 copy-done.2
  169.8 0.0 all-reduce.3.cloned.1.call-update
  169.9 0.0 all-reduce.5.cloned.1.call-start
  169.9 70.5 %all-reduce.3.cloned.1.call-done = f32[16,64,128]{2,1,0:T(8,128)} async-done(((f32[16,64,128]{2,1,0:T(8,128)}), f32[16,64,128]{2,1,0:T(8,128)}) %all-reduce.3.cloned.1.call-update) | async-done | bytes 524304 | tf_op jit(solution)/shard_map/psum | solution.py:44
  240.4 1.1 fusion.16
  241.5 0.6 gather_fusion.3
  242.2 0.8 fusion.2
  243.0 2.5 broadcast.23
  245.5 4.8 %scatter_fusion.3 = f32[128,64,128]{2,1,0:T(8,128)} fusion(f32[128,64,128]{2,1,0:T(8,128)} %broadcast.23, s32[32]{0:T(128)S(1)} %copy-done.15, f32[32,64,128]{2,1,0:T(8,128)S(1)} %fusion.2), kind=kCustom, calls=%fused_computation.9 | custom fusion | flops 262144 | bytes 3145856 | tf_op jit(solution)/shard_map/scatter-add | solution.py:30
  250.3 2.7 convert_element_type.56
  253.0 66.9 %all_to_all.20 = bf16[64,2,64,128]{3,2,1,0:T(8,128)(2,1)S(1)} all-to-all(bf16[64,2,64,128]{3,2,1,0:T(8,128)(2,1)S(1)} %bitcast.43), channel_id=1, replica_groups=mesh['region'=64,'seg'=8] {'region'}, dimensions={0} | all-to-all | bytes 4194304 | tf_op jit(solution)/shard_map/all_to_all | solution.py:32
  319.9 2.5 bitcast_convert_fusion
  322.5 13.6 %scatter_fusion.4 = f32[8,64,128]{2,1,0:T(8,128)S(1)} fusion(f32[8,64,128]{2,1,0:T(8,128)S(1)} %broadcast.22, s32[128]{0:T(128)S(1)} %copy-done.11, f32[128,64,128]{2,1,0:T(8,128)} %bitcast_convert_fusion), kind=kCustom, calls=%fused_computation.10 | custom fusion | flops 1048576 | bytes 12583424 | tf_op jit(solution)/shard_map/scatter-add | solution.py:34
  336.1 0.1 fusion.18
  336.2 1.0 gather_fusion.4
  337.1 0.3 broadcast_select_fusion
  337.4 56.8 %all_to_all.21 = bf16[64,2,64,128]{3,2,1,0:T(8,128)(2,1)S(1)} all-to-all(bf16[64,2,64,128]{3,2,1,0:T(8,128)(2,1)S(1)} %bitcast.44), channel_id=1, replica_groups=mesh['region'=64,'seg'=8] {'region'}, dimensions={0} | all-to-all | bytes 4194304 | tf_op jit(solution)/shard_map/all_to_all | solution.py:39
  394.3 1.4 gather_fusion.5
  395.7 1.5 fusion
  397.3 2.1 scatter_fusion.5
  399.4 0.8 copy-done.1
  400.2 0.0 all-reduce.5.cloned.1.call-update
  400.2 67.5 %all-reduce.5.cloned.1.call-done = f32[16,64,128]{2,1,0:T(8,128)} async-done(((f32[16,64,128]{2,1,0:T(8,128)}), f32[16,64,128]{2,1,0:T(8,128)}) %all-reduce.5.cloned.1.call-update) | async-done | bytes 524304 | tf_op jit(solution)/shard_map/psum | solution.py:44
  467.7 1.9 maximum_convert_fusion
  (53 shorter events, 0.3 us)
Async XLA Ops:
  6.5 2.9 copy-start
  7.8 5.0 %copy-start.14 = (s32[32]{0:T(128)}, s32[32]{0:T(128)S(1)}, u32[]{:S(2)}) copy-start(s32[32]{0:T(128)S(1)} %get-tuple-element.13) | copy-start | bytes 388
  7.8 5.0 %copy-start.16 = (pred[32]{0:T(512)(128)(4,1)}, pred[32]{0:T(512)(128)(4,1)S(1)}, u32[]{:S(2)}) copy-start(pred[32]{0:T(512)(128)(4,1)S(1)} %get-tuple-element.10) | copy-start | bytes 100
  21.6 15.0 %copy-start.22 = (s32[1,1,64,2]{2,3,1,0:T(2,128)S(1)}, s32[1,1,64,2]{2,3,1,0:T(2,128)}, u32[]{:S(2)}) copy-start(s32[1,1,64,2]{2,3,1,0:T(2,128)} %param.15) | copy-start | bytes 1540
  21.6 66.3 %all-to-all-start = ((bf16[64,2,64,128]{3,2,1,0:T(8,128)(2,1)}), bf16[64,2,64,128]{3,2,1,0:T(8,128)(2,1)S(1)}, u32[]{:S(2)}, u32[]{:S(2)}) async-start(bf16[64,2,64,128]{3,2,1,0:T(8,128)(2,1)} %bitcast.42), calls=%async_computation | async-start | bytes 4194304 | tf_op jit(solution)/shard_map/all_to_all | solution.py:32
  36.9 53.6 %copy-start.10 = (s32[128]{0:T(128)}, s32[128]{0:T(128)S(1)}, u32[]{:S(2)}) copy-start(s32[128]{0:T(128)S(1)} %reshape.114) | copy-start | bytes 1540
  90.5 13.6 %copy-start.6 = (bf16[1,8,64,128]{3,2,1,0:T(8,128)(2,1)S(1)}, bf16[1,8,64,128]{3,2,1,0:T(8,128)(2,1)}, u32[]{:S(2)}) copy-start(bf16[1,8,64,128]{3,2,1,0:T(8,128)(2,1)} %param.16) | copy-start | bytes 393220
  90.5 13.6 %copy-start.8 = (bf16[1,8,64,128]{3,2,1,0:T(8,128)(2,1)S(1)}, bf16[1,8,64,128]{3,2,1,0:T(8,128)(2,1)}, u32[]{:S(2)}) copy-start(bf16[1,8,64,128]{3,2,1,0:T(8,128)(2,1)} %param.17) | copy-start | bytes 393220
  104.1 1.0 copy-start.18
  106.7 6.0 %copy-start.15 = (s32[32]{0:T(128)S(1)}, s32[32]{0:T(128)}, u32[]{:S(2)}) copy-start(s32[32]{0:T(128)} %copy-done.14) | copy-start | bytes 388
  106.7 58.6 %copy-start.12 = (pred[32]{0:T(512)(128)(4,1)S(1)}, pred[32]{0:T(512)(128)(4,1)}, u32[]{:S(2)}) copy-start(pred[32]{0:T(512)(128)(4,1)} %get-tuple-element.12) | copy-start | bytes 100
  106.7 57.2 %all-to-all-start.1 = ((bf16[64,2,64,128]{3,2,1,0:T(8,128)(2,1)}), bf16[64,2,64,128]{3,2,1,0:T(8,128)(2,1)S(1)}, u32[]{:S(2)}, u32[]{:S(2)}) async-start(bf16[64,2,64,128]{3,2,1,0:T(8,128)(2,1)} %bitcast.7), calls=%async_computation.1 | async-start | bytes 4194304 | tf_op jit(solution)/shard_map/all_to_all | solution.py:39
  112.7 127.7 %all-reduce.3.cloned.1.call-start = ((), (), s32[]{:S(2)}) async-start(), calls=%async_computation.4 | async-start | bytes 1048576 | tf_op jit(solution)/shard_map/psum | solution.py:44
  112.8 54.1 %copy-start.20 = (s32[32]{0:T(128)}, s32[32]{0:T(128)S(1)}, u32[]{:S(2)}) copy-start(s32[32]{0:T(128)S(1)} %slice_bitcast_fusion) | copy-start | bytes 388
  166.8 73.6 %copy-start.3 = (bf16[16,64,128]{2,1,0:T(8,128)(2,1)S(1)}, bf16[16,64,128]{2,1,0:T(8,128)(2,1)}, u32[]{:S(2)}) copy-start(bf16[16,64,128]{2,1,0:T(8,128)(2,1)} %param.12) | copy-start | bytes 786436
  169.0 0.8 copy-start.2
  169.0 73.1 %copy-start.17 = (pred[32]{0:T(512)(128)(4,1)S(1)}, pred[32]{0:T(512)(128)(4,1)}, u32[]{:S(2)}) copy-start(pred[32]{0:T(512)(128)(4,1)} %copy-done.16) | copy-start | bytes 100
  169.9 297.9 %all-reduce.5.cloned.1.call-start = ((), (), s32[]{:S(2)}) async-start(), calls=%async_computation.5 | async-start | bytes 1048576 | tf_op jit(solution)/shard_map/psum | solution.py:44
  319.9 2.6 copy-start.11
  322.5 13.6 %copy-start.7 = (bf16[1,8,64,128]{3,2,1,0:T(8,128)(2,1)S(1)}, bf16[1,8,64,128]{3,2,1,0:T(8,128)(2,1)}, u32[]{:S(2)}) copy-start(bf16[1,8,64,128]{3,2,1,0:T(8,128)(2,1)} %param.16) | copy-start | bytes 393220
  322.5 13.6 %copy-start.9 = (bf16[1,8,64,128]{3,2,1,0:T(8,128)(2,1)S(1)}, bf16[1,8,64,128]{3,2,1,0:T(8,128)(2,1)}, u32[]{:S(2)}) copy-start(bf16[1,8,64,128]{3,2,1,0:T(8,128)(2,1)} %param.17) | copy-start | bytes 393220
  336.2 1.0 copy-start.19
  337.4 58.3 %copy-start.13 = (pred[32]{0:T(512)(128)(4,1)S(1)}, pred[32]{0:T(512)(128)(4,1)}, u32[]{:S(2)}) copy-start(pred[32]{0:T(512)(128)(4,1)} %get-tuple-element.12) | copy-start | bytes 100
  394.3 3.0 copy-start.21
  397.2 70.5 %copy-start.4 = (bf16[16,64,128]{2,1,0:T(8,128)(2,1)S(1)}, bf16[16,64,128]{2,1,0:T(8,128)(2,1)}, u32[]{:S(2)}) copy-start(bf16[16,64,128]{2,1,0:T(8,128)(2,1)} %param.12) | copy-start | bytes 786436
  397.2 70.5 %copy-start.5 = (f32[16,64,128]{2,1,0:T(8,128)S(1)}, f32[16,64,128]{2,1,0:T(8,128)}, u32[]{:S(2)}) copy-start(f32[16,64,128]{2,1,0:T(8,128)} %all-reduce.3.cloned.1.call-done) | copy-start | bytes 1572868
  399.4 0.8 copy-start.1
Sparse Core Ops, SparseCore 0:
  170.0 70.3 all-reduce.2
  400.3 67.3 all-reduce.4
where the time goes:
time: 482 us; the launch traced here: 476 us
  waiting for transfers between devices  240 us (50%)
  blocking collectives  124 us (26%)
  other arithmetic  58.8 us (12%)
  starting transfers between devices  21.1 us (4%)
  local copies, waits for them, and re-layouts  14.7 us (3%)
  between operations  13.8 us (3%)
    psum x2, waiting for transfers between devices, per_device(): total = lax.psum(grad, 'seg')  138 us
    all_to_all x1, blocking collectives, per_device(): lax.all_to_all(outgoing, 'region', split_axis=0, concat_axis=0, tiled=True)  66.9 us
    all_to_all x1, blocking collectives, per_device(): lax.all_to_all(answer, 'region', split_axis=0, concat_axis=0, tiled=True)  56.8 us
    all_to_all x1, waiting for transfers between devices, per_device(): lax.all_to_all(answer, 'region', split_axis=0, concat_axis=0, tiled=True)  51.1 us
    all_to_all x1, waiting for transfers between devices, per_device(): lax.all_to_all(outgoing, 'region', split_axis=0, concat_axis=0, tiled=True)  50.4 us
    scatter-add x2, other arithmetic, per_device(): jax.ops.segment_sum(ray_flat.astype(jnp.float32), owned, num_segments=ray...  27.1 us
    all_to_all x1, starting transfers between devices, per_device(): lax.all_to_all(outgoing, 'region', split_axis=0, concat_axis=0, tiled=True)  15 us
  transfers between devices with their start and end apart: 4, of which 4 were waited for; matrix products, arithmetic and copies ran while one was open for 0% of the time, Pallas kernels for 0%

commit v1 on v0

v1 whole, which is shorter than its diff:
```python
import jax
import jax.numpy as jnp
from jax import lax
from jax.experimental import pallas as pl
from jax.experimental.pallas import tpu as pltpu
from jax.sharding import Mesh, PartitionSpec as P

CAP = 2
ITERS = 2
BF = jnp.bfloat16
F32 = jnp.float32
NEAR = ("x", "zl", "c")
REGION = ("x", "zh", "zl", "c")

VM = pl.BlockSpec(memory_space=pltpu.VMEM)
SM = pl.BlockSpec(memory_space=pltpu.SMEM)
PARAMS = pltpu.CompilerParams(vmem_limit_bytes=40 * 1024 * 1024)


def slot_row(entries, i):
    owner = entries[i, 0]
    near = ((owner >> 4) << 2) | (owner & 3)
    return near * 8 + ((owner >> 2) & 3) * CAP + entries[i, 1]


def project_kernel(entries, image, mat, out, prod, acc):
    n = mat.shape[0]
    for i in range(n):
        prod[i] = lax.dot_general(
            image[entries[i, 2]], mat[i], (((1,), (1,)), ((), ())), preferred_element_type=F32
        )
    out[...] = jnp.zeros_like(out)
    for i in range(n):
        acc[slot_row(entries, i)] = jnp.zeros(acc.shape[1:], F32)
    for i in range(n):
        row = slot_row(entries, i)
        acc[row] = acc[row] + prod[i]
    for i in range(n):
        row = slot_row(entries, i)
        out[row] = acc[row].astype(BF)


def project(entries, image, mat):
    n, slices, width = mat.shape[0], image.shape[1], image.shape[2]
    return pl.pallas_call(
        project_kernel,
        out_shape=jax.ShapeDtypeStruct((128, slices, width), BF),
        in_specs=[SM, VM, VM],
        out_specs=VM,
        scratch_shapes=[pltpu.VMEM((n, slices, width), F32), pltpu.VMEM((128, slices, width), F32)],
        compiler_params=PARAMS,
    )(entries, image, mat)


def near_sum_kernel(far, m0, m1, m2, m3, got, o0, o1, o2, o3, acc):
    maps, outs = (m0, m1, m2, m3), (o0, o1, o2, o3)
    zh = far[0]
    for j in range(4):
        owner = (zh + j) & 3
        m = maps[(4 - j) % 4]
        acc[...] = jnp.zeros_like(acc)
        for near in range(16):
            q = (near >> 2) * 16 + zh * 4 + (near & 3)
            for c in range(CAP):
                t = m[q * CAP + c]
                acc[t] = acc[t] + got[near * 8 + owner * CAP + c].astype(F32)
        outs[j][...] = acc[...].astype(BF)


def near_sum(far, maps, got):
    slices, width = got.shape[1:]
    one = jax.ShapeDtypeStruct((8, slices, width), BF)
    return pl.pallas_call(
        near_sum_kernel,
        out_shape=(one,) * 4,
        in_specs=[SM] * 5 + [VM],
        out_specs=(VM,) * 4,
        scratch_shapes=[pltpu.VMEM((8, slices, width), F32)],
        compiler_params=PARAMS,
    )(far, *maps, got)


def residual_kernel(p0, p1, p2, p3, sino, wts, out):
    total = (p0[...].astype(F32) + p1[...].astype(F32)) + (p2[...].astype(F32) + p3[...].astype(F32))
    out[...] = (wts[...].astype(F32) * (sino[...].astype(F32) - total)).astype(BF)


def residual(parts, sino, wts):
    return pl.pallas_call(
        residual_kernel,
        out_shape=jax.ShapeDtypeStruct(sino.shape, BF),
        in_specs=[VM] * 6,
        out_specs=VM,
        compiler_params=PARAMS,
    )(*parts, sino, wts)


def select_kernel(far, m0, m1, m2, m3, r0, r1, r2, r3, out):
    maps, res = (m0, m1, m2, m3), (r0, r1, r2, r3)
    zh = far[0]
    for j in range(4):
        owner = (zh + 4 - j) & 3
        for near in range(16):
            q = (near >> 2) * 16 + zh * 4 + (near & 3)
            for c in range(CAP):
                out[near * 8 + owner * CAP + c] = res[j][maps[j][q * CAP + c]]


def select(far, maps, res):
    slices, width = res[0].shape[1:]
    return pl.pallas_call(
        select_kernel,
        out_shape=jax.ShapeDtypeStruct((128, slices, width), BF),
        in_specs=[SM] * 5 + [VM] * 4,
        out_specs=VM,
        compiler_params=PARAMS,
    )(far, *maps, *res)


def backproject_kernel(entries, reply, mat, out, prod, acc):
    n = mat.shape[0]
    for i in range(n):
        prod[i] = jnp.dot(reply[slot_row(entries, i)], mat[i], preferred_element_type=F32)
    acc[...] = jnp.zeros_like(acc)
    for i in range(n):
        v = entries[i, 2]
        acc[v] = acc[v] + prod[i]
    out[...] = acc[...].astype(BF)


def backproject(entries, reply, mat, vox_tiles):
    n, slices, width = mat.shape[0], reply.shape[1], reply.shape[2]
    return pl.pallas_call(
        backproject_kernel,
        out_shape=jax.ShapeDtypeStruct((vox_tiles, slices, width), BF),
        in_specs=[SM, VM, VM],
        out_specs=VM,
        scratch_shapes=[pltpu.VMEM((n, slices, width), F32), pltpu.VMEM((vox_tiles, slices, width), F32)],
        compiler_params=PARAMS,
    )(entries, reply, mat)


def update_kernel(got, mine, new, spread):
    own = mine.shape[0]
    segs = got.shape[0] // own
    total = got[0:own].astype(F32)
    for s in range(1, segs):
        total = total + got[s * own : (s + 1) * own].astype(F32)
    x = jnp.maximum(mine[...] + total, 0.0)
    new[...] = x
    rounded = x.astype(BF)
    for s in range(segs):
        spread[s * own : (s + 1) * own] = rounded


def update(got, mine):
    return pl.pallas_call(
        update_kernel,
        out_shape=(jax.ShapeDtypeStruct(mine.shape, F32), jax.ShapeDtypeStruct(got.shape, BF)),
        in_specs=[VM, VM],
        out_specs=(VM, VM),
        compiler_params=PARAMS,
    )(got, mine)


def exchange(v, axes):
    return lax.all_to_all(v, axes, split_axis=0, concat_axis=0, tiled=True)


def far_send(v, j):
    return v if j == 0 else lax.ppermute(v, "zh", [(i, (i + j) % 4) for i in range(4)])


def per_device(image_start, tiles, tile_list, recv_map, sinogram, weights):
    mat = tiles[0, 0]
    entries = tile_list[0, 0]
    flat_map = recv_map[0, 0].reshape(-1)
    sino, wts = sinogram[0], weights[0]
    vox_tiles = image_start.shape[0]
    own = vox_tiles // lax.axis_size("y")
    far = lax.axis_index("zh").astype(jnp.int32).reshape(1)
    maps = [far_send(flat_map, j) for j in range(4)]
    mine = lax.dynamic_slice_in_dim(image_start, lax.axis_index("y") * own, own, 0).astype(F32)
    image = image_start
    for _ in range(ITERS):
        got = exchange(project(entries, image, mat), NEAR)
        sums = near_sum(far, maps, got)
        res = residual([far_send(sums[j], j) for j in range(4)], sino, wts)
        reply = exchange(select(far, maps, [far_send(res, j) for j in range(4)]), NEAR)
        grads = exchange(backproject(entries, reply, mat, vox_tiles), "y")
        mine, spread = update(grads, mine)
        image = exchange(spread, "y")
    return image


def solution(mesh):
    fine = Mesh(mesh.devices.reshape(4, 4, 2, 2, 8), ("x", "zh", "zl", "c", "y"))
    return jax.shard_map(
        per_device,
        mesh=fine,
        in_specs=(
            P(REGION, None, None),
            P("y", REGION, None, None, None),
            P("y", REGION, None, None),
            P("y", REGION, None, None),
            P("y", REGION, None, None),
            P("y", REGION, None, None),
        ),
        out_specs=P(REGION, None, None),
        check_vma=False,
    )
```

time: 482 us -> 301 us (0.62)
  waiting for transfers between devices: 240 us -> 67.9 us
  other arithmetic: 58.8 us -> 0.76 us
  starting transfers between devices: 21.1 us -> 73.9 us
  between operations: 13.8 us -> 0.28 us
  blocking collectives: 124 us -> 137 us
  Pallas kernels: 0 us -> 12.2 us
  local copies, waits for them, and re-layouts: 14.7 us -> 5.22 us
    psum x2 -> x0, waiting for transfers between devices: 138 us -> none  [per_device(): total = lax.psum(grad, 'seg')]
    all_to_all x2, waiting for transfers between devices: 102 us -> 9.32 us  [exchange(): return lax.all_to_all(v, axes, split_axis=0, concat_axis=0, tiled=True)]
    ppermute x0 -> x15, waiting for transfers between devices: none -> 58.6 us  [far_send(): lax.ppermute(v, 'zh', [(i, (i + j) % 4) for i in range(4)])]
    ppermute x0 -> x15, starting transfers between devices: none -> 56.6 us  [far_send(): lax.ppermute(v, 'zh', [(i, (i + j) % 4) for i in range(4)])]
    scatter-add x6 -> x0, other arithmetic: 40.9 us -> none  [the longest x2 27.1 us: per_device(): jax.ops.segment_sum(ray_flat.astype(jnp.float32), owned, num_segments=ray...]
    convert_element_type x8 -> x1, other arithmetic: 14.9 us -> 0.76 us  [per_device(): lax.dynamic_slice_in_dim(image_start, lax.axis_index('y') * own, own, 0)]
    all_to_all x2 -> x6, blocking collectives: 124 us -> 137 us  [exchange(): return lax.all_to_all(v, axes, split_axis=0, concat_axis=0, tiled=True)]
    pallas_call x0 -> x12, Pallas kernels: none -> 12.2 us  [the longest x2 3.87 us: project(): pl.pallas_call(project_kernel, out_shape=jax.ShapeDtypeStruct((128, slice...]
  transfers between devices with their start and end apart: 4 -> 17, of which waited for: 4 -> 10; matrix products, arithmetic and copies ran while one was open for 0% -> 0% of each run, Pallas kernels for 0% -> 0%
where the time goes in v1:
time: 301 us; the launch traced here: 297 us
  blocking collectives  137 us (46%)
  starting transfers between devices  73.9 us (25%)
  waiting for transfers between devices  67.9 us (23%)
  Pallas kernels  12.2 us (4%)
  local copies, waits for them, and re-layouts  5.22 us (2%)
    all_to_all x6, blocking collectives, exchange(): return lax.all_to_all(v, axes, split_axis=0, concat_axis=0, tiled=True)  137 us
    ppermute x15, waiting for transfers between devices, far_send(): lax.ppermute(v, 'zh', [(i, (i + j) % 4) for i in range(4)])  58.6 us
    ppermute x15, starting transfers between devices, far_send(): lax.ppermute(v, 'zh', [(i, (i + j) % 4) for i in range(4)])  56.6 us
    all_to_all x2, starting transfers between devices, exchange(): return lax.all_to_all(v, axes, split_axis=0, concat_axis=0, tiled=True)  17.3 us
    all_to_all x2, waiting for transfers between devices, exchange(): return lax.all_to_all(v, axes, split_axis=0, concat_axis=0, tiled=True)  9.32 us
  transfers between devices with their start and end apart: 17, of which 10 were waited for; matrix products, arithmetic and copies ran while one was open for 0% of the time, Pallas kernels for 0%

profile of v1, /device:TPU:1, one launch (start us, length us, event | category | flops | bytes accessed | tf_op | source)
XLA Modules:
  0.0 297.1 jit_solution(12173642069105045268)
XLA Ops:
  0.0 0.8 copy.17
  0.8 1.2 copy-done
  2.0 0.9 copy-done.5
  2.9 1.9 shard_map.64
  4.9 1.3 copy-done.2
  6.2 10.5 %all-to-all-start = ((bf16[128,64,128]{2,1,0:T(8,128)(2,1)}), bf16[128,64,128]{2,1,0:T(8,128)(2,1)S(1)}, u32[]{:S(2)}, u32[]{:S(2)}) async-start(bf16[128,64,128]{2,1,0:T(8,128)(2,1)} %copy-done.2), calls=%async_computation | async-start | bytes 4194304 | tf_op jit(solution)/shard_map/all_to_all | solution.py:167
  17.0 7.0 %collective-permute-start.2 = (s32[128]{0:T(128)S(1)}, s32[128]{0:T(128)S(1)}, u32[]{:S(2)}, u32[]{:S(2)}) collective-permute-start(s32[128]{0:T(128)S(1)} %reshape_squeeze.3.m0), channel_id=1, source_target_pairs={{0,96},{32,0},{64,32},{96,64},{1,97},{33,1},{65,33},{97,65},{2,98}... | collective-permute-start | bytes 1544 | tf_op jit(solution)/shard_map/ppermute | solution.py:171
  24.0 1.9 collective-permute-start.1
  26.0 4.2 %collective-permute-start = (s32[128]{0:T(128)S(1)}, s32[128]{0:T(128)S(1)}, u32[]{:S(2)}, u32[]{:S(2)}) collective-permute-start(s32[128]{0:T(128)S(1)} %reshape_squeeze.3.m0), channel_id=1, source_target_pairs={{0,32},{32,64},{64,96},{96,0},{1,33},{33,65},{65,97},{97,1},{2,34}... | collective-permute-start | bytes 1544 | tf_op jit(solution)/shard_map/ppermute | solution.py:171
  30.2 16.4 %collective-permute-done.1.m2 = s32[128]{0:T(128)S(1)} collective-permute-done((s32[128]{0:T(128)S(1)}, s32[128]{0:T(128)S(1)}, u32[]{:S(2)}, u32[]{:S(2)}) %collective-permute-start.1) | collective-permute-done | bytes 544 | tf_op jit(solution)/shard_map/ppermute | solution.py:171
  46.7 1.4 shard_map.65
  48.1 4.0 %collective-permute-start.3 = (bf16[8,64,128]{2,1,0:T(8,128)(2,1)S(1)}, bf16[8,64,128]{2,1,0:T(8,128)(2,1)S(1)}, u32[]{:S(2)}, u32[]{:S(2)}) collective-permute-start(bf16[8,64,128]{2,1,0:T(8,128)(2,1)S(1)} %get-tuple-element.17), channel_id=1, source_target_pairs={{0,32},{32,64},{64,96},{96,0},{1,33},{33,65},{65,97},{97,1},{2,34}... | collective-permute-start | bytes 393224 | tf_op jit(solution)/shard_map/ppermute | solution.py:171
  52.1 4.2 %collective-permute-start.4 = (bf16[8,64,128]{2,1,0:T(8,128)(2,1)S(1)}, bf16[8,64,128]{2,1,0:T(8,128)(2,1)S(1)}, u32[]{:S(2)}, u32[]{:S(2)}) collective-permute-start(bf16[8,64,128]{2,1,0:T(8,128)(2,1)S(1)} %get-tuple-element.18), channel_id=1, source_target_pairs={{0,64},{32,96},{64,0},{96,32},{1,65},{33,97},{65,1},{97,33},{2,66}... | collective-permute-start | bytes 393224 | tf_op jit(solution)/shard_map/ppermute | solution.py:171
  56.3 3.4 %collective-permute-start.5 = (bf16[8,64,128]{2,1,0:T(8,128)(2,1)S(1)}, bf16[8,64,128]{2,1,0:T(8,128)(2,1)S(1)}, u32[]{:S(2)}, u32[]{:S(2)}) collective-permute-start(bf16[8,64,128]{2,1,0:T(8,128)(2,1)S(1)} %get-tuple-element.19), channel_id=1, source_target_pairs={{0,96},{32,0},{64,32},{96,64},{1,97},{33,1},{65,33},{97,65},{2,98}... | collective-permute-start | bytes 393224 | tf_op jit(solution)/shard_map/ppermute | solution.py:171
  59.7 7.9 %collective-permute-done.4.p2 = bf16[8,64,128]{2,1,0:T(8,128)(2,1)S(1)} collective-permute-done((bf16[8,64,128]{2,1,0:T(8,128)(2,1)S(1)}, bf16[8,64,128]{2,1,0:T(8,128)(2,1)S(1)}, u32[]{:S(2)}, u32[]{:S(2)}) %collective-permute-start.4) | collective-permute-done | bytes 131104 | tf_op jit(solution)/shard_map/ppermute | solution.py:171
  67.6 3.4 %collective-permute-done.5.p3 = bf16[8,64,128]{2,1,0:T(8,128)(2,1)S(1)} collective-permute-done((bf16[8,64,128]{2,1,0:T(8,128)(2,1)S(1)}, bf16[8,64,128]{2,1,0:T(8,128)(2,1)S(1)}, u32[]{:S(2)}, u32[]{:S(2)}) %collective-permute-start.5) | collective-permute-done | bytes 131104 | tf_op jit(solution)/shard_map/ppermute | solution.py:171
  71.1 3.7 %collective-permute-start.8 = (bf16[8,64,128]{2,1,0:T(8,128)(2,1)S(1)}, bf16[8,64,128]{2,1,0:T(8,128)(2,1)S(1)}, u32[]{:S(2)}, u32[]{:S(2)}) collective-permute-start(bf16[8,64,128]{2,1,0:T(8,128)(2,1)S(1)} %shard_map.66.r0), channel_id=1, source_target_pairs={{0,96},{32,0},{64,32},{96,64},{1,97},{33,1},{65,33},{97,65},{2,98}... | collective-permute-start | bytes 393224 | tf_op jit(solution)/shard_map/ppermute | solution.py:171
  74.8 5.0 %collective-permute-start.7 = (bf16[8,64,128]{2,1,0:T(8,128)(2,1)S(1)}, bf16[8,64,128]{2,1,0:T(8,128)(2,1)S(1)}, u32[]{:S(2)}, u32[]{:S(2)}) collective-permute-start(bf16[8,64,128]{2,1,0:T(8,128)(2,1)S(1)} %shard_map.66.r0), channel_id=1, source_target_pairs={{0,64},{32,96},{64,0},{96,32},{1,65},{33,97},{65,1},{97,33},{2,66}... | collective-permute-start | bytes 393224 | tf_op jit(solution)/shard_map/ppermute | solution.py:171
  79.8 1.9 collective-permute-start.6
  81.8 6.8 %collective-permute-done.7.r2 = bf16[8,64,128]{2,1,0:T(8,128)(2,1)S(1)} collective-permute-done((bf16[8,64,128]{2,1,0:T(8,128)(2,1)S(1)}, bf16[8,64,128]{2,1,0:T(8,128)(2,1)S(1)}, u32[]{:S(2)}, u32[]{:S(2)}) %collective-permute-start.7) | collective-permute-done | bytes 131104 | tf_op jit(solution)/shard_map/ppermute | solution.py:171
  88.6 4.3 %collective-permute-done.6.r1 = bf16[8,64,128]{2,1,0:T(8,128)(2,1)S(1)} collective-permute-done((bf16[8,64,128]{2,1,0:T(8,128)(2,1)S(1)}, bf16[8,64,128]{2,1,0:T(8,128)(2,1)S(1)}, u32[]{:S(2)}, u32[]{:S(2)}) %collective-permute-start.6) | collective-permute-done | bytes 131104 | tf_op jit(solution)/shard_map/ppermute | solution.py:171
  92.9 0.7 shard_map.67
  93.6 31.2 %all_to_all.40.reply = bf16[128,64,128]{2,1,0:T(8,128)(2,1)S(1)} all-to-all(bf16[128,64,128]{2,1,0:T(8,128)(2,1)S(1)} %shard_map.67), channel_id=1, replica_groups=mesh['x'=4,'zh'=4,'zl'=2,'c'=2,'y'=8] {'x','zl','c'}, dimensions={0} | all-to-all | bytes 4194304 | tf_op jit(solution)/shard_map/all_to_all | solution.py:167
  124.8 1.9 shard_map.68
  126.8 6.8 %all-to-all-start.2 = ((bf16[16,64,128]{2,1,0:T(8,128)(2,1)}), bf16[16,64,128]{2,1,0:T(8,128)(2,1)S(1)}, u32[]{:S(2)}, u32[]{:S(2)}) async-start(bf16[16,64,128]{2,1,0:T(8,128)(2,1)} %shard_map.68), calls=%async_computation.2 | async-start | bytes 524288 | tf_op jit(solution)/shard_map/all_to_all | solution.py:167
  133.6 0.8 dynamic-slice_convert_fusion.mine
  134.4 9.3 %all-to-all-done.2.got = bf16[16,64,128]{2,1,0:T(8,128)(2,1)S(1)} async-done(((bf16[16,64,128]{2,1,0:T(8,128)(2,1)}), bf16[16,64,128]{2,1,0:T(8,128)(2,1)S(1)}, u32[]{:S(2)}, u32[]{:S(2)}) %all-to-all-start.2) | async-done | bytes 262176 | tf_op jit(solution)/shard_map/all_to_all | solution.py:167
  143.7 12.0 %all_to_all.41.image = bf16[16,64,128]{2,1,0:T(8,128)(2,1)S(1)} all-to-all(bf16[16,64,128]{2,1,0:T(8,128)(2,1)S(1)} %get-tuple-element.20), channel_id=1, replica_groups=mesh['x'=4,'zh'=4,'zl'=2,'c'=2,'y'=8] {'y'}, dimensions={0} | all-to-all | bytes 524288 | tf_op jit(solution)/shard_map/all_to_all | solution.py:167
  155.7 1.9 shard_map.70
  157.7 35.1 %all_to_all.42.got = bf16[128,64,128]{2,1,0:T(8,128)(2,1)S(1)} all-to-all(bf16[128,64,128]{2,1,0:T(8,128)(2,1)S(1)} %shard_map.70), channel_id=1, replica_groups=mesh['x'=4,'zh'=4,'zl'=2,'c'=2,'y'=8] {'x','zl','c'}, dimensions={0} | all-to-all | bytes 4194304 | tf_op jit(solution)/shard_map/all_to_all | solution.py:167
  192.8 1.4 shard_map.71
  194.2 2.6 collective-permute-start.9
  196.8 4.2 %collective-permute-start.10 = (bf16[8,64,128]{2,1,0:T(8,128)(2,1)S(1)}, bf16[8,64,128]{2,1,0:T(8,128)(2,1)S(1)}, u32[]{:S(2)}, u32[]{:S(2)}) collective-permute-start(bf16[8,64,128]{2,1,0:T(8,128)(2,1)S(1)} %get-tuple-element.23), channel_id=1, source_target_pairs={{0,64},{32,96},{64,0},{96,32},{1,65},{33,97},{65,1},{97,33},{2,66}... | collective-permute-start | bytes 393224 | tf_op jit(solution)/shard_map/ppermute | solution.py:171
  201.0 4.4 %collective-permute-start.11 = (bf16[8,64,128]{2,1,0:T(8,128)(2,1)S(1)}, bf16[8,64,128]{2,1,0:T(8,128)(2,1)S(1)}, u32[]{:S(2)}, u32[]{:S(2)}) collective-permute-start(bf16[8,64,128]{2,1,0:T(8,128)(2,1)S(1)} %get-tuple-element.24), channel_id=1, source_target_pairs={{0,96},{32,0},{64,32},{96,64},{1,97},{33,1},{65,33},{97,65},{2,98}... | collective-permute-start | bytes 393224 | tf_op jit(solution)/shard_map/ppermute | solution.py:171
  205.4 5.2 %collective-permute-done.10.p2 = bf16[8,64,128]{2,1,0:T(8,128)(2,1)S(1)} collective-permute-done((bf16[8,64,128]{2,1,0:T(8,128)(2,1)S(1)}, bf16[8,64,128]{2,1,0:T(8,128)(2,1)S(1)}, u32[]{:S(2)}, u32[]{:S(2)}) %collective-permute-start.10) | collective-permute-done | bytes 131104 | tf_op jit(solution)/shard_map/ppermute | solution.py:171
  210.6 5.6 %collective-permute-done.11.p3 = bf16[8,64,128]{2,1,0:T(8,128)(2,1)S(1)} collective-permute-done((bf16[8,64,128]{2,1,0:T(8,128)(2,1)S(1)}, bf16[8,64,128]{2,1,0:T(8,128)(2,1)S(1)}, u32[]{:S(2)}, u32[]{:S(2)}) %collective-permute-start.11) | collective-permute-done | bytes 131104 | tf_op jit(solution)/shard_map/ppermute | solution.py:171
  216.3 1.9 collective-permute-start.14
  218.2 4.3 %collective-permute-start.13 = (bf16[8,64,128]{2,1,0:T(8,128)(2,1)S(1)}, bf16[8,64,128]{2,1,0:T(8,128)(2,1)S(1)}, u32[]{:S(2)}, u32[]{:S(2)}) collective-permute-start(bf16[8,64,128]{2,1,0:T(8,128)(2,1)S(1)} %shard_map.72.r0), channel_id=1, source_target_pairs={{0,64},{32,96},{64,0},{96,32},{1,65},{33,97},{65,1},{97,33},{2,66}... | collective-permute-start | bytes 393224 | tf_op jit(solution)/shard_map/ppermute | solution.py:171
  222.6 3.7 %collective-permute-start.12 = (bf16[8,64,128]{2,1,0:T(8,128)(2,1)S(1)}, bf16[8,64,128]{2,1,0:T(8,128)(2,1)S(1)}, u32[]{:S(2)}, u32[]{:S(2)}) collective-permute-start(bf16[8,64,128]{2,1,0:T(8,128)(2,1)S(1)} %shard_map.72.r0), channel_id=1, source_target_pairs={{0,32},{32,64},{64,96},{96,0},{1,33},{33,65},{65,97},{97,1},{2,34}... | collective-permute-start | bytes 393224 | tf_op jit(solution)/shard_map/ppermute | solution.py:171
  226.3 1.7 collective-permute-done.13.r2
  228.0 7.3 %collective-permute-done.12.r1 = bf16[8,64,128]{2,1,0:T(8,128)(2,1)S(1)} collective-permute-done((bf16[8,64,128]{2,1,0:T(8,128)(2,1)S(1)}, bf16[8,64,128]{2,1,0:T(8,128)(2,1)S(1)}, u32[]{:S(2)}, u32[]{:S(2)}) %collective-permute-start.12) | collective-permute-done | bytes 131104 | tf_op jit(solution)/shard_map/ppermute | solution.py:171
  235.3 0.7 shard_map.73
  236.0 33.9 %all_to_all.43.reply = bf16[128,64,128]{2,1,0:T(8,128)(2,1)S(1)} all-to-all(bf16[128,64,128]{2,1,0:T(8,128)(2,1)S(1)} %shard_map.73), channel_id=1, replica_groups=mesh['x'=4,'zh'=4,'zl'=2,'c'=2,'y'=8] {'x','zl','c'}, dimensions={0} | all-to-all | bytes 4194304 | tf_op jit(solution)/shard_map/all_to_all | solution.py:167
  269.9 1.2 shard_map.74
  271.1 12.6 %all_to_all.44.got = bf16[16,64,128]{2,1,0:T(8,128)(2,1)S(1)} all-to-all(bf16[16,64,128]{2,1,0:T(8,128)(2,1)S(1)} %shard_map.74), channel_id=1, replica_groups=mesh['x'=4,'zh'=4,'zl'=2,'c'=2,'y'=8] {'y'}, dimensions={0} | all-to-all | bytes 524288 | tf_op jit(solution)/shard_map/all_to_all | solution.py:167
  283.7 0.7 shard_map.75
  284.4 12.1 %all_to_all.45 = bf16[16,64,128]{2,1,0:T(8,128)(2,1)S(1)} all-to-all(bf16[16,64,128]{2,1,0:T(8,128)(2,1)S(1)} %get-tuple-element.26), channel_id=1, replica_groups=mesh['x'=4,'zh'=4,'zl'=2,'c'=2,'y'=8] {'y'}, dimensions={0} | all-to-all | bytes 524288 | tf_op jit(solution)/shard_map/all_to_all | solution.py:167
  296.4 0.7 copy.19
  (23 shorter events, 0.5 us)
Async XLA Ops:
  0.8 1.2 copy-start
  2.0 0.9 copy-start.5
  4.9 1.3 copy-start.2
  6.2 10.5 %copy-start.6 = (s32[1,1,64,2]{2,3,1,0:T(2,128)S(1)}, s32[1,1,64,2]{2,3,1,0:T(2,128)}, u32[]{:S(2)}) copy-start(s32[1,1,64,2]{2,3,1,0:T(2,128)} %param.9) | copy-start | bytes 1540
  6.2 40.5 %all-to-all-start = ((bf16[128,64,128]{2,1,0:T(8,128)(2,1)}), bf16[128,64,128]{2,1,0:T(8,128)(2,1)S(1)}, u32[]{:S(2)}, u32[]{:S(2)}) async-start(bf16[128,64,128]{2,1,0:T(8,128)(2,1)} %copy-done.2), calls=%async_computation | async-start | bytes 4194304 | tf_op jit(solution)/shard_map/all_to_all | solution.py:167
  16.7 54.2 %copy-start.3 = (bf16[1,8,64,128]{3,2,1,0:T(8,128)(2,1)S(1)}, bf16[1,8,64,128]{3,2,1,0:T(8,128)(2,1)}, u32[]{:S(2)}) copy-start(bf16[1,8,64,128]{3,2,1,0:T(8,128)(2,1)} %param.10) | copy-start | bytes 393220
  16.8 54.2 %copy-start.4 = (bf16[1,8,64,128]{3,2,1,0:T(8,128)(2,1)S(1)}, bf16[1,8,64,128]{3,2,1,0:T(8,128)(2,1)}, u32[]{:S(2)}) copy-start(bf16[1,8,64,128]{3,2,1,0:T(8,128)(2,1)} %param.11) | copy-start | bytes 393220
  17.0 13.2 %collective-permute-start.2 = (s32[128]{0:T(128)S(1)}, s32[128]{0:T(128)S(1)}, u32[]{:S(2)}, u32[]{:S(2)}) collective-permute-start(s32[128]{0:T(128)S(1)} %reshape_squeeze.3.m0), channel_id=1, source_target_pairs={{0,96},{32,0},{64,32},{96,64},{1,97},{33,1},{65,33},{97,65},{2,98}... | collective-permute-start | bytes 1544 | tf_op jit(solution)/shard_map/ppermute | solution.py:171
  24.0 22.6 %collective-permute-start.1 = (s32[128]{0:T(128)S(1)}, s32[128]{0:T(128)S(1)}, u32[]{:S(2)}, u32[]{:S(2)}) collective-permute-start(s32[128]{0:T(128)S(1)} %reshape_squeeze.3.m0), channel_id=1, source_target_pairs={{0,64},{32,96},{64,0},{96,32},{1,65},{33,97},{65,1},{97,33},{2,66}... | collective-permute-start | bytes 1544 | tf_op jit(solution)/shard_map/ppermute | solution.py:171
  26.0 20.7 %collective-permute-start = (s32[128]{0:T(128)S(1)}, s32[128]{0:T(128)S(1)}, u32[]{:S(2)}, u32[]{:S(2)}) collective-permute-start(s32[128]{0:T(128)S(1)} %reshape_squeeze.3.m0), channel_id=1, source_target_pairs={{0,32},{32,64},{64,96},{96,0},{1,33},{33,65},{65,97},{97,1},{2,34}... | collective-permute-start | bytes 1544 | tf_op jit(solution)/shard_map/ppermute | solution.py:171
  48.1 11.6 %collective-permute-start.3 = (bf16[8,64,128]{2,1,0:T(8,128)(2,1)S(1)}, bf16[8,64,128]{2,1,0:T(8,128)(2,1)S(1)}, u32[]{:S(2)}, u32[]{:S(2)}) collective-permute-start(bf16[8,64,128]{2,1,0:T(8,128)(2,1)S(1)} %get-tuple-element.17), channel_id=1, source_target_pairs={{0,32},{32,64},{64,96},{96,0},{1,33},{33,65},{65,97},{97,1},{2,34}... | collective-permute-start | bytes 393224 | tf_op jit(solution)/shard_map/ppermute | solution.py:171
  52.1 15.5 %collective-permute-start.4 = (bf16[8,64,128]{2,1,0:T(8,128)(2,1)S(1)}, bf16[8,64,128]{2,1,0:T(8,128)(2,1)S(1)}, u32[]{:S(2)}, u32[]{:S(2)}) collective-permute-start(bf16[8,64,128]{2,1,0:T(8,128)(2,1)S(1)} %get-tuple-element.18), channel_id=1, source_target_pairs={{0,64},{32,96},{64,0},{96,32},{1,65},{33,97},{65,1},{97,33},{2,66}... | collective-permute-start | bytes 393224 | tf_op jit(solution)/shard_map/ppermute | solution.py:171
  56.3 14.7 %collective-permute-start.5 = (bf16[8,64,128]{2,1,0:T(8,128)(2,1)S(1)}, bf16[8,64,128]{2,1,0:T(8,128)(2,1)S(1)}, u32[]{:S(2)}, u32[]{:S(2)}) collective-permute-start(bf16[8,64,128]{2,1,0:T(8,128)(2,1)S(1)} %get-tuple-element.19), channel_id=1, source_target_pairs={{0,96},{32,0},{64,32},{96,64},{1,97},{33,1},{65,33},{97,65},{2,98}... | collective-permute-start | bytes 393224 | tf_op jit(solution)/shard_map/ppermute | solution.py:171
  71.1 10.7 %collective-permute-start.8 = (bf16[8,64,128]{2,1,0:T(8,128)(2,1)S(1)}, bf16[8,64,128]{2,1,0:T(8,128)(2,1)S(1)}, u32[]{:S(2)}, u32[]{:S(2)}) collective-permute-start(bf16[8,64,128]{2,1,0:T(8,128)(2,1)S(1)} %shard_map.66.r0), channel_id=1, source_target_pairs={{0,96},{32,0},{64,32},{96,64},{1,97},{33,1},{65,33},{97,65},{2,98}... | collective-permute-start | bytes 393224 | tf_op jit(solution)/shard_map/ppermute | solution.py:171
  74.8 13.8 %collective-permute-start.7 = (bf16[8,64,128]{2,1,0:T(8,128)(2,1)S(1)}, bf16[8,64,128]{2,1,0:T(8,128)(2,1)S(1)}, u32[]{:S(2)}, u32[]{:S(2)}) collective-permute-start(bf16[8,64,128]{2,1,0:T(8,128)(2,1)S(1)} %shard_map.66.r0), channel_id=1, source_target_pairs={{0,64},{32,96},{64,0},{96,32},{1,65},{33,97},{65,1},{97,33},{2,66}... | collective-permute-start | bytes 393224 | tf_op jit(solution)/shard_map/ppermute | solution.py:171
  79.8 13.1 %collective-permute-start.6 = (bf16[8,64,128]{2,1,0:T(8,128)(2,1)S(1)}, bf16[8,64,128]{2,1,0:T(8,128)(2,1)S(1)}, u32[]{:S(2)}, u32[]{:S(2)}) collective-permute-start(bf16[8,64,128]{2,1,0:T(8,128)(2,1)S(1)} %shard_map.66.r0), channel_id=1, source_target_pairs={{0,32},{32,64},{64,96},{96,0},{1,33},{33,65},{65,97},{97,1},{2,34}... | collective-permute-start | bytes 393224 | tf_op jit(solution)/shard_map/ppermute | solution.py:171
  93.6 31.2 %copy-start.1 = (bf16[1,1,32,128,128]{4,3,2,1,0:T(8,128)(2,1)S(1)}, bf16[1,1,32,128,128]{4,3,2,1,0:T(8,128)(2,1)}, u32[]{:S(2)}) copy-start(bf16[1,1,32,128,128]{4,3,2,1,0:T(8,128)(2,1)} %param.7) | copy-start | bytes 3145732
  126.8 16.9 %all-to-all-start.2 = ((bf16[16,64,128]{2,1,0:T(8,128)(2,1)}), bf16[16,64,128]{2,1,0:T(8,128)(2,1)S(1)}, u32[]{:S(2)}, u32[]{:S(2)}) async-start(bf16[16,64,128]{2,1,0:T(8,128)(2,1)} %shard_map.68), calls=%async_computation.2 | async-start | bytes 524288 | tf_op jit(solution)/shard_map/all_to_all | solution.py:167
  194.2 11.3 %collective-permute-start.9 = (bf16[8,64,128]{2,1,0:T(8,128)(2,1)S(1)}, bf16[8,64,128]{2,1,0:T(8,128)(2,1)S(1)}, u32[]{:S(2)}, u32[]{:S(2)}) collective-permute-start(bf16[8,64,128]{2,1,0:T(8,128)(2,1)S(1)} %get-tuple-element.22), channel_id=1, source_target_pairs={{0,32},{32,64},{64,96},{96,0},{1,33},{33,65},{65,97},{97,1},{2,34}... | collective-permute-start | bytes 393224 | tf_op jit(solution)/shard_map/ppermute | solution.py:171
  196.8 13.8 %collective-permute-start.10 = (bf16[8,64,128]{2,1,0:T(8,128)(2,1)S(1)}, bf16[8,64,128]{2,1,0:T(8,128)(2,1)S(1)}, u32[]{:S(2)}, u32[]{:S(2)}) collective-permute-start(bf16[8,64,128]{2,1,0:T(8,128)(2,1)S(1)} %get-tuple-element.23), channel_id=1, source_target_pairs={{0,64},{32,96},{64,0},{96,32},{1,65},{33,97},{65,1},{97,33},{2,66}... | collective-permute-start | bytes 393224 | tf_op jit(solution)/shard_map/ppermute | solution.py:171
  201.0 15.2 %collective-permute-start.11 = (bf16[8,64,128]{2,1,0:T(8,128)(2,1)S(1)}, bf16[8,64,128]{2,1,0:T(8,128)(2,1)S(1)}, u32[]{:S(2)}, u32[]{:S(2)}) collective-permute-start(bf16[8,64,128]{2,1,0:T(8,128)(2,1)S(1)} %get-tuple-element.24), channel_id=1, source_target_pairs={{0,96},{32,0},{64,32},{96,64},{1,97},{33,1},{65,33},{97,65},{2,98}... | collective-permute-start | bytes 393224 | tf_op jit(solution)/shard_map/ppermute | solution.py:171
  216.3 10.0 %collective-permute-start.14 = (bf16[8,64,128]{2,1,0:T(8,128)(2,1)S(1)}, bf16[8,64,128]{2,1,0:T(8,128)(2,1)S(1)}, u32[]{:S(2)}, u32[]{:S(2)}) collective-permute-start(bf16[8,64,128]{2,1,0:T(8,128)(2,1)S(1)} %shard_map.72.r0), channel_id=1, source_target_pairs={{0,96},{32,0},{64,32},{96,64},{1,97},{33,1},{65,33},{97,65},{2,98}... | collective-permute-start | bytes 393224 | tf_op jit(solution)/shard_map/ppermute | solution.py:171
  218.2 9.7 %collective-permute-start.13 = (bf16[8,64,128]{2,1,0:T(8,128)(2,1)S(1)}, bf16[8,64,128]{2,1,0:T(8,128)(2,1)S(1)}, u32[]{:S(2)}, u32[]{:S(2)}) collective-permute-start(bf16[8,64,128]{2,1,0:T(8,128)(2,1)S(1)} %shard_map.72.r0), channel_id=1, source_target_pairs={{0,64},{32,96},{64,0},{96,32},{1,65},{33,97},{65,1},{97,33},{2,66}... | collective-permute-start | bytes 393224 | tf_op jit(solution)/shard_map/ppermute | solution.py:171
  222.6 12.7 %collective-permute-start.12 = (bf16[8,64,128]{2,1,0:T(8,128)(2,1)S(1)}, bf16[8,64,128]{2,1,0:T(8,128)(2,1)S(1)}, u32[]{:S(2)}, u32[]{:S(2)}) collective-permute-start(bf16[8,64,128]{2,1,0:T(8,128)(2,1)S(1)} %shard_map.72.r0), channel_id=1, source_target_pairs={{0,32},{32,64},{64,96},{96,0},{1,33},{33,65},{65,97},{97,1},{2,34}... | collective-permute-start | bytes 393224 | tf_op jit(solution)/shard_map/ppermute | solution.py:171

commit v2 on v1

--- a/solution.py
+++ b/solution.py
@@ -52,69 +52,70 @@
     )(entries, image, mat)
 
 
-def near_sum_kernel(far, m0, m1, m2, m3, got, o0, o1, o2, o3, acc):
-    maps, outs = (m0, m1, m2, m3), (o0, o1, o2, o3)
-    zh = far[0]
-    for j in range(4):
-        owner = (zh + j) & 3
-        m = maps[(4 - j) % 4]
-        acc[...] = jnp.zeros_like(acc)
-        for near in range(16):
-            q = (near >> 2) * 16 + zh * 4 + (near & 3)
-            for c in range(CAP):
-                t = m[q * CAP + c]
-                acc[t] = acc[t] + got[near * 8 + owner * CAP + c].astype(F32)
-        outs[j][...] = acc[...].astype(BF)
-
-
-def near_sum(far, maps, got):
-    slices, width = got.shape[1:]
-    one = jax.ShapeDtypeStruct((8, slices, width), BF)
-    return pl.pallas_call(
-        near_sum_kernel,
-        out_shape=(one,) * 4,
-        in_specs=[SM] * 5 + [VM],
-        out_specs=(VM,) * 4,
-        scratch_shapes=[pltpu.VMEM((8, slices, width), F32)],
-        compiler_params=PARAMS,
-    )(far, *maps, got)
-
-
-def residual_kernel(p0, p1, p2, p3, sino, wts, out):
-    total = (p0[...].astype(F32) + p1[...].astype(F32)) + (p2[...].astype(F32) + p3[...].astype(F32))
-    out[...] = (wts[...].astype(F32) * (sino[...].astype(F32) - total)).astype(BF)
-
-
-def residual(parts, sino, wts):
-    return pl.pallas_call(
-        residual_kernel,
-        out_shape=jax.ShapeDtypeStruct(sino.shape, BF),
-        in_specs=[VM] * 6,
-        out_specs=VM,
-        compiler_params=PARAMS,
-    )(*parts, sino, wts)
-
-
-def select_kernel(far, m0, m1, m2, m3, r0, r1, r2, r3, out):
-    maps, res = (m0, m1, m2, m3), (r0, r1, r2, r3)
-    zh = far[0]
-    for j in range(4):
+def near_sum_kernel(place, m0, m1, m2, m3, got, out, acc):
+    zh = place[0]
+    acc[...] = jnp.zeros_like(acc)
+    for j, m in enumerate((m0, m1, m2, m3)):
         owner = (zh + 4 - j) & 3
         for near in range(16):
             q = (near >> 2) * 16 + zh * 4 + (near & 3)
             for c in range(CAP):
-                out[near * 8 + owner * CAP + c] = res[j][maps[j][q * CAP + c]]
-
-
-def select(far, maps, res):
-    slices, width = res[0].shape[1:]
+                t = owner * 8 + m[q * CAP + c]
+                acc[t] = acc[t] + got[near * 8 + owner * CAP + c].astype(F32)
+    out[...] = acc[...].astype(BF)
+
+
+def near_sum(place, maps, got):
+    slices, width = got.shape[1:]
+    return pl.pallas_call(
+        near_sum_kernel,
+        out_shape=jax.ShapeDtypeStruct((32, slices, width), BF),
+        in_specs=[SM] * 5 + [VM],
+        out_specs=VM,
+        scratch_shapes=[pltpu.VMEM((32, slices, width), F32)],
+        compiler_params=PARAMS,
+    )(place, *maps, got)
+
+
+def residual_kernel(parts, sino, wts, out):
+    n = sino.shape[0]
+    total = parts[0:n].astype(F32)
+    for k in range(1, 4):
+        total = total + parts[k * n : (k + 1) * n].astype(F32)
+    res = (wts[...].astype(F32) * (sino[...].astype(F32) - total)).astype(BF)
+    for k in range(4):
+        out[k * n : (k + 1) * n] = res
+
+
+def residual(parts, sino, wts):
+    return pl.pallas_call(
+        residual_kernel,
+        out_shape=jax.ShapeDtypeStruct(parts.shape, BF),
+        in_specs=[VM] * 3,
+        out_specs=VM,
+        compiler_params=PARAMS,
+    )(parts, sino, wts)
+
+
+def select_kernel(place, m0, m1, m2, m3, res, out):
+    zh = place[0]
+    for j, m in enumerate((m0, m1, m2, m3)):
+        owner = (zh + 4 - j) & 3
+        for near in range(16):
+            q = (near >> 2) * 16 + zh * 4 + (near & 3)
+            for c in range(CAP):
+                out[near * 8 + owner * CAP + c] = res[owner * 8 + m[q * CAP + c]]
+
+
+def select(place, maps, res):
+    slices, width = res.shape[1:]
     return pl.pallas_call(
         select_kernel,
         out_shape=jax.ShapeDtypeStruct((128, slices, width), BF),
-        in_specs=[SM] * 5 + [VM] * 4,
-        out_specs=VM,
-        compiler_params=PARAMS,
-    )(far, *maps, *res)
+        in_specs=[SM] * 5 + [VM],
+        out_specs=VM,
+        compiler_params=PARAMS,
+    )(place, *maps, res)
 
 
 def backproject_kernel(entries, reply, mat, out, prod, acc):
@@ -140,27 +141,31 @@
     )(entries, reply, mat)
 
 
-def update_kernel(got, mine, new, spread):
-    own = mine.shape[0]
+def update_kernel(place, got, mine, new, spread):
+    own = new.shape[0]
     segs = got.shape[0] // own
     total = got[0:own].astype(F32)
     for s in range(1, segs):
         total = total + got[s * own : (s + 1) * own].astype(F32)
-    x = jnp.maximum(mine[...] + total, 0.0)
+    at = 0 if mine.shape[0] == own else place[1]
+    x = jnp.maximum(mine[pl.ds(at, own)].astype(F32) + total, 0.0)
     new[...] = x
     rounded = x.astype(BF)
     for s in range(segs):
         spread[s * own : (s + 1) * own] = rounded
 
 
-def update(got, mine):
+def update(place, got, mine, own):
     return pl.pallas_call(
         update_kernel,
-        out_shape=(jax.ShapeDtypeStruct(mine.shape, F32), jax.ShapeDtypeStruct(got.shape, BF)),
-        in_specs=[VM, VM],
+        out_shape=(
+            jax.ShapeDtypeStruct((own,) + got.shape[1:], F32),
+            jax.ShapeDtypeStruct(got.shape, BF),
+        ),
+        in_specs=[SM, VM, VM],
         out_specs=(VM, VM),
         compiler_params=PARAMS,
-    )(got, mine)
+    )(place, got, mine)
 
 
 def exchange(v, axes):
@@ -178,17 +183,16 @@
     sino, wts = sinogram[0], weights[0]
     vox_tiles = image_start.shape[0]
     own = vox_tiles // lax.axis_size("y")
-    far = lax.axis_index("zh").astype(jnp.int32).reshape(1)
+    place = jnp.stack([lax.axis_index("zh"), lax.axis_index("y") * own]).astype(jnp.int32)
     maps = [far_send(flat_map, j) for j in range(4)]
-    mine = lax.dynamic_slice_in_dim(image_start, lax.axis_index("y") * own, own, 0).astype(F32)
-    image = image_start
+    image = mine = image_start
     for _ in range(ITERS):
         got = exchange(project(entries, image, mat), NEAR)
-        sums = near_sum(far, maps, got)
-        res = residual([far_send(sums[j], j) for j in range(4)], sino, wts)
-        reply = exchange(select(far, maps, [far_send(res, j) for j in range(4)]), NEAR)
+        parts = exchange(near_sum(place, maps, got), "zh")
+        res = exchange(residual(parts, sino, wts), "zh")
+        reply = exchange(select(place, maps, res), NEAR)
         grads = exchange(backproject(entries, reply, mat, vox_tiles), "y")
-        mine, spread = update(grads, mine)
+        mine, spread = update(place, grads, mine, own)
         image = exchange(spread, "y")
     return image
 

time: 301 us -> 288 us (0.957)
  blocking collectives: 137 us -> 226 us
  waiting for transfers between devices: 67.9 us -> 16.4 us
  starting transfers between devices: 73.9 us -> 23.7 us
    all_to_all x6 -> x11, blocking collectives: 137 us -> 226 us  [exchange(): return lax.all_to_all(v, axes, split_axis=0, concat_axis=0, tiled=True)]
    ppermute x15 -> x3, starting transfers between devices: 56.6 us -> 13.2 us  [far_send(): lax.ppermute(v, 'zh', [(i, (i + j) % 4) for i in range(4)])]
    ppermute x15 -> x3, waiting for transfers between devices: 58.6 us -> 16.4 us  [far_send(): lax.ppermute(v, 'zh', [(i, (i + j) % 4) for i in range(4)])]
    all_to_all x2 -> x1, waiting for transfers between devices: 9.32 us -> 0.01 us  [exchange(): return lax.all_to_all(v, axes, split_axis=0, concat_axis=0, tiled=True)]
    all_to_all x2 -> x1, starting transfers between devices: 17.3 us -> 10.5 us  [exchange(): return lax.all_to_all(v, axes, split_axis=0, concat_axis=0, tiled=True)]
  transfers between devices with their start and end apart: 17 -> 4, of which waited for: 10 -> 1; matrix products, arithmetic and copies ran while one was open for 0% -> 0% of each run, Pallas kernels for 0% -> 0%
where the time goes in v2:
time: 288 us; the launch traced here: 284 us
  blocking collectives  226 us (78%)
  starting transfers between devices  23.7 us (8%)
  waiting for transfers between devices  16.4 us (6%)
  Pallas kernels  12.7 us (4%)
  local copies, waits for them, and re-layouts  5.23 us (2%)
    all_to_all x11, blocking collectives, exchange(): return lax.all_to_all(v, axes, split_axis=0, concat_axis=0, tiled=True)  226 us
    ppermute x3, waiting for transfers between devices, far_send(): lax.ppermute(v, 'zh', [(i, (i + j) % 4) for i in range(4)])  16.4 us
    ppermute x3, starting transfers between devices, far_send(): lax.ppermute(v, 'zh', [(i, (i + j) % 4) for i in range(4)])  13.2 us
    all_to_all x1, starting transfers between devices, exchange(): return lax.all_to_all(v, axes, split_axis=0, concat_axis=0, tiled=True)  10.5 us
  transfers between devices with their start and end apart: 4, of which 1 were waited for; matrix products, arithmetic and copies ran while one was open for 0% of the time, Pallas kernels for 0%

profile of v2, /device:TPU:1, one launch (start us, length us, event | category | flops | bytes accessed | tf_op | source)
XLA Modules:
  0.0 284.1 jit_solution(10931291623122138766)
XLA Ops:
  0.0 0.8 copy.17
  0.8 1.2 copy-done
  2.0 0.9 copy-done.3
  2.9 1.9 shard_map.64
  4.9 0.0 copy-start.2
  4.9 1.3 copy-done.2
  6.2 10.5 %all-to-all-start = ((bf16[128,64,128]{2,1,0:T(8,128)(2,1)}), bf16[128,64,128]{2,1,0:T(8,128)(2,1)S(1)}, u32[]{:S(2)}, u32[]{:S(2)}) async-start(bf16[128,64,128]{2,1,0:T(8,128)(2,1)} %copy-done.2), calls=%async_computation | async-start | bytes 4194304 | tf_op jit(solution)/shard_map/all_to_all | solution.py:172
  16.7 0.0 copy-done.7
  16.7 0.0 copy-start.5
  16.8 0.0 copy-start.6
  16.8 0.1 copy.12
  16.9 0.1 reshape_squeeze.3.m0
  17.0 7.0 %collective-permute-start.2 = (s32[128]{0:T(128)S(1)}, s32[128]{0:T(128)S(1)}, u32[]{:S(2)}, u32[]{:S(2)}) collective-permute-start(s32[128]{0:T(128)S(1)} %reshape_squeeze.3.m0), channel_id=1, source_target_pairs={{0,96},{32,0},{64,32},{96,64},{1,97},{33,1},{65,33},{97,65},{2,98}... | collective-permute-start | bytes 1544 | tf_op jit(solution)/shard_map/ppermute | solution.py:176
  24.0 1.9 collective-permute-start.1
  26.0 4.2 %collective-permute-start = (s32[128]{0:T(128)S(1)}, s32[128]{0:T(128)S(1)}, u32[]{:S(2)}, u32[]{:S(2)}) collective-permute-start(s32[128]{0:T(128)S(1)} %reshape_squeeze.3.m0), channel_id=1, source_target_pairs={{0,32},{32,64},{64,96},{96,0},{1,33},{33,65},{65,97},{97,1},{2,34}... | collective-permute-start | bytes 1544 | tf_op jit(solution)/shard_map/ppermute | solution.py:176
  30.2 0.1 pad_add_fusion.place
  30.3 0.0 collective-permute-done.2.m3
  30.3 16.4 %collective-permute-done.1.m2 = s32[128]{0:T(128)S(1)} collective-permute-done((s32[128]{0:T(128)S(1)}, s32[128]{0:T(128)S(1)}, u32[]{:S(2)}, u32[]{:S(2)}) %collective-permute-start.1) | collective-permute-done | bytes 544 | tf_op jit(solution)/shard_map/ppermute | solution.py:176
  46.7 0.0 collective-permute-done.m1
  46.7 0.0 all-to-all-done.got
  46.7 1.4 shard_map.65
  48.1 16.7 %all_to_all.60.parts = bf16[32,64,128]{2,1,0:T(8,128)(2,1)S(1)} all-to-all(bf16[32,64,128]{2,1,0:T(8,128)(2,1)S(1)} %shard_map.65), channel_id=1, replica_groups=mesh['x'=4,'zh'=4,'zl'=2,'c'=2,'y'=8] {'zh'}, dimensions={0} | all-to-all | bytes 1048576 | tf_op jit(solution)/shard_map/all_to_all | solution.py:172
  64.8 0.0 copy-done.5
  64.8 0.0 copy-done.6
  64.8 0.1 shard_map.66
  64.9 15.6 %all_to_all.61.res = bf16[32,64,128]{2,1,0:T(8,128)(2,1)S(1)} all-to-all(bf16[32,64,128]{2,1,0:T(8,128)(2,1)S(1)} %shard_map.66), channel_id=1, replica_groups=mesh['x'=4,'zh'=4,'zl'=2,'c'=2,'y'=8] {'zh'}, dimensions={0} | all-to-all | bytes 1048576 | tf_op jit(solution)/shard_map/all_to_all | solution.py:172
  80.5 0.8 shard_map.67
  81.2 0.0 copy-start.1
  81.3 37.3 %all_to_all.62.reply = bf16[128,64,128]{2,1,0:T(8,128)(2,1)S(1)} all-to-all(bf16[128,64,128]{2,1,0:T(8,128)(2,1)S(1)} %shard_map.67), channel_id=1, replica_groups=mesh['x'=4,'zh'=4,'zl'=2,'c'=2,'y'=8] {'x','zl','c'}, dimensions={0} | all-to-all | bytes 4194304 | tf_op jit(solution)/shard_map/all_to_all | solution.py:172
  118.6 0.0 copy-done.1
  118.6 1.2 shard_map.68
  119.8 16.8 %all_to_all.63.got = bf16[16,64,128]{2,1,0:T(8,128)(2,1)S(1)} all-to-all(bf16[16,64,128]{2,1,0:T(8,128)(2,1)S(1)} %shard_map.68), channel_id=1, replica_groups=mesh['x'=4,'zh'=4,'zl'=2,'c'=2,'y'=8] {'y'}, dimensions={0} | all-to-all | bytes 524288 | tf_op jit(solution)/shard_map/all_to_all | solution.py:172
  136.6 0.0 copy-done.4
  136.6 0.6 shard_map.69
  137.2 11.9 %all_to_all.64.image = bf16[16,64,128]{2,1,0:T(8,128)(2,1)S(1)} all-to-all(bf16[16,64,128]{2,1,0:T(8,128)(2,1)S(1)} %get-tuple-element.8), channel_id=1, replica_groups=mesh['x'=4,'zh'=4,'zl'=2,'c'=2,'y'=8] {'y'}, dimensions={0} | all-to-all | bytes 524288 | tf_op jit(solution)/shard_map/all_to_all | solution.py:172
  149.1 1.9 shard_map.70
  151.1 35.1 %all_to_all.65.got = bf16[128,64,128]{2,1,0:T(8,128)(2,1)S(1)} all-to-all(bf16[128,64,128]{2,1,0:T(8,128)(2,1)S(1)} %shard_map.70), channel_id=1, replica_groups=mesh['x'=4,'zh'=4,'zl'=2,'c'=2,'y'=8] {'x','zl','c'}, dimensions={0} | all-to-all | bytes 4194304 | tf_op jit(solution)/shard_map/all_to_all | solution.py:172
  186.2 1.4 shard_map.71
  187.6 15.1 %all_to_all.66.parts = bf16[32,64,128]{2,1,0:T(8,128)(2,1)S(1)} all-to-all(bf16[32,64,128]{2,1,0:T(8,128)(2,1)S(1)} %shard_map.71), channel_id=1, replica_groups=mesh['x'=4,'zh'=4,'zl'=2,'c'=2,'y'=8] {'zh'}, dimensions={0} | all-to-all | bytes 1048576 | tf_op jit(solution)/shard_map/all_to_all | solution.py:172
  202.7 0.1 shard_map.72
  202.8 15.8 %all_to_all.67.res = bf16[32,64,128]{2,1,0:T(8,128)(2,1)S(1)} all-to-all(bf16[32,64,128]{2,1,0:T(8,128)(2,1)S(1)} %shard_map.72), channel_id=1, replica_groups=mesh['x'=4,'zh'=4,'zl'=2,'c'=2,'y'=8] {'zh'}, dimensions={0} | all-to-all | bytes 1048576 | tf_op jit(solution)/shard_map/all_to_all | solution.py:172
  218.6 0.8 shard_map.73
  219.4 36.9 %all_to_all.68.reply = bf16[128,64,128]{2,1,0:T(8,128)(2,1)S(1)} all-to-all(bf16[128,64,128]{2,1,0:T(8,128)(2,1)S(1)} %shard_map.73), channel_id=1, replica_groups=mesh['x'=4,'zh'=4,'zl'=2,'c'=2,'y'=8] {'x','zl','c'}, dimensions={0} | all-to-all | bytes 4194304 | tf_op jit(solution)/shard_map/all_to_all | solution.py:172
  256.3 1.2 shard_map.74
  257.6 12.6 %all_to_all.69.got = bf16[16,64,128]{2,1,0:T(8,128)(2,1)S(1)} all-to-all(bf16[16,64,128]{2,1,0:T(8,128)(2,1)S(1)} %shard_map.74), channel_id=1, replica_groups=mesh['x'=4,'zh'=4,'zl'=2,'c'=2,'y'=8] {'y'}, dimensions={0} | all-to-all | bytes 524288 | tf_op jit(solution)/shard_map/all_to_all | solution.py:172
  270.2 1.2 shard_map.75
  271.4 12.1 %all_to_all.70 = bf16[16,64,128]{2,1,0:T(8,128)(2,1)S(1)} all-to-all(bf16[16,64,128]{2,1,0:T(8,128)(2,1)S(1)} %get-tuple-element.10), channel_id=1, replica_groups=mesh['x'=4,'zh'=4,'zl'=2,'c'=2,'y'=8] {'y'}, dimensions={0} | all-to-all | bytes 524288 | tf_op jit(solution)/shard_map/all_to_all | solution.py:172
  283.4 0.7 copy.19
  (4 shorter events, 0.0 us)
Async XLA Ops:
  0.8 1.2 copy-start
  2.0 0.9 copy-start.3
  4.9 1.3 copy-start.2
  6.2 10.5 %copy-start.7 = (s32[1,1,64,2]{2,3,1,0:T(2,128)S(1)}, s32[1,1,64,2]{2,3,1,0:T(2,128)}, u32[]{:S(2)}) copy-start(s32[1,1,64,2]{2,3,1,0:T(2,128)} %param.9) | copy-start | bytes 1540
  6.2 40.5 %all-to-all-start = ((bf16[128,64,128]{2,1,0:T(8,128)(2,1)}), bf16[128,64,128]{2,1,0:T(8,128)(2,1)S(1)}, u32[]{:S(2)}, u32[]{:S(2)}) async-start(bf16[128,64,128]{2,1,0:T(8,128)(2,1)} %copy-done.2), calls=%async_computation | async-start | bytes 4194304 | tf_op jit(solution)/shard_map/all_to_all | solution.py:172
  16.7 48.1 %copy-start.5 = (bf16[1,8,64,128]{3,2,1,0:T(8,128)(2,1)S(1)}, bf16[1,8,64,128]{3,2,1,0:T(8,128)(2,1)}, u32[]{:S(2)}) copy-start(bf16[1,8,64,128]{3,2,1,0:T(8,128)(2,1)} %param.10) | copy-start | bytes 393220
  16.8 48.1 %copy-start.6 = (bf16[1,8,64,128]{3,2,1,0:T(8,128)(2,1)S(1)}, bf16[1,8,64,128]{3,2,1,0:T(8,128)(2,1)}, u32[]{:S(2)}) copy-start(bf16[1,8,64,128]{3,2,1,0:T(8,128)(2,1)} %param.11) | copy-start | bytes 393220
  17.0 13.3 %collective-permute-start.2 = (s32[128]{0:T(128)S(1)}, s32[128]{0:T(128)S(1)}, u32[]{:S(2)}, u32[]{:S(2)}) collective-permute-start(s32[128]{0:T(128)S(1)} %reshape_squeeze.3.m0), channel_id=1, source_target_pairs={{0,96},{32,0},{64,32},{96,64},{1,97},{33,1},{65,33},{97,65},{2,98}... | collective-permute-start | bytes 1544 | tf_op jit(solution)/shard_map/ppermute | solution.py:176
  24.0 22.6 %collective-permute-start.1 = (s32[128]{0:T(128)S(1)}, s32[128]{0:T(128)S(1)}, u32[]{:S(2)}, u32[]{:S(2)}) collective-permute-start(s32[128]{0:T(128)S(1)} %reshape_squeeze.3.m0), channel_id=1, source_target_pairs={{0,64},{32,96},{64,0},{96,32},{1,65},{33,97},{65,1},{97,33},{2,66}... | collective-permute-start | bytes 1544 | tf_op jit(solution)/shard_map/ppermute | solution.py:176
  26.0 20.7 %collective-permute-start = (s32[128]{0:T(128)S(1)}, s32[128]{0:T(128)S(1)}, u32[]{:S(2)}, u32[]{:S(2)}) collective-permute-start(s32[128]{0:T(128)S(1)} %reshape_squeeze.3.m0), channel_id=1, source_target_pairs={{0,32},{32,64},{64,96},{96,0},{1,33},{33,65},{65,97},{97,1},{2,34}... | collective-permute-start | bytes 1544 | tf_op jit(solution)/shard_map/ppermute | solution.py:176
  81.2 37.3 %copy-start.1 = (bf16[1,1,32,128,128]{4,3,2,1,0:T(8,128)(2,1)S(1)}, bf16[1,1,32,128,128]{4,3,2,1,0:T(8,128)(2,1)}, u32[]{:S(2)}) copy-start(bf16[1,1,32,128,128]{4,3,2,1,0:T(8,128)(2,1)} %param.7) | copy-start | bytes 3145732
  118.6 18.0 %copy-start.4 = (bf16[16,64,128]{2,1,0:T(8,128)(2,1)S(1)}, bf16[16,64,128]{2,1,0:T(8,128)(2,1)}, u32[]{:S(2)}) copy-start(bf16[16,64,128]{2,1,0:T(8,128)(2,1)} %mine.1) | copy-start | bytes 786436

commit v3 on v2

--- a/solution.py
+++ b/solution.py
@@ -14,24 +14,28 @@
 
 VM = pl.BlockSpec(memory_space=pltpu.VMEM)
 SM = pl.BlockSpec(memory_space=pltpu.SMEM)
+BIG = pltpu.CompilerParams(vmem_limit_bytes=56 * 1024 * 1024)
 PARAMS = pltpu.CompilerParams(vmem_limit_bytes=40 * 1024 * 1024)
 
 
 def slot_row(entries, i):
-    owner = entries[i, 0]
+    owner = entries[0, 0, i]
     near = ((owner >> 4) << 2) | (owner & 3)
-    return near * 8 + ((owner >> 2) & 3) * CAP + entries[i, 1]
-
-
-def project_kernel(entries, image, mat, out, prod, acc):
-    n = mat.shape[0]
-    for i in range(n):
+    return near * 8 + ((owner >> 2) & 3) * CAP + entries[1, 0, i]
+
+
+def project_tiles(entries, image, mat, out, prod, acc, tiles):
+    share = out.shape[0] // mat.shape[0]
+    for i in tiles:
         prod[i] = lax.dot_general(
-            image[entries[i, 2]], mat[i], (((1,), (1,)), ((), ())), preferred_element_type=F32
+            image[entries[2, 0, i]], mat[i], (((1,), (1,)), ((), ())), preferred_element_type=F32
         )
-    out[...] = jnp.zeros_like(out)
-    for i in range(n):
+        out[i * share : (i + 1) * share] = jnp.zeros((share,) + out.shape[1:], BF)
         acc[slot_row(entries, i)] = jnp.zeros(acc.shape[1:], F32)
+
+
+def sum_slots(entries, out, prod, acc):
+    n = prod.shape[0]
     for i in range(n):
         row = slot_row(entries, i)
         acc[row] = acc[row] + prod[i]
@@ -40,15 +44,40 @@
         out[row] = acc[row].astype(BF)
 
 
-def project(entries, image, mat):
+def project_kernel(entries, image, mat, out, prod, acc):
+    project_tiles(entries, image, mat, out, prod, acc, range(mat.shape[0]))
+    sum_slots(entries, out, prod, acc)
+
+
+def first_project_kernel(entries, image_in, mat_in, out, prod, acc, image, mat, sem):
+    parts = sem.shape[0] - 1
+    size = mat.shape[0] // parts
+    loads = [pltpu.make_async_copy(image_in, image, sem.at[parts])]
+    for k in range(parts):
+        rows = pl.ds(k * size, size)
+        loads.append(pltpu.make_async_copy(mat_in.at[rows], mat.at[rows], sem.at[k]))
+    for load in loads:
+        load.start()
+    loads[0].wait()
+    for k in range(parts):
+        loads[1 + k].wait()
+        project_tiles(entries, image, mat, out, prod, acc, range(k * size, (k + 1) * size))
+    sum_slots(entries, out, prod, acc)
+
+
+def project(entries, image, mat, first):
     n, slices, width = mat.shape[0], image.shape[1], image.shape[2]
-    return pl.pallas_call(
-        project_kernel,
+    scratch = [pltpu.VMEM((n, slices, width), F32), pltpu.VMEM((128, slices, width), F32)]
+    if first:
+        scratch += [pltpu.VMEM(image.shape, BF), pltpu.VMEM(mat.shape, BF), pltpu.SemaphoreType.DMA((5,))]
+    far_spec = pl.BlockSpec(memory_space=pl.ANY)
+    return pl.pallas_call(
+        first_project_kernel if first else project_kernel,
         out_shape=jax.ShapeDtypeStruct((128, slices, width), BF),
-        in_specs=[SM, VM, VM],
-        out_specs=VM,
-        scratch_shapes=[pltpu.VMEM((n, slices, width), F32), pltpu.VMEM((128, slices, width), F32)],
-        compiler_params=PARAMS,
+        in_specs=[SM, far_spec, far_spec] if first else [SM, VM, VM],
+        out_specs=VM,
+        scratch_shapes=scratch,
+        compiler_params=BIG if first else PARAMS,
     )(entries, image, mat)
 
 
@@ -60,7 +89,7 @@
         for near in range(16):
             q = (near >> 2) * 16 + zh * 4 + (near & 3)
             for c in range(CAP):
-                t = owner * 8 + m[q * CAP + c]
+                t = owner * 8 + m[c, q]
                 acc[t] = acc[t] + got[near * 8 + owner * CAP + c].astype(F32)
     out[...] = acc[...].astype(BF)
 
@@ -82,15 +111,13 @@
     total = parts[0:n].astype(F32)
     for k in range(1, 4):
         total = total + parts[k * n : (k + 1) * n].astype(F32)
-    res = (wts[...].astype(F32) * (sino[...].astype(F32) - total)).astype(BF)
-    for k in range(4):
-        out[k * n : (k + 1) * n] = res
+    out[...] = (wts[...].astype(F32) * (sino[...].astype(F32) - total)).astype(BF)
 
 
 def residual(parts, sino, wts):
     return pl.pallas_call(
         residual_kernel,
-        out_shape=jax.ShapeDtypeStruct(parts.shape, BF),
+        out_shape=jax.ShapeDtypeStruct(sino.shape, BF),
         in_specs=[VM] * 3,
         out_specs=VM,
         compiler_params=PARAMS,
@@ -104,7 +131,7 @@
         for near in range(16):
             q = (near >> 2) * 16 + zh * 4 + (near & 3)
             for c in range(CAP):
-                out[near * 8 + owner * CAP + c] = res[owner * 8 + m[q * CAP + c]]
+                out[near * 8 + owner * CAP + c] = res[owner * 8 + m[c, q]]
 
 
 def select(place, maps, res):
@@ -124,7 +151,7 @@
         prod[i] = jnp.dot(reply[slot_row(entries, i)], mat[i], preferred_element_type=F32)
     acc[...] = jnp.zeros_like(acc)
     for i in range(n):
-        v = entries[i, 2]
+        v = entries[2, 0, i]
         acc[v] = acc[v] + prod[i]
     out[...] = acc[...].astype(BF)
 
@@ -141,31 +168,33 @@
     )(entries, reply, mat)
 
 
-def update_kernel(place, got, mine, new, spread):
-    own = new.shape[0]
-    segs = got.shape[0] // own
+def update_kernel(place, got, mine, spread, *new):
+    segs = lax.axis_size("y")
+    own = got.shape[0] // segs
     total = got[0:own].astype(F32)
     for s in range(1, segs):
         total = total + got[s * own : (s + 1) * own].astype(F32)
     at = 0 if mine.shape[0] == own else place[1]
     x = jnp.maximum(mine[pl.ds(at, own)].astype(F32) + total, 0.0)
-    new[...] = x
+    for ref in new:
+        ref[...] = x
     rounded = x.astype(BF)
     for s in range(segs):
         spread[s * own : (s + 1) * own] = rounded
 
 
-def update(place, got, mine, own):
-    return pl.pallas_call(
+def update(place, got, mine, own, last):
+    shapes = [jax.ShapeDtypeStruct(got.shape, BF)]
+    if not last:
+        shapes.append(jax.ShapeDtypeStruct((own,) + got.shape[1:], F32))
+    out = pl.pallas_call(
         update_kernel,
-        out_shape=(
-            jax.ShapeDtypeStruct((own,) + got.shape[1:], F32),
-            jax.ShapeDtypeStruct(got.shape, BF),
-        ),
+        out_shape=shapes,
         in_specs=[SM, VM, VM],
-        out_specs=(VM, VM),
+        out_specs=[VM] * len(shapes),
         compiler_params=PARAMS,
     )(place, got, mine)
+    return out[0], None if last else out[1]
 
 
 def exchange(v, axes):
@@ -178,21 +207,21 @@
 
 def per_device(image_start, tiles, tile_list, recv_map, sinogram, weights):
     mat = tiles[0, 0]
-    entries = tile_list[0, 0]
-    flat_map = recv_map[0, 0].reshape(-1)
+    entries = jnp.transpose(tile_list[0], (2, 0, 1))
+    own_map = recv_map[0, 0].T
     sino, wts = sinogram[0], weights[0]
     vox_tiles = image_start.shape[0]
     own = vox_tiles // lax.axis_size("y")
     place = jnp.stack([lax.axis_index("zh"), lax.axis_index("y") * own]).astype(jnp.int32)
-    maps = [far_send(flat_map, j) for j in range(4)]
+    maps = [far_send(own_map, j) for j in range(4)]
     image = mine = image_start
-    for _ in range(ITERS):
-        got = exchange(project(entries, image, mat), NEAR)
+    for step in range(ITERS):
+        got = exchange(project(entries, image, mat, step == 0), NEAR)
         parts = exchange(near_sum(place, maps, got), "zh")
-        res = exchange(residual(parts, sino, wts), "zh")
+        res = lax.all_gather(residual(parts, sino, wts), "zh", axis=0, tiled=True)
         reply = exchange(select(place, maps, res), NEAR)
         grads = exchange(backproject(entries, reply, mat, vox_tiles), "y")
-        mine, spread = update(place, grads, mine, own)
+        spread, mine = update(place, grads, mine, own, step == ITERS - 1)
         image = exchange(spread, "y")
     return image
 

time: 288 us -> 284 us (0.986)
  local copies, waits for them, and re-layouts: 5.23 us -> 0.74 us
    all_to_all x11 -> x9, blocking collectives: 226 us -> 197 us  [exchange(): return lax.all_to_all(v, axes, split_axis=0, concat_axis=0, tiled=True)]
    all_gather x0 -> x2, blocking collectives: none -> 27.6 us  [per_device(): res = lax.all_gather(residual(parts, sino, wts), 'zh', axis=0, tiled=True)]
    unnamed x18 -> x13, local copies, waits for them, and re-layouts: 4.33 us -> 0.74 us
  transfers between devices with their start and end apart: 4 -> 4, of which waited for: 1 -> 2; matrix products, arithmetic and copies ran while one was open for 0% -> 0% of each run, Pallas kernels for 0% -> 0%
where the time goes in v3:
time: 284 us; the launch traced here: 280 us
  blocking collectives  224 us (79%)
  starting transfers between devices  23.7 us (8%)
  waiting for transfers between devices  16.9 us (6%)
  Pallas kernels  14.1 us (5%)
    all_to_all x9, blocking collectives, exchange(): return lax.all_to_all(v, axes, split_axis=0, concat_axis=0, tiled=True)  197 us
    all_gather x2, blocking collectives, per_device(): res = lax.all_gather(residual(parts, sino, wts), 'zh', axis=0, tiled=True)  27.6 us
    ppermute x3, waiting for transfers between devices, far_send(): lax.ppermute(v, 'zh', [(i, (i + j) % 4) for i in range(4)])  16.9 us
    ppermute x3, starting transfers between devices, far_send(): lax.ppermute(v, 'zh', [(i, (i + j) % 4) for i in range(4)])  13.3 us
    all_to_all x1, starting transfers between devices, exchange(): return lax.all_to_all(v, axes, split_axis=0, concat_axis=0, tiled=True)  10.4 us
    pallas_call x2, Pallas kernels, project(): pl.pallas_call(first_project_kernel if first else project_kernel, out_sha...  6.21 us
  transfers between devices with their start and end apart: 4, of which 2 were waited for; matrix products, arithmetic and copies ran while one was open for 0% of the time, Pallas kernels for 0%

profile of v3, /device:TPU:1, one launch (start us, length us, event | category | flops | bytes accessed | tf_op | source)
XLA Modules:
  0.0 279.9 jit_solution(14141951187597375576)
XLA Ops:
  0.0 4.5 %shard_map.64 = bf16[128,64,128]{2,1,0:T(8,128)(2,1)} custom-call(s32[3,1,32]{2,1,0:T(1,128)} %bitcast.19, bf16[16,64,128]{2,1,0:T(8,128)(2,1)} %mine.1, bf16[32,128,128]{2,1,0:T(8,128)(2,1)} %bitcast.11), custom_call_target="tpu_custom_call" | custom-call | tf_op jit(solution)/shard_map/pallas_call | solution.py:74
  4.5 0.0 copy-start.5
  4.5 10.4 %all-to-all-start = ((bf16[128,64,128]{2,1,0:T(8,128)(2,1)}), bf16[128,64,128]{2,1,0:T(8,128)(2,1)S(1)}, u32[]{:S(2)}, u32[]{:S(2)}) async-start(bf16[128,64,128]{2,1,0:T(8,128)(2,1)} %shard_map.64), calls=%async_computation | async-start | bytes 4194304 | tf_op jit(solution)/shard_map/all_to_all | solution.py:201
  14.9 0.0 copy-start.2
  14.9 0.0 copy-start.3
  15.0 0.0 copy-done.5
  15.0 7.2 %collective-permute-start.2 = (s32[2,64]{1,0:T(2,128)S(1)}, s32[2,64]{1,0:T(2,128)S(1)}, u32[]{:S(2)}, u32[]{:S(2)}) collective-permute-start(s32[2,64]{1,0:T(2,128)S(1)} %bitcast.23), channel_id=1, source_target_pairs={{0,96},{32,0},{64,32},{96,64},{1,97},{33,1},{65,33},{97,65},{2,98}... | collective-permute-start | bytes 1544 | tf_op jit(solution)/shard_map/ppermute | solution.py:205
  22.1 1.9 collective-permute-start.1
  24.1 4.2 %collective-permute-start = (s32[2,64]{1,0:T(2,128)S(1)}, s32[2,64]{1,0:T(2,128)S(1)}, u32[]{:S(2)}, u32[]{:S(2)}) collective-permute-start(s32[2,64]{1,0:T(2,128)S(1)} %bitcast.25), channel_id=1, source_target_pairs={{0,32},{32,64},{64,96},{96,0},{1,33},{33,65},{65,97},{97,1},{2,34}... | collective-permute-start | bytes 1544 | tf_op jit(solution)/shard_map/ppermute | solution.py:205
  28.3 0.1 pad_add_fusion.place
  28.4 0.0 collective-permute-done.2.m3
  28.4 16.5 %collective-permute-done.1.m2 = s32[2,64]{1,0:T(2,128)S(1)} collective-permute-done((s32[2,64]{1,0:T(2,128)S(1)}, s32[2,64]{1,0:T(2,128)S(1)}, u32[]{:S(2)}, u32[]{:S(2)}) %collective-permute-start.1) | collective-permute-done | bytes 544 | tf_op jit(solution)/shard_map/ppermute | solution.py:205
  44.9 0.3 collective-permute-done.m1
  45.2 0.0 all-to-all-done.got
  45.2 1.4 shard_map.65
  46.7 16.5 %all_to_all.50.parts = bf16[32,64,128]{2,1,0:T(8,128)(2,1)S(1)} all-to-all(bf16[32,64,128]{2,1,0:T(8,128)(2,1)S(1)} %shard_map.65), channel_id=1, replica_groups=mesh['x'=4,'zh'=4,'zl'=2,'c'=2,'y'=8] {'zh'}, dimensions={0} | all-to-all | bytes 1048576 | tf_op jit(solution)/shard_map/all_to_all | solution.py:201
  63.1 0.0 copy-done.2
  63.1 0.0 copy-done.3
  63.1 0.1 shard_map.66
  63.2 14.0 %all_gather.6.res = bf16[32,64,128]{2,1,0:T(8,128)(2,1)S(1)} all-gather(bf16[8,64,128]{2,1,0:T(8,128)(2,1)S(1)} %shard_map.66), channel_id=1, replica_groups=mesh['x'=4,'zh'=4,'zl'=2,'c'=2,'y'=8] {'zh'}, dimensions={0}, use_global_device_ids=true | all-gather | bytes 655360 | tf_op jit(solution)/shard_map/all_gather | solution.py:221
  77.3 0.8 shard_map.67
  78.1 0.0 copy-start
  78.1 0.0 copy-start.4
  78.1 37.4 %all_to_all.51.reply = bf16[128,64,128]{2,1,0:T(8,128)(2,1)S(1)} all-to-all(bf16[128,64,128]{2,1,0:T(8,128)(2,1)S(1)} %shard_map.67), channel_id=1, replica_groups=mesh['x'=4,'zh'=4,'zl'=2,'c'=2,'y'=8] {'x','zl','c'}, dimensions={0} | all-to-all | bytes 4194304 | tf_op jit(solution)/shard_map/all_to_all | solution.py:201
  115.6 0.0 copy-done
  115.6 0.0 copy-done.4
  115.6 0.0 copy-start.1
  115.6 1.0 shard_map.68
  116.6 16.9 %all_to_all.52.got = bf16[16,64,128]{2,1,0:T(8,128)(2,1)S(1)} all-to-all(bf16[16,64,128]{2,1,0:T(8,128)(2,1)S(1)} %shard_map.68), channel_id=1, replica_groups=mesh['x'=4,'zh'=4,'zl'=2,'c'=2,'y'=8] {'y'}, dimensions={0} | all-to-all | bytes 524288 | tf_op jit(solution)/shard_map/all_to_all | solution.py:201
  133.5 0.0 copy-done.1
  133.5 0.6 shard_map.69
  134.1 12.0 %all_to_all.53.image = bf16[16,64,128]{2,1,0:T(8,128)(2,1)S(1)} all-to-all(bf16[16,64,128]{2,1,0:T(8,128)(2,1)S(1)} %get-tuple-element.7), channel_id=1, replica_groups=mesh['x'=4,'zh'=4,'zl'=2,'c'=2,'y'=8] {'y'}, dimensions={0} | all-to-all | bytes 524288 | tf_op jit(solution)/shard_map/all_to_all | solution.py:201
  146.1 1.7 shard_map.70
  147.8 35.1 %all_to_all.54.got = bf16[128,64,128]{2,1,0:T(8,128)(2,1)S(1)} all-to-all(bf16[128,64,128]{2,1,0:T(8,128)(2,1)S(1)} %shard_map.70), channel_id=1, replica_groups=mesh['x'=4,'zh'=4,'zl'=2,'c'=2,'y'=8] {'x','zl','c'}, dimensions={0} | all-to-all | bytes 4194304 | tf_op jit(solution)/shard_map/all_to_all | solution.py:201
  182.9 1.4 shard_map.71
  184.3 15.8 %all_to_all.55.parts = bf16[32,64,128]{2,1,0:T(8,128)(2,1)S(1)} all-to-all(bf16[32,64,128]{2,1,0:T(8,128)(2,1)S(1)} %shard_map.71), channel_id=1, replica_groups=mesh['x'=4,'zh'=4,'zl'=2,'c'=2,'y'=8] {'zh'}, dimensions={0} | all-to-all | bytes 1048576 | tf_op jit(solution)/shard_map/all_to_all | solution.py:201
  200.1 0.1 shard_map.72
  200.2 13.5 %all_gather.7.res = bf16[32,64,128]{2,1,0:T(8,128)(2,1)S(1)} all-gather(bf16[8,64,128]{2,1,0:T(8,128)(2,1)S(1)} %shard_map.72), channel_id=1, replica_groups=mesh['x'=4,'zh'=4,'zl'=2,'c'=2,'y'=8] {'zh'}, dimensions={0}, use_global_device_ids=true | all-gather | bytes 655360 | tf_op jit(solution)/shard_map/all_gather | solution.py:221
  213.8 0.8 shard_map.73
  214.6 38.3 %all_to_all.56.reply = bf16[128,64,128]{2,1,0:T(8,128)(2,1)S(1)} all-to-all(bf16[128,64,128]{2,1,0:T(8,128)(2,1)S(1)} %shard_map.73), channel_id=1, replica_groups=mesh['x'=4,'zh'=4,'zl'=2,'c'=2,'y'=8] {'x','zl','c'}, dimensions={0} | all-to-all | bytes 4194304 | tf_op jit(solution)/shard_map/all_to_all | solution.py:201
  252.9 1.0 shard_map.74
  253.9 12.6 %all_to_all.57.got = bf16[16,64,128]{2,1,0:T(8,128)(2,1)S(1)} all-to-all(bf16[16,64,128]{2,1,0:T(8,128)(2,1)S(1)} %shard_map.74), channel_id=1, replica_groups=mesh['x'=4,'zh'=4,'zl'=2,'c'=2,'y'=8] {'y'}, dimensions={0} | all-to-all | bytes 524288 | tf_op jit(solution)/shard_map/all_to_all | solution.py:201
  266.5 0.6 shard_map.75
  267.1 12.1 %all_to_all.58 = bf16[16,64,128]{2,1,0:T(8,128)(2,1)S(1)} all-to-all(bf16[16,64,128]{2,1,0:T(8,128)(2,1)S(1)} %shard_map.75), channel_id=1, replica_groups=mesh['x'=4,'zh'=4,'zl'=2,'c'=2,'y'=8] {'y'}, dimensions={0} | all-to-all | bytes 524288 | tf_op jit(solution)/shard_map/all_to_all | solution.py:201
  279.1 0.7 copy.8
Async XLA Ops:
  4.5 10.4 %copy-start.5 = (s32[1,1,64,2]{2,3,1,0:T(2,128)S(1)}, s32[1,1,64,2]{2,3,1,0:T(2,128)}, u32[]{:S(2)}) copy-start(s32[1,1,64,2]{2,3,1,0:T(2,128)} %param.9) | copy-start | bytes 1540
  4.5 40.7 %all-to-all-start = ((bf16[128,64,128]{2,1,0:T(8,128)(2,1)}), bf16[128,64,128]{2,1,0:T(8,128)(2,1)S(1)}, u32[]{:S(2)}, u32[]{:S(2)}) async-start(bf16[128,64,128]{2,1,0:T(8,128)(2,1)} %shard_map.64), calls=%async_computation | async-start | bytes 4194304 | tf_op jit(solution)/shard_map/all_to_all | solution.py:201
  14.9 48.2 %copy-start.2 = (bf16[1,8,64,128]{3,2,1,0:T(8,128)(2,1)S(1)}, bf16[1,8,64,128]{3,2,1,0:T(8,128)(2,1)}, u32[]{:S(2)}) copy-start(bf16[1,8,64,128]{3,2,1,0:T(8,128)(2,1)} %param.10) | copy-start | bytes 393220
  14.9 48.2 %copy-start.3 = (bf16[1,8,64,128]{3,2,1,0:T(8,128)(2,1)S(1)}, bf16[1,8,64,128]{3,2,1,0:T(8,128)(2,1)}, u32[]{:S(2)}) copy-start(bf16[1,8,64,128]{3,2,1,0:T(8,128)(2,1)} %param.11) | copy-start | bytes 393220
  15.0 13.4 %collective-permute-start.2 = (s32[2,64]{1,0:T(2,128)S(1)}, s32[2,64]{1,0:T(2,128)S(1)}, u32[]{:S(2)}, u32[]{:S(2)}) collective-permute-start(s32[2,64]{1,0:T(2,128)S(1)} %bitcast.23), channel_id=1, source_target_pairs={{0,96},{32,0},{64,32},{96,64},{1,97},{33,1},{65,33},{97,65},{2,98}... | collective-permute-start | bytes 1544 | tf_op jit(solution)/shard_map/ppermute | solution.py:205
  22.1 22.8 %collective-permute-start.1 = (s32[2,64]{1,0:T(2,128)S(1)}, s32[2,64]{1,0:T(2,128)S(1)}, u32[]{:S(2)}, u32[]{:S(2)}) collective-permute-start(s32[2,64]{1,0:T(2,128)S(1)} %bitcast.24), channel_id=1, source_target_pairs={{0,64},{32,96},{64,0},{96,32},{1,65},{33,97},{65,1},{97,33},{2,66}... | collective-permute-start | bytes 1544 | tf_op jit(solution)/shard_map/ppermute | solution.py:205
  24.1 21.2 %collective-permute-start = (s32[2,64]{1,0:T(2,128)S(1)}, s32[2,64]{1,0:T(2,128)S(1)}, u32[]{:S(2)}, u32[]{:S(2)}) collective-permute-start(s32[2,64]{1,0:T(2,128)S(1)} %bitcast.25), channel_id=1, source_target_pairs={{0,32},{32,64},{64,96},{96,0},{1,33},{33,65},{65,97},{97,1},{2,34}... | collective-permute-start | bytes 1544 | tf_op jit(solution)/shard_map/ppermute | solution.py:205
  78.1 37.5 %copy-start = (bf16[1,1,32,128,128]{4,3,2,1,0:T(8,128)(2,1)S(1)}, bf16[1,1,32,128,128]{4,3,2,1,0:T(8,128)(2,1)}, u32[]{:S(2)}) copy-start(bf16[1,1,32,128,128]{4,3,2,1,0:T(8,128)(2,1)} %param.7) | copy-start | bytes 3145732
  78.1 37.5 %copy-start.4 = (s32[1,1,32,3]{2,1,3,0:T(1,128)S(1)}, s32[1,1,32,3]{2,1,3,0:T(1,128)}, u32[]{:S(2)}) copy-start(s32[1,1,32,3]{2,1,3,0:T(1,128)} %param.8) | copy-start | bytes 1156
  115.6 17.9 %copy-start.1 = (bf16[16,64,128]{2,1,0:T(8,128)(2,1)S(1)}, bf16[16,64,128]{2,1,0:T(8,128)(2,1)}, u32[]{:S(2)}) copy-start(bf16[16,64,128]{2,1,0:T(8,128)(2,1)} %mine.1) | copy-start | bytes 786436

commit v4 on v3

--- a/solution.py
+++ b/solution.py
@@ -49,49 +49,94 @@
     sum_slots(entries, out, prod, acc)
 
 
-def first_project_kernel(entries, image_in, mat_in, out, prod, acc, image, mat, sem):
+def first_project_kernel(entries, image_in, mat_in, out, prod, acc, image, mat, rows, blank, last, sem, blank_sem, row_sem):
     parts = sem.shape[0] - 1
-    size = mat.shape[0] // parts
+    n = mat.shape[0]
+    size = n // parts
     loads = [pltpu.make_async_copy(image_in, image, sem.at[parts])]
     for k in range(parts):
-        rows = pl.ds(k * size, size)
-        loads.append(pltpu.make_async_copy(mat_in.at[rows], mat.at[rows], sem.at[k]))
+        block = pl.ds(k * size, size)
+        loads.append(pltpu.make_async_copy(mat_in.at[block], mat.at[block], sem.at[k]))
     for load in loads:
         load.start()
+    blank[...] = jnp.zeros_like(blank)
+    depth = blank.shape[0]
+    blanks = []
+    for k in range(out.shape[0] // depth):
+        blanks.append(pltpu.make_async_copy(blank, out.at[pl.ds(k * depth, depth)], blank_sem.at[k]))
+    for copy in blanks:
+        copy.start()
+    for i in range(n):
+        row = slot_row(entries, i)
+        acc[row] = jnp.zeros(acc.shape[1:], F32)
+        last[row] = i
     loads[0].wait()
     for k in range(parts):
         loads[1 + k].wait()
-        project_tiles(entries, image, mat, out, prod, acc, range(k * size, (k + 1) * size))
-    sum_slots(entries, out, prod, acc)
+        for i in range(k * size, (k + 1) * size):
+            prod[i] = lax.dot_general(
+                image[entries[2, 0, i]], mat[i], (((1,), (1,)), ((), ())), preferred_element_type=F32
+            )
+    for i in range(n):
+        row = slot_row(entries, i)
+        acc[row] = acc[row] + prod[i]
+    for copy in blanks:
+        copy.wait()
+    for i in range(n):
+        row = slot_row(entries, i)
+        rows[i] = acc[row].astype(BF)
+
+        @pl.when(last[row] == i)
+        def _():
+            pltpu.make_async_copy(rows.at[i], out.at[row], row_sem.at[i]).start()
+
+    for i in range(n):
+        row = slot_row(entries, i)
+
+        @pl.when(last[row] == i)
+        def _():
+            pltpu.make_async_copy(rows.at[i], out.at[row], row_sem.at[i]).wait()
 
 
 def project(entries, image, mat, first):
     n, slices, width = mat.shape[0], image.shape[1], image.shape[2]
     scratch = [pltpu.VMEM((n, slices, width), F32), pltpu.VMEM((128, slices, width), F32)]
     if first:
-        scratch += [pltpu.VMEM(image.shape, BF), pltpu.VMEM(mat.shape, BF), pltpu.SemaphoreType.DMA((5,))]
-    far_spec = pl.BlockSpec(memory_space=pl.ANY)
+        scratch += [
+            pltpu.VMEM(image.shape, BF),
+            pltpu.VMEM(mat.shape, BF),
+            pltpu.VMEM((n, slices, width), BF),
+            pltpu.VMEM((32, slices, width), BF),
+            pltpu.SMEM((128,), jnp.int32),
+            pltpu.SemaphoreType.DMA((5,)),
+            pltpu.SemaphoreType.DMA((4,)),
+            pltpu.SemaphoreType.DMA((n,)),
+        ]
+    loose = pl.BlockSpec(memory_space=pl.ANY)
     return pl.pallas_call(
         first_project_kernel if first else project_kernel,
         out_shape=jax.ShapeDtypeStruct((128, slices, width), BF),
-        in_specs=[SM, far_spec, far_spec] if first else [SM, VM, VM],
-        out_specs=VM,
+        in_specs=[SM, loose, loose] if first else [SM, VM, VM],
+        out_specs=loose if first else VM,
         scratch_shapes=scratch,
         compiler_params=BIG if first else PARAMS,
     )(entries, image, mat)
 
 
-def near_sum_kernel(place, m0, m1, m2, m3, got, out, acc):
+def near_sum_kernel(place, m0, m1, m2, m3, got, out, a0, a1, a2, a3):
+    maps, accs = (m0, m1, m2, m3), (a0, a1, a2, a3)
     zh = place[0]
-    acc[...] = jnp.zeros_like(acc)
-    for j, m in enumerate((m0, m1, m2, m3)):
-        owner = (zh + 4 - j) & 3
-        for near in range(16):
-            q = (near >> 2) * 16 + zh * 4 + (near & 3)
-            for c in range(CAP):
-                t = owner * 8 + m[c, q]
+    owners = [(zh + 4 - j) & 3 for j in range(4)]
+    for acc in accs:
+        acc[...] = jnp.zeros_like(acc)
+    for near in range(16):
+        q = (near >> 2) * 16 + zh * 4 + (near & 3)
+        for c in range(CAP):
+            for owner, m, acc in zip(owners, maps, accs):
+                t = m[c, q]
                 acc[t] = acc[t] + got[near * 8 + owner * CAP + c].astype(F32)
-    out[...] = acc[...].astype(BF)
+    for owner, acc in zip(owners, accs):
+        out[pl.ds(owner * 8, 8)] = acc[...].astype(BF)
 
 
 def near_sum(place, maps, got):
@@ -101,7 +146,7 @@
         out_shape=jax.ShapeDtypeStruct((32, slices, width), BF),
         in_specs=[SM] * 5 + [VM],
         out_specs=VM,
-        scratch_shapes=[pltpu.VMEM((32, slices, width), F32)],
+        scratch_shapes=[pltpu.VMEM((8, slices, width), F32)] * 4,
         compiler_params=PARAMS,
     )(place, *maps, got)
 

time: 284 us -> 283 us (level)
  no operation moved by 1% of the time
where the time goes in v4:
time: 283 us; the launch traced here: 279 us
  blocking collectives  224 us (79%)
  starting transfers between devices  23.7 us (8%)
  waiting for transfers between devices  16.9 us (6%)
  Pallas kernels  13.4 us (5%)
    all_to_all x9, blocking collectives, exchange(): return lax.all_to_all(v, axes, split_axis=0, concat_axis=0, tiled=True)  197 us
    all_gather x2, blocking collectives, per_device(): res = lax.all_gather(residual(parts, sino, wts), 'zh', axis=0, tiled=True)  26.9 us
    ppermute x3, waiting for transfers between devices, far_send(): lax.ppermute(v, 'zh', [(i, (i + j) % 4) for i in range(4)])  16.9 us
    ppermute x3, starting transfers between devices, far_send(): lax.ppermute(v, 'zh', [(i, (i + j) % 4) for i in range(4)])  13.3 us
    all_to_all x1, starting transfers between devices, exchange(): return lax.all_to_all(v, axes, split_axis=0, concat_axis=0, tiled=True)  10.4 us
    pallas_call x2, Pallas kernels, project(): pl.pallas_call(first_project_kernel if first else project_kernel, out_sha...  6.28 us
  transfers between devices with their start and end apart: 4, of which 2 were waited for; matrix products, arithmetic and copies ran while one was open for 0% of the time, Pallas kernels for 0%

profile of v4, /device:TPU:1, one launch (start us, length us, event | category | flops | bytes accessed | tf_op | source)
XLA Modules:
  0.0 278.9 jit_solution(5448558565420647425)
XLA Ops:
  0.0 4.6 %shard_map.64 = bf16[128,64,128]{2,1,0:T(8,128)(2,1)} custom-call(s32[3,1,32]{2,1,0:T(1,128)} %bitcast.19, bf16[16,64,128]{2,1,0:T(8,128)(2,1)} %mine.1, bf16[32,128,128]{2,1,0:T(8,128)(2,1)} %bitcast.11), custom_call_target="tpu_custom_call" | custom-call | tf_op jit(solution)/shard_map/pallas_call | solution.py:116
  4.6 0.0 copy-start.5
  4.6 10.4 %all-to-all-start = ((bf16[128,64,128]{2,1,0:T(8,128)(2,1)}), bf16[128,64,128]{2,1,0:T(8,128)(2,1)S(1)}, u32[]{:S(2)}, u32[]{:S(2)}) async-start(bf16[128,64,128]{2,1,0:T(8,128)(2,1)} %shard_map.64), calls=%async_computation | async-start | bytes 4194304 | tf_op jit(solution)/shard_map/all_to_all | solution.py:246
  15.0 0.0 copy-start.2
  15.0 0.0 copy-start.3
  15.0 0.0 copy-done.5
  15.1 7.1 %collective-permute-start.2 = (s32[2,64]{1,0:T(2,128)S(1)}, s32[2,64]{1,0:T(2,128)S(1)}, u32[]{:S(2)}, u32[]{:S(2)}) collective-permute-start(s32[2,64]{1,0:T(2,128)S(1)} %bitcast.23), channel_id=1, source_target_pairs={{0,96},{32,0},{64,32},{96,64},{1,97},{33,1},{65,33},{97,65},{2,98}... | collective-permute-start | bytes 1544 | tf_op jit(solution)/shard_map/ppermute | solution.py:250
  22.2 1.9 collective-permute-start.1
  24.1 4.2 %collective-permute-start = (s32[2,64]{1,0:T(2,128)S(1)}, s32[2,64]{1,0:T(2,128)S(1)}, u32[]{:S(2)}, u32[]{:S(2)}) collective-permute-start(s32[2,64]{1,0:T(2,128)S(1)} %bitcast.25), channel_id=1, source_target_pairs={{0,32},{32,64},{64,96},{96,0},{1,33},{33,65},{65,97},{97,1},{2,34}... | collective-permute-start | bytes 1544 | tf_op jit(solution)/shard_map/ppermute | solution.py:250
  28.4 0.1 pad_add_fusion.place
  28.5 0.0 collective-permute-done.2.m3
  28.5 16.5 %collective-permute-done.1.m2 = s32[2,64]{1,0:T(2,128)S(1)} collective-permute-done((s32[2,64]{1,0:T(2,128)S(1)}, s32[2,64]{1,0:T(2,128)S(1)}, u32[]{:S(2)}, u32[]{:S(2)}) %collective-permute-start.1) | collective-permute-done | bytes 544 | tf_op jit(solution)/shard_map/ppermute | solution.py:250
  45.0 0.3 collective-permute-done.m1
  45.3 0.0 all-to-all-done.got
  45.3 1.1 shard_map.65
  46.4 16.4 %all_to_all.50.parts = bf16[32,64,128]{2,1,0:T(8,128)(2,1)S(1)} all-to-all(bf16[32,64,128]{2,1,0:T(8,128)(2,1)S(1)} %shard_map.65), channel_id=1, replica_groups=mesh['x'=4,'zh'=4,'zl'=2,'c'=2,'y'=8] {'zh'}, dimensions={0} | all-to-all | bytes 1048576 | tf_op jit(solution)/shard_map/all_to_all | solution.py:246
  62.8 0.0 copy-done.2
  62.8 0.0 copy-done.3
  62.8 0.1 shard_map.66
  62.9 13.3 %all_gather.6.res = bf16[32,64,128]{2,1,0:T(8,128)(2,1)S(1)} all-gather(bf16[8,64,128]{2,1,0:T(8,128)(2,1)S(1)} %shard_map.66), channel_id=1, replica_groups=mesh['x'=4,'zh'=4,'zl'=2,'c'=2,'y'=8] {'zh'}, dimensions={0}, use_global_device_ids=true | all-gather | bytes 655360 | tf_op jit(solution)/shard_map/all_gather | solution.py:266
  76.2 0.8 shard_map.67
  77.1 0.0 copy-start
  77.1 0.0 copy-start.4
  77.1 38.2 %all_to_all.51.reply = bf16[128,64,128]{2,1,0:T(8,128)(2,1)S(1)} all-to-all(bf16[128,64,128]{2,1,0:T(8,128)(2,1)S(1)} %shard_map.67), channel_id=1, replica_groups=mesh['x'=4,'zh'=4,'zl'=2,'c'=2,'y'=8] {'x','zl','c'}, dimensions={0} | all-to-all | bytes 4194304 | tf_op jit(solution)/shard_map/all_to_all | solution.py:246
  115.3 0.0 copy-done
  115.3 0.0 copy-done.4
  115.3 0.0 copy-start.1
  115.3 1.0 shard_map.68
  116.3 16.7 %all_to_all.52.got = bf16[16,64,128]{2,1,0:T(8,128)(2,1)S(1)} all-to-all(bf16[16,64,128]{2,1,0:T(8,128)(2,1)S(1)} %shard_map.68), channel_id=1, replica_groups=mesh['x'=4,'zh'=4,'zl'=2,'c'=2,'y'=8] {'y'}, dimensions={0} | all-to-all | bytes 524288 | tf_op jit(solution)/shard_map/all_to_all | solution.py:246
  133.0 0.0 copy-done.1
  133.0 0.6 shard_map.69
  133.6 12.0 %all_to_all.53.image = bf16[16,64,128]{2,1,0:T(8,128)(2,1)S(1)} all-to-all(bf16[16,64,128]{2,1,0:T(8,128)(2,1)S(1)} %get-tuple-element.7), channel_id=1, replica_groups=mesh['x'=4,'zh'=4,'zl'=2,'c'=2,'y'=8] {'y'}, dimensions={0} | all-to-all | bytes 524288 | tf_op jit(solution)/shard_map/all_to_all | solution.py:246
  145.6 1.7 shard_map.70
  147.3 35.1 %all_to_all.54.got = bf16[128,64,128]{2,1,0:T(8,128)(2,1)S(1)} all-to-all(bf16[128,64,128]{2,1,0:T(8,128)(2,1)S(1)} %shard_map.70), channel_id=1, replica_groups=mesh['x'=4,'zh'=4,'zl'=2,'c'=2,'y'=8] {'x','zl','c'}, dimensions={0} | all-to-all | bytes 4194304 | tf_op jit(solution)/shard_map/all_to_all | solution.py:246
  182.4 1.1 shard_map.71
  183.4 15.7 %all_to_all.55.parts = bf16[32,64,128]{2,1,0:T(8,128)(2,1)S(1)} all-to-all(bf16[32,64,128]{2,1,0:T(8,128)(2,1)S(1)} %shard_map.71), channel_id=1, replica_groups=mesh['x'=4,'zh'=4,'zl'=2,'c'=2,'y'=8] {'zh'}, dimensions={0} | all-to-all | bytes 1048576 | tf_op jit(solution)/shard_map/all_to_all | solution.py:246
  199.2 0.1 shard_map.72
  199.3 13.5 %all_gather.7.res = bf16[32,64,128]{2,1,0:T(8,128)(2,1)S(1)} all-gather(bf16[8,64,128]{2,1,0:T(8,128)(2,1)S(1)} %shard_map.72), channel_id=1, replica_groups=mesh['x'=4,'zh'=4,'zl'=2,'c'=2,'y'=8] {'zh'}, dimensions={0}, use_global_device_ids=true | all-gather | bytes 655360 | tf_op jit(solution)/shard_map/all_gather | solution.py:266
  212.8 0.8 shard_map.73
  213.6 38.3 %all_to_all.56.reply = bf16[128,64,128]{2,1,0:T(8,128)(2,1)S(1)} all-to-all(bf16[128,64,128]{2,1,0:T(8,128)(2,1)S(1)} %shard_map.73), channel_id=1, replica_groups=mesh['x'=4,'zh'=4,'zl'=2,'c'=2,'y'=8] {'x','zl','c'}, dimensions={0} | all-to-all | bytes 4194304 | tf_op jit(solution)/shard_map/all_to_all | solution.py:246
  252.0 1.0 shard_map.74
  253.0 12.6 %all_to_all.57.got = bf16[16,64,128]{2,1,0:T(8,128)(2,1)S(1)} all-to-all(bf16[16,64,128]{2,1,0:T(8,128)(2,1)S(1)} %shard_map.74), channel_id=1, replica_groups=mesh['x'=4,'zh'=4,'zl'=2,'c'=2,'y'=8] {'y'}, dimensions={0} | all-to-all | bytes 524288 | tf_op jit(solution)/shard_map/all_to_all | solution.py:246
  265.5 0.6 shard_map.75
  266.1 12.1 %all_to_all.58 = bf16[16,64,128]{2,1,0:T(8,128)(2,1)S(1)} all-to-all(bf16[16,64,128]{2,1,0:T(8,128)(2,1)S(1)} %shard_map.75), channel_id=1, replica_groups=mesh['x'=4,'zh'=4,'zl'=2,'c'=2,'y'=8] {'y'}, dimensions={0} | all-to-all | bytes 524288 | tf_op jit(solution)/shard_map/all_to_all | solution.py:246
  278.2 0.7 copy.8
Async XLA Ops:
  4.6 10.5 %copy-start.5 = (s32[1,1,64,2]{2,3,1,0:T(2,128)S(1)}, s32[1,1,64,2]{2,3,1,0:T(2,128)}, u32[]{:S(2)}) copy-start(s32[1,1,64,2]{2,3,1,0:T(2,128)} %param.9) | copy-start | bytes 1540
  4.6 40.7 %all-to-all-start = ((bf16[128,64,128]{2,1,0:T(8,128)(2,1)}), bf16[128,64,128]{2,1,0:T(8,128)(2,1)S(1)}, u32[]{:S(2)}, u32[]{:S(2)}) async-start(bf16[128,64,128]{2,1,0:T(8,128)(2,1)} %shard_map.64), calls=%async_computation | async-start | bytes 4194304 | tf_op jit(solution)/shard_map/all_to_all | solution.py:246
  15.0 47.8 %copy-start.2 = (bf16[1,8,64,128]{3,2,1,0:T(8,128)(2,1)S(1)}, bf16[1,8,64,128]{3,2,1,0:T(8,128)(2,1)}, u32[]{:S(2)}) copy-start(bf16[1,8,64,128]{3,2,1,0:T(8,128)(2,1)} %param.10) | copy-start | bytes 393220
  15.0 47.8 %copy-start.3 = (bf16[1,8,64,128]{3,2,1,0:T(8,128)(2,1)S(1)}, bf16[1,8,64,128]{3,2,1,0:T(8,128)(2,1)}, u32[]{:S(2)}) copy-start(bf16[1,8,64,128]{3,2,1,0:T(8,128)(2,1)} %param.11) | copy-start | bytes 393220
  15.1 13.4 %collective-permute-start.2 = (s32[2,64]{1,0:T(2,128)S(1)}, s32[2,64]{1,0:T(2,128)S(1)}, u32[]{:S(2)}, u32[]{:S(2)}) collective-permute-start(s32[2,64]{1,0:T(2,128)S(1)} %bitcast.23), channel_id=1, source_target_pairs={{0,96},{32,0},{64,32},{96,64},{1,97},{33,1},{65,33},{97,65},{2,98}... | collective-permute-start | bytes 1544 | tf_op jit(solution)/shard_map/ppermute | solution.py:250
  22.2 22.8 %collective-permute-start.1 = (s32[2,64]{1,0:T(2,128)S(1)}, s32[2,64]{1,0:T(2,128)S(1)}, u32[]{:S(2)}, u32[]{:S(2)}) collective-permute-start(s32[2,64]{1,0:T(2,128)S(1)} %bitcast.24), channel_id=1, source_target_pairs={{0,64},{32,96},{64,0},{96,32},{1,65},{33,97},{65,1},{97,33},{2,66}... | collective-permute-start | bytes 1544 | tf_op jit(solution)/shard_map/ppermute | solution.py:250
  24.1 21.2 %collective-permute-start = (s32[2,64]{1,0:T(2,128)S(1)}, s32[2,64]{1,0:T(2,128)S(1)}, u32[]{:S(2)}, u32[]{:S(2)}) collective-permute-start(s32[2,64]{1,0:T(2,128)S(1)} %bitcast.25), channel_id=1, source_target_pairs={{0,32},{32,64},{64,96},{96,0},{1,33},{33,65},{65,97},{97,1},{2,34}... | collective-permute-start | bytes 1544 | tf_op jit(solution)/shard_map/ppermute | solution.py:250
  77.1 38.2 %copy-start = (bf16[1,1,32,128,128]{4,3,2,1,0:T(8,128)(2,1)S(1)}, bf16[1,1,32,128,128]{4,3,2,1,0:T(8,128)(2,1)}, u32[]{:S(2)}) copy-start(bf16[1,1,32,128,128]{4,3,2,1,0:T(8,128)(2,1)} %param.7) | copy-start | bytes 3145732
  77.1 38.2 %copy-start.4 = (s32[1,1,32,3]{2,1,3,0:T(1,128)S(1)}, s32[1,1,32,3]{2,1,3,0:T(1,128)}, u32[]{:S(2)}) copy-start(s32[1,1,32,3]{2,1,3,0:T(1,128)} %param.8) | copy-start | bytes 1156
  115.3 17.7 %copy-start.1 = (bf16[16,64,128]{2,1,0:T(8,128)(2,1)S(1)}, bf16[16,64,128]{2,1,0:T(8,128)(2,1)}, u32[]{:S(2)}) copy-start(bf16[16,64,128]{2,1,0:T(8,128)(2,1)} %mine.1) | copy-start | bytes 786436

commit v5 on v2

v5 whole, which is shorter than its diff:
```python
import functools

import jax
import jax.numpy as jnp
from jax import lax
from jax.experimental import pallas as pl
from jax.experimental.pallas import tpu as pltpu
from jax.sharding import Mesh, PartitionSpec as P

CAP = 2
ITERS = 2
BF = jnp.bfloat16
F32 = jnp.float32
NEAR = ("x", "zl")
REGION = ("x", "zh", "zl", "c")
ROWS = 256

VM = pl.BlockSpec(memory_space=pltpu.VMEM)
SM = pl.BlockSpec(memory_space=pltpu.SMEM)
PARAMS = pltpu.CompilerParams(vmem_limit_bytes=40 * 1024 * 1024)


def slot_row(entries, a, i):
    owner = entries[0, 0, i]
    near = ((owner >> 4) << 1) | ((owner >> 1) & 1)
    return near * 32 + a * 16 + ((owner >> 2) & 3) * 4 + (owner & 1) * CAP + entries[1, 0, i]


def half(place, slices):
    return pl.ds(pl.multiple_of(place[1] * slices, slices), slices)


def project_kernel(place, e0, e1, *refs):
    images, (m0, m1, out, prod, acc) = refs[:-5], refs[-5:]
    n, slices = m0.shape[0], out.shape[1]
    sides = ((e0, m0, place[1]), (e1, m1, 1 - place[1]))
    for side, (entries, mat, a) in enumerate(sides):
        for i in range(n):
            v = entries[2, 0, i]
            if len(images) == 2:
                x = images[side][v, half(place, slices)]
            else:
                x = images[0][v * 2 + a]
            prod[side * n + i] = lax.dot_general(x, mat[i], (((1,), (1,)), ((), ())), preferred_element_type=F32)
            acc[slot_row(entries, a, i)] = jnp.zeros(acc.shape[1:], F32)
    out[...] = jnp.zeros_like(out)
    for side, (entries, _, a) in enumerate(sides):
        for i in range(n):
            row = slot_row(entries, a, i)
            acc[row] = acc[row] + prod[side * n + i]
    for entries, _, a in sides:
        for i in range(n):
            row = slot_row(entries, a, i)
            out[row] = acc[row].astype(BF)


def project(place, entries, images, mats, slices):
    n, width = mats[0].shape[0], mats[0].shape[2]
    return pl.pallas_call(
        project_kernel,
        out_shape=jax.ShapeDtypeStruct((ROWS, slices, width), BF),
        in_specs=[SM] * 3 + [VM] * (len(images) + 2),
        out_specs=VM,
        scratch_shapes=[pltpu.VMEM((2 * n, slices, width), F32), pltpu.VMEM((ROWS, slices, width), F32)],
        compiler_params=PARAMS,
    )(place, *entries, *images, *mats)


def slot_routes(place, maps):
    zh, c = place[0], place[1]
    for near in range(8):
        for a in range(2):
            q = (near >> 1) * 16 + zh * 4 + (near & 1) * 2 + a
            for s in range(CAP):
                for j, m in enumerate(maps):
                    owner = (zh + 4 - j) & 3
                    for k in range(2):
                        b = c if k == 0 else 1 - c
                        yield near * 32 + a * 16 + owner * 4 + b * CAP + s, j, k, m[k, s, q]


def near_sum_kernel(place, m0, m1, m2, m3, got, out, *accs):
    for acc in accs:
        acc[...] = jnp.zeros_like(acc)
    for row, j, k, t in slot_routes(place, (m0, m1, m2, m3)):
        acc = accs[j * 2 + k]
        acc[t] = acc[t] + got[row].astype(F32)
    for j in range(4):
        for k in range(2):
            b = place[1] if k == 0 else 1 - place[1]
            out[pl.ds(((place[0] + 4 - j) & 3) * 16 + b * 8, 8)] = accs[j * 2 + k][...].astype(BF)


def near_sum(place, maps, got):
    slices, width = got.shape[1:]
    return pl.pallas_call(
        near_sum_kernel,
        out_shape=jax.ShapeDtypeStruct((64, slices, width), BF),
        in_specs=[SM] * 5 + [VM],
        out_specs=VM,
        scratch_shapes=[pltpu.VMEM((8, slices, width), F32)] * 8,
        compiler_params=PARAMS,
    )(place, *maps, got)


def residual_kernel(place, parts, s0, s1, w0, w1, out):
    slices = out.shape[1]
    for k, (sino, wts) in enumerate(((s0, w0), (s1, w1))):
        b = place[1] if k == 0 else 1 - place[1]
        total = parts[pl.ds(b * 8, 8)].astype(F32)
        for z in range(1, 4):
            total = total + parts[pl.ds(z * 16 + b * 8, 8)].astype(F32)
        mine = half(place, slices)
        res = wts[:, mine].astype(F32) * (sino[:, mine].astype(F32) - total)
        out[pl.ds(b * 8, 8)] = res.astype(BF)


def residual(place, parts, sinos, weights):
    return pl.pallas_call(
        residual_kernel,
        out_shape=jax.ShapeDtypeStruct((16,) + parts.shape[1:], BF),
        in_specs=[SM] + [VM] * 5,
        out_specs=VM,
        compiler_params=PARAMS,
    )(place, parts, *sinos, *weights)


def select_kernel(place, m0, m1, m2, m3, res, out):
    for row, j, k, t in slot_routes(place, (m0, m1, m2, m3)):
        b = place[1] if k == 0 else 1 - place[1]
        out[row] = res[((place[0] + 4 - j) & 3) * 16 + b * 8 + t]


def select(place, maps, res):
    slices, width = res.shape[1:]
    return pl.pallas_call(
        select_kernel,
        out_shape=jax.ShapeDtypeStruct((ROWS, slices, width), BF),
        in_specs=[SM] * 5 + [VM],
        out_specs=VM,
        compiler_params=PARAMS,
    )(place, *maps, res)


def backproject_kernel(place, e0, e1, reply, m0, m1, out, prod, acc):
    n = m0.shape[0]
    sides = ((e0, m0, place[1]), (e1, m1, 1 - place[1]))
    for side, (entries, mat, a) in enumerate(sides):
        for i in range(n):
            prod[side * n + i] = jnp.dot(reply[slot_row(entries, a, i)], mat[i], preferred_element_type=F32)
    acc[...] = jnp.zeros_like(acc)
    for side, (entries, _, a) in enumerate(sides):
        for i in range(n):
            v = entries[2, 0, i] * 2 + a
            acc[v] = acc[v] + prod[side * n + i]
    out[...] = acc[...].astype(BF)


def backproject(place, entries, reply, mats, vox_tiles):
    n, slices, width = mats[0].shape[0], reply.shape[1], reply.shape[2]
    return pl.pallas_call(
        backproject_kernel,
        out_shape=jax.ShapeDtypeStruct((2 * vox_tiles, slices, width), BF),
        in_specs=[SM] * 3 + [VM] * 3,
        out_specs=VM,
        scratch_shapes=[pltpu.VMEM((2 * n, slices, width), F32), pltpu.VMEM((2 * vox_tiles, slices, width), F32)],
        compiler_params=PARAMS,
    )(place, *entries, reply, *mats)


def update_kernel(first, last, place, got, *refs):
    olds, outs = refs[: 2 if first else 1], refs[2 if first else 1 :]
    spread = outs[0]
    segs = lax.axis_size("y")
    own, slices = got.shape[0] // segs, got.shape[1]
    total = got[0:own].astype(F32)
    for s in range(1, segs):
        total = total + got[s * own : (s + 1) * own].astype(F32)
    if first:
        state = outs[1]
        for side, old in enumerate(olds):
            a = place[1] if side == 0 else 1 - place[1]
            for k in range(own // 2):
                state[k * 2 + a] = old[place[2] + k, half(place, slices)].astype(F32)
        x = jnp.maximum(state[...] + total, 0.0)
        state[...] = x
    else:
        x = jnp.maximum(olds[0][...] + total, 0.0)
        if not last:
            outs[1][...] = x
    rounded = x.astype(BF)
    for s in range(segs):
        if last:
            for k in range(own):
                spread[s * own + (k % 2) * (own // 2) + k // 2] = rounded[k]
        else:
            spread[s * own : (s + 1) * own] = rounded


def update(place, got, olds, own, last):
    shapes = [jax.ShapeDtypeStruct(got.shape, BF)]
    if not last:
        shapes.append(jax.ShapeDtypeStruct((own,) + got.shape[1:], F32))
    out = pl.pallas_call(
        functools.partial(update_kernel, len(olds) == 2, last),
        out_shape=shapes,
        in_specs=[SM] + [VM] * (1 + len(olds)),
        out_specs=[VM] * len(shapes),
        compiler_params=PARAMS,
    )(place, got, *olds)
    return out[0], out[1:]


def join_kernel(got, out):
    slices = got.shape[1]
    own = got.shape[0] // (2 * lax.axis_size("y"))
    for r in range(got.shape[0]):
        y, c, k = r // (2 * own), r // own % 2, r % own
        out[y * own + k, c * slices : (c + 1) * slices] = got[r]


def join(got, shape):
    return pl.pallas_call(
        join_kernel,
        out_shape=jax.ShapeDtypeStruct(shape, BF),
        in_specs=[VM],
        out_specs=VM,
        compiler_params=PARAMS,
    )(got)


def exchange(v, axes):
    return lax.all_to_all(v, axes, split_axis=0, concat_axis=0, tiled=True)


def far_send(v, j):
    return v if j == 0 else lax.ppermute(v, "zh", [(i, (i + j) % 4) for i in range(4)])


def with_sibling(v):
    return v, lax.ppermute(v, "c", [(0, 1), (1, 0)])


def per_device(image_start, tiles, tile_list, recv_map, sinogram, weights):
    mats = with_sibling(tiles[0, 0])
    images = with_sibling(image_start)
    entries = with_sibling(jnp.transpose(tile_list[0], (2, 0, 1)))
    both_maps = jnp.stack(with_sibling(recv_map[0, 0].T))
    sinos, wts = with_sibling(sinogram[0]), with_sibling(weights[0])
    vox_tiles, slices = image_start.shape[0], image_start.shape[1] // 2
    own = vox_tiles // lax.axis_size("y")
    place = jnp.stack(
        [lax.axis_index("zh"), lax.axis_index("c"), lax.axis_index("y") * own]
    ).astype(jnp.int32)
    maps = [far_send(both_maps, j) for j in range(4)]
    state = images
    for step in range(ITERS):
        last = step == ITERS - 1
        got = exchange(project(place, entries, images, mats, slices), NEAR)
        parts = exchange(near_sum(place, maps, got), "zh")
        res = lax.all_gather(residual(place, parts, sinos, wts), "zh", axis=0, tiled=True)
        reply = exchange(select(place, maps, res), NEAR)
        grads = exchange(backproject(place, entries, reply, mats, vox_tiles), "y")
        spread, state = update(place, grads, state, 2 * own, last)
        images = (exchange(spread, ("y", "c") if last else "y"),)
    return join(images[0], image_start.shape)


def solution(mesh):
    fine = Mesh(mesh.devices.reshape(4, 4, 2, 2, 8), ("x", "zh", "zl", "c", "y"))
    return jax.shard_map(
        per_device,
        mesh=fine,
        in_specs=(
            P(REGION, None, None),
            P("y", REGION, None, None, None),
            P("y", REGION, None, None),
            P("y", REGION, None, None),
            P("y", REGION, None, None),
            P("y", REGION, None, None),
        ),
        out_specs=P(REGION, None, None),
        check_vma=False,
    )
```

time: 288 us -> 271 us (0.941); the launches traced: 284 us -> 271 us
  blocking collectives: 226 us -> 187 us
  starting transfers between devices: 23.7 us -> 41.6 us
  Pallas kernels: 12.7 us -> 16.9 us
    all_to_all x11 -> x8, blocking collectives: 226 us -> 158 us  [exchange(): return lax.all_to_all(v, axes, split_axis=0, concat_axis=0, tiled=True)]
    all_gather x0 -> x2, blocking collectives: none -> 29.1 us  [per_device(): lax.all_gather(residual(place, parts, sinos, wts), 'zh', axis=0, tiled=True)]
    ppermute x0 -> x6, starting transfers between devices: none -> 21.1 us  [with_sibling(): return (v, lax.ppermute(v, 'c', [(0, 1), (1, 0)]))]
    ppermute x3, waiting for transfers between devices: 16.4 us -> 12.1 us  [far_send(): lax.ppermute(v, 'zh', [(i, (i + j) % 4) for i in range(4)])]
    pallas_call x12 -> x13, Pallas kernels: 12.7 us -> 16.9 us  [the longest x2 6.31 us: project(): pl.pallas_call(project_kernel, out_shape=jax.ShapeDtypeStruct((ROWS, slic...]
    all_to_all x1 -> x2, waiting for transfers between devices: 0.01 us -> 3.42 us  [exchange(): return lax.all_to_all(v, axes, split_axis=0, concat_axis=0, tiled=True)]
    ppermute x0 -> x6, waiting for transfers between devices: none -> 3.24 us  [with_sibling(): return (v, lax.ppermute(v, 'c', [(0, 1), (1, 0)]))]
    all_to_all x1 -> x2, starting transfers between devices: 10.5 us -> 7.46 us  [exchange(): return lax.all_to_all(v, axes, split_axis=0, concat_axis=0, tiled=True)]
  transfers between devices with their start and end apart: 4 -> 11, of which waited for: 1 -> 6; matrix products, arithmetic and copies ran while one was open for 0% -> 0% of each run, Pallas kernels for 0% -> 0%
where the time goes in v5:
time: 271 us
  blocking collectives  187 us (69%)
  starting transfers between devices  41.6 us (15%)
  waiting for transfers between devices  18.7 us (7%)
  Pallas kernels  16.9 us (6%)
  local copies, waits for them, and re-layouts  5.86 us (2%)
    all_to_all x8, blocking collectives, exchange(): return lax.all_to_all(v, axes, split_axis=0, concat_axis=0, tiled=True)  158 us
    all_gather x2, blocking collectives, per_device(): lax.all_gather(residual(place, parts, sinos, wts), 'zh', axis=0, tiled=True)  29.1 us
    ppermute x6, starting transfers between devices, with_sibling(): return (v, lax.ppermute(v, 'c', [(0, 1), (1, 0)]))  21.1 us
    ppermute x3, starting transfers between devices, far_send(): lax.ppermute(v, 'zh', [(i, (i + j) % 4) for i in range(4)])  13 us
    ppermute x3, waiting for transfers between devices, far_send(): lax.ppermute(v, 'zh', [(i, (i + j) % 4) for i in range(4)])  12.1 us
    all_to_all x2, starting transfers between devices, exchange(): return lax.all_to_all(v, axes, split_axis=0, concat_axis=0, tiled=True)  7.46 us
    pallas_call x2, Pallas kernels, project(): pl.pallas_call(project_kernel, out_shape=jax.ShapeDtypeStruct((ROWS, slic...  6.31 us
    unnamed x32, local copies, waits for them, and re-layouts  5.86 us
  transfers between devices with their start and end apart: 11, of which 6 were waited for; matrix products, arithmetic and copies ran while one was open for 0% of the time, Pallas kernels for 0%

profile of v5, /device:TPU:1, one launch (start us, length us, event | category | flops | bytes accessed | tf_op | source)
XLA Modules:
  0.0 270.5 jit_solution(9273051877740338363)
XLA Ops:
  0.0 8.8 %collective-permute-start.6 = (bf16[32,128,128]{2,1,0:T(8,128)(2,1)}, bf16[32,128,128]{2,1,0:T(8,128)(2,1)S(1)}, u32[]{:S(2)}, u32[]{:S(2)}) collective-permute-start(bf16[32,128,128]{2,1,0:T(8,128)(2,1)} %bitcast.15), channel_id=1, source_target_pairs={{0,8},{8,0},{1,9},{9,1},{2,10},{10,2},{3,11},{11,3},{4,12},{12,4},... | collective-permute-start | bytes 3145736 | tf_op jit(solution)/shard_map/ppermute | solution.py:241
  8.8 1.9 collective-permute-start.5
  10.7 2.4 collective-permute-start
  13.1 0.1 pad_add_fusion.1.place
  13.2 0.9 collective-permute-done.e1
  14.2 1.2 copy-done
  15.4 0.9 copy-done.3
  16.3 0.7 copy-done.11
  17.0 3.8 %shard_map.64 = bf16[256,32,128]{2,1,0:T(8,128)(2,1)} custom-call(s32[3]{0:T(128)S(1)} %pad_add_fusion.1.place, s32[3,1,32]{2,1,0:T(1,128)S(1)} %bitcast.27, s32[3,1,32]{2,1,0:T(1,128)S(1)} %collective-permute-done.e1, bf16[16,64,128]{2,1,0:T(8,128)(2,1)S(1)} %copy-done.3, bf16[16,64,128]{2,1,0:T(8,128)(2,1)S(1)} %collective-permute-done.5.refs_1_, ...), custom_call_target="tpu_custom_call" | custom-call | tf_op jit(solution)/shard_map/pallas_call | solution.py:59
  20.8 3.7 %all-to-all-start = ((bf16[256,32,128]{2,1,0:T(8,128)(2,1)}), bf16[256,32,128]{2,1,0:T(8,128)(2,1)S(1)}, u32[]{:S(2)}, u32[]{:S(2)}) async-start(bf16[256,32,128]{2,1,0:T(8,128)(2,1)} %shard_map.64), calls=%async_computation | async-start | bytes 4194304 | tf_op jit(solution)/shard_map/all_to_all | solution.py:233
  24.6 2.4 collective-permute-start.1
  27.0 0.8 collective-permute-done.1
  27.8 6.9 %collective-permute-start.4 = (s32[2,2,64]{2,1,0:T(2,128)S(1)}, s32[2,2,64]{2,1,0:T(2,128)S(1)}, u32[]{:S(2)}, u32[]{:S(2)}) collective-permute-start(s32[2,2,64]{2,1,0:T(2,128)S(1)} %pad_add_fusion.m0), channel_id=1, source_target_pairs={{0,96},{32,0},{64,32},{96,64},{1,97},{33,1},{65,33},{97,65},{2,98}... | collective-permute-start | bytes 3080 | tf_op jit(solution)/shard_map/ppermute | solution.py:237
  34.6 1.9 collective-permute-start.3
  36.6 4.2 %collective-permute-start.2 = (s32[2,2,64]{2,1,0:T(2,128)S(1)}, s32[2,2,64]{2,1,0:T(2,128)S(1)}, u32[]{:S(2)}, u32[]{:S(2)}) collective-permute-start(s32[2,2,64]{2,1,0:T(2,128)S(1)} %pad_add_fusion.m0), channel_id=1, source_target_pairs={{0,32},{32,64},{64,96},{96,0},{1,33},{33,65},{65,97},{97,1},{2,34}... | collective-permute-start | bytes 3080 | tf_op jit(solution)/shard_map/ppermute | solution.py:237
  40.8 11.7 %collective-permute-done.3.m2 = s32[2,2,64]{2,1,0:T(2,128)S(1)} collective-permute-done((s32[2,2,64]{2,1,0:T(2,128)S(1)}, s32[2,2,64]{2,1,0:T(2,128)S(1)}, u32[]{:S(2)}, u32[]{:S(2)}) %collective-permute-start.3) | collective-permute-done | bytes 1056 | tf_op jit(solution)/shard_map/ppermute | solution.py:237
  52.6 0.3 collective-permute-done.2.m1
  52.9 0.6 copy-done.8
  53.5 0.7 copy-done.9
  54.2 1.1 shard_map.65
  55.3 0.8 copy-done.2
  56.1 3.7 %all-to-all-start.1 = ((bf16[64,32,128]{2,1,0:T(8,128)(2,1)}), bf16[64,32,128]{2,1,0:T(8,128)(2,1)S(1)}, u32[]{:S(2)}, u32[]{:S(2)}) async-start(bf16[64,32,128]{2,1,0:T(8,128)(2,1)} %copy-done.2), calls=%async_computation.1 | async-start | bytes 1048576 | tf_op jit(solution)/shard_map/all_to_all | solution.py:233
  59.8 3.7 %collective-permute-start.7 = (bf16[8,64,128]{2,1,0:T(8,128)(2,1)S(1)}, bf16[8,64,128]{2,1,0:T(8,128)(2,1)S(1)}, u32[]{:S(2)}, u32[]{:S(2)}) collective-permute-start(bf16[8,64,128]{2,1,0:T(8,128)(2,1)S(1)} %bitcast.20), channel_id=1, source_target_pairs={{0,8},{8,0},{1,9},{9,1},{2,10},{10,2},{3,11},{11,3},{4,12},{12,4},... | collective-permute-start | bytes 393224 | tf_op jit(solution)/shard_map/ppermute | solution.py:241
  63.5 1.9 collective-permute-start.8
  65.5 1.5 collective-permute-done.8.w1
  67.0 3.4 %all-to-all-done.1.parts = bf16[64,32,128]{2,1,0:T(8,128)(2,1)S(1)} async-done(((bf16[64,32,128]{2,1,0:T(8,128)(2,1)}), bf16[64,32,128]{2,1,0:T(8,128)(2,1)S(1)}, u32[]{:S(2)}, u32[]{:S(2)}) %all-to-all-start.1) | async-done | bytes 524320 | tf_op jit(solution)/shard_map/all_to_all | solution.py:233
  70.4 0.9 copy-done.6
  71.3 0.7 shard_map.66
  72.0 15.8 %all_gather.6.res = bf16[64,32,128]{2,1,0:T(8,128)(2,1)S(1)} all-gather(bf16[16,32,128]{2,1,0:T(8,128)(2,1)S(1)} %shard_map.66), channel_id=1, replica_groups=mesh['x'=4,'zh'=4,'zl'=2,'c'=2,'y'=8] {'zh'}, dimensions={0}, use_global_device_ids=true | all-gather | bytes 655360 | tf_op jit(solution)/shard_map/all_gather | solution.py:261
  87.8 1.3 shard_map.67
  89.1 29.1 %all_to_all.50.reply = bf16[256,32,128]{2,1,0:T(8,128)(2,1)S(1)} all-to-all(bf16[256,32,128]{2,1,0:T(8,128)(2,1)S(1)} %shard_map.67), channel_id=1, replica_groups=mesh['x'=4,'zh'=4,'zl'=2,'c'=2,'y'=8] {'x','zl'}, dimensions={0} | all-to-all | bytes 4194304 | tf_op jit(solution)/shard_map/all_to_all | solution.py:233
  118.3 1.3 shard_map.68
  119.6 16.2 %all_to_all.51.got = bf16[32,32,128]{2,1,0:T(8,128)(2,1)S(1)} all-to-all(bf16[32,32,128]{2,1,0:T(8,128)(2,1)S(1)} %shard_map.68), channel_id=1, replica_groups=mesh['x'=4,'zh'=4,'zl'=2,'c'=2,'y'=8] {'y'}, dimensions={0} | all-to-all | bytes 524288 | tf_op jit(solution)/shard_map/all_to_all | solution.py:233
  135.7 0.6 shard_map.69
  136.4 11.7 %all_to_all.52.refs_0_ = bf16[32,32,128]{2,1,0:T(8,128)(2,1)S(1)} all-to-all(bf16[32,32,128]{2,1,0:T(8,128)(2,1)S(1)} %get-tuple-element.7), channel_id=1, replica_groups=mesh['x'=4,'zh'=4,'zl'=2,'c'=2,'y'=8] {'y'}, dimensions={0} | all-to-all | bytes 524288 | tf_op jit(solution)/shard_map/all_to_all | solution.py:233
  148.1 2.5 shard_map.70
  150.6 21.7 %all_to_all.53.got = bf16[256,32,128]{2,1,0:T(8,128)(2,1)S(1)} all-to-all(bf16[256,32,128]{2,1,0:T(8,128)(2,1)S(1)} %shard_map.70), channel_id=1, replica_groups=mesh['x'=4,'zh'=4,'zl'=2,'c'=2,'y'=8] {'x','zl'}, dimensions={0} | all-to-all | bytes 4194304 | tf_op jit(solution)/shard_map/all_to_all | solution.py:233
  172.3 1.1 shard_map.71
  173.4 20.1 %all_to_all.54.parts = bf16[64,32,128]{2,1,0:T(8,128)(2,1)S(1)} all-to-all(bf16[64,32,128]{2,1,0:T(8,128)(2,1)S(1)} %shard_map.71), channel_id=1, replica_groups=mesh['x'=4,'zh'=4,'zl'=2,'c'=2,'y'=8] {'zh'}, dimensions={0} | all-to-all | bytes 1048576 | tf_op jit(solution)/shard_map/all_to_all | solution.py:233
  193.5 0.7 shard_map.72
  194.2 13.3 %all_gather.7.res = bf16[64,32,128]{2,1,0:T(8,128)(2,1)S(1)} all-gather(bf16[16,32,128]{2,1,0:T(8,128)(2,1)S(1)} %shard_map.72), channel_id=1, replica_groups=mesh['x'=4,'zh'=4,'zl'=2,'c'=2,'y'=8] {'zh'}, dimensions={0}, use_global_device_ids=true | all-gather | bytes 655360 | tf_op jit(solution)/shard_map/all_gather | solution.py:261
  207.5 1.3 shard_map.73
  208.7 20.1 %all_to_all.55.reply = bf16[256,32,128]{2,1,0:T(8,128)(2,1)S(1)} all-to-all(bf16[256,32,128]{2,1,0:T(8,128)(2,1)S(1)} %shard_map.73), channel_id=1, replica_groups=mesh['x'=4,'zh'=4,'zl'=2,'c'=2,'y'=8] {'x','zl'}, dimensions={0} | all-to-all | bytes 4194304 | tf_op jit(solution)/shard_map/all_to_all | solution.py:233
  228.9 1.3 shard_map.74
  230.2 12.9 %all_to_all.56.got = bf16[32,32,128]{2,1,0:T(8,128)(2,1)S(1)} all-to-all(bf16[32,32,128]{2,1,0:T(8,128)(2,1)S(1)} %shard_map.74), channel_id=1, replica_groups=mesh['x'=4,'zh'=4,'zl'=2,'c'=2,'y'=8] {'y'}, dimensions={0} | all-to-all | bytes 524288 | tf_op jit(solution)/shard_map/all_to_all | solution.py:233
  243.0 0.6 shard_map.75
  243.6 26.2 %all_to_all.57.got = bf16[32,32,128]{2,1,0:T(8,128)(2,1)S(1)} all-to-all(bf16[32,32,128]{2,1,0:T(8,128)(2,1)S(1)} %shard_map.75), channel_id=1, replica_groups=mesh['x'=4,'zh'=4,'zl'=2,'c'=2,'y'=8] {'y','c'}, dimensions={0} | all-to-all | bytes 524288 | tf_op jit(solution)/shard_map/all_to_all | solution.py:233
  269.8 0.7 shard_map.76
  (31 shorter events, 0.1 us)
Async XLA Ops:
  0.0 14.1 %collective-permute-start.6 = (bf16[32,128,128]{2,1,0:T(8,128)(2,1)}, bf16[32,128,128]{2,1,0:T(8,128)(2,1)S(1)}, u32[]{:S(2)}, u32[]{:S(2)}) collective-permute-start(bf16[32,128,128]{2,1,0:T(8,128)(2,1)} %bitcast.15), channel_id=1, source_target_pairs={{0,8},{8,0},{1,9},{9,1},{2,10},{10,2},{3,11},{11,3},{4,12},{12,4},... | collective-permute-start | bytes 3145736 | tf_op jit(solution)/shard_map/ppermute | solution.py:241
  8.8 5.4 %collective-permute-start.5 = (bf16[16,64,128]{2,1,0:T(8,128)(2,1)}, bf16[16,64,128]{2,1,0:T(8,128)(2,1)S(1)}, u32[]{:S(2)}, u32[]{:S(2)}) collective-permute-start(bf16[16,64,128]{2,1,0:T(8,128)(2,1)} %refs_0_.3), channel_id=1, source_target_pairs={{0,8},{8,0},{1,9},{9,1},{2,10},{10,2},{3,11},{11,3},{4,12},{12,4},... | collective-permute-start | bytes 786440 | tf_op jit(solution)/shard_map/ppermute | solution.py:241
  10.7 3.4 %collective-permute-start = (s32[3,1,32]{2,1,0:T(1,128)}, s32[3,1,32]{2,1,0:T(1,128)S(1)}, u32[]{:S(2)}, u32[]{:S(2)}) collective-permute-start(s32[3,1,32]{2,1,0:T(1,128)} %bitcast.26), channel_id=1, source_target_pairs={{0,8},{8,0},{1,9},{9,1},{2,10},{10,2},{3,11},{11,3},{4,12},{12,4},... | collective-permute-start | bytes 1160 | tf_op jit(solution)/shard_map/ppermute | solution.py:241
  14.1 6.7 %copy-start.13 = (s32[3,1,32]{2,1,0:T(1,128)}, s32[3,1,32]{2,1,0:T(1,128)S(1)}, u32[]{:S(2)}) copy-start(s32[3,1,32]{2,1,0:T(1,128)S(1)} %collective-permute-done.e1) | copy-start | bytes 1156
  14.1 1.2 copy-start
  15.4 0.9 copy-start.3
  16.3 0.7 copy-start.11
  20.8 3.8 %copy-start.15 = (s32[1,1,64,2]{2,3,1,0:T(2,128)S(1)}, s32[1,1,64,2]{2,3,1,0:T(2,128)}, u32[]{:S(2)}) copy-start(s32[1,1,64,2]{2,3,1,0:T(2,128)} %param.9) | copy-start | bytes 1540
  20.8 32.7 %all-to-all-start = ((bf16[256,32,128]{2,1,0:T(8,128)(2,1)}), bf16[256,32,128]{2,1,0:T(8,128)(2,1)S(1)}, u32[]{:S(2)}, u32[]{:S(2)}) async-start(bf16[256,32,128]{2,1,0:T(8,128)(2,1)} %shard_map.64), calls=%async_computation | async-start | bytes 4194304 | tf_op jit(solution)/shard_map/all_to_all | solution.py:233
  24.6 35.3 %copy-start.5 = (bf16[1,8,64,128]{3,2,1,0:T(8,128)(2,1)S(1)}, bf16[1,8,64,128]{3,2,1,0:T(8,128)(2,1)}, u32[]{:S(2)}) copy-start(bf16[1,8,64,128]{3,2,1,0:T(8,128)(2,1)} %param.10) | copy-start | bytes 393220
  24.6 3.2 %collective-permute-start.1 = (s32[2,64]{1,0:T(2,128)S(1)}, s32[2,64]{1,0:T(2,128)S(1)}, u32[]{:S(2)}, u32[]{:S(2)}) collective-permute-start(s32[2,64]{1,0:T(2,128)S(1)} %bitcast.31), channel_id=1, source_target_pairs={{0,8},{8,0},{1,9},{9,1},{2,10},{10,2},{3,11},{11,3},{4,12},{12,4},... | collective-permute-start | bytes 1544 | tf_op jit(solution)/shard_map/ppermute | solution.py:241
  27.8 13.1 %collective-permute-start.4 = (s32[2,2,64]{2,1,0:T(2,128)S(1)}, s32[2,2,64]{2,1,0:T(2,128)S(1)}, u32[]{:S(2)}, u32[]{:S(2)}) collective-permute-start(s32[2,2,64]{2,1,0:T(2,128)S(1)} %pad_add_fusion.m0), channel_id=1, source_target_pairs={{0,96},{32,0},{64,32},{96,64},{1,97},{33,1},{65,33},{97,65},{2,98}... | collective-permute-start | bytes 3080 | tf_op jit(solution)/shard_map/ppermute | solution.py:237
  34.6 17.9 %collective-permute-start.3 = (s32[2,2,64]{2,1,0:T(2,128)S(1)}, s32[2,2,64]{2,1,0:T(2,128)S(1)}, u32[]{:S(2)}, u32[]{:S(2)}) collective-permute-start(s32[2,2,64]{2,1,0:T(2,128)S(1)} %pad_add_fusion.m0), channel_id=1, source_target_pairs={{0,64},{32,96},{64,0},{96,32},{1,65},{33,97},{65,1},{97,33},{2,66}... | collective-permute-start | bytes 3080 | tf_op jit(solution)/shard_map/ppermute | solution.py:237
  36.6 16.3 %collective-permute-start.2 = (s32[2,2,64]{2,1,0:T(2,128)S(1)}, s32[2,2,64]{2,1,0:T(2,128)S(1)}, u32[]{:S(2)}, u32[]{:S(2)}) collective-permute-start(s32[2,2,64]{2,1,0:T(2,128)S(1)} %pad_add_fusion.m0), channel_id=1, source_target_pairs={{0,32},{32,64},{64,96},{96,0},{1,33},{33,65},{65,97},{97,1},{2,34}... | collective-permute-start | bytes 3080 | tf_op jit(solution)/shard_map/ppermute | solution.py:237
  52.9 0.6 copy-start.8
  53.5 0.7 copy-start.9
  55.3 0.8 copy-start.2
  56.1 31.7 %copy-start.10 = (s32[2,2,64]{2,1,0:T(2,128)S(1)}, s32[2,2,64]{2,1,0:T(2,128)}, u32[]{:S(2)}) copy-start(s32[2,2,64]{2,1,0:T(2,128)} %copy-done.8) | copy-start | bytes 3076
  56.1 14.3 %all-to-all-start.1 = ((bf16[64,32,128]{2,1,0:T(8,128)(2,1)}), bf16[64,32,128]{2,1,0:T(8,128)(2,1)S(1)}, u32[]{:S(2)}, u32[]{:S(2)}) async-start(bf16[64,32,128]{2,1,0:T(8,128)(2,1)} %copy-done.2), calls=%async_computation.1 | async-start | bytes 1048576 | tf_op jit(solution)/shard_map/all_to_all | solution.py:233
  59.8 5.6 %collective-permute-start.7 = (bf16[8,64,128]{2,1,0:T(8,128)(2,1)S(1)}, bf16[8,64,128]{2,1,0:T(8,128)(2,1)S(1)}, u32[]{:S(2)}, u32[]{:S(2)}) collective-permute-start(bf16[8,64,128]{2,1,0:T(8,128)(2,1)S(1)} %bitcast.20), channel_id=1, source_target_pairs={{0,8},{8,0},{1,9},{9,1},{2,10},{10,2},{3,11},{11,3},{4,12},{12,4},... | collective-permute-start | bytes 393224 | tf_op jit(solution)/shard_map/ppermute | solution.py:241
  63.5 3.5 %collective-permute-start.8 = (bf16[8,64,128]{2,1,0:T(8,128)(2,1)}, bf16[8,64,128]{2,1,0:T(8,128)(2,1)S(1)}, u32[]{:S(2)}, u32[]{:S(2)}) collective-permute-start(bf16[8,64,128]{2,1,0:T(8,128)(2,1)} %bitcast.23), channel_id=1, source_target_pairs={{0,8},{8,0},{1,9},{9,1},{2,10},{10,2},{3,11},{11,3},{4,12},{12,4},... | collective-permute-start | bytes 393224 | tf_op jit(solution)/shard_map/ppermute | solution.py:241
  70.4 0.9 copy-start.6
  89.1 29.2 %copy-start.1 = (bf16[1,1,32,128,128]{4,3,2,1,0:T(8,128)(2,1)S(1)}, bf16[1,1,32,128,128]{4,3,2,1,0:T(8,128)(2,1)}, u32[]{:S(2)}) copy-start(bf16[1,1,32,128,128]{4,3,2,1,0:T(8,128)(2,1)} %param.7) | copy-start | bytes 3145732
  89.1 29.2 %copy-start.12 = (s32[1,1,32,3]{2,1,3,0:T(1,128)S(1)}, s32[1,1,32,3]{2,1,3,0:T(1,128)}, u32[]{:S(2)}) copy-start(s32[1,1,32,3]{2,1,3,0:T(1,128)} %param.8) | copy-start | bytes 1156
  89.1 29.2 %copy-start.14 = (s32[3,1,32]{2,1,0:T(1,128)S(1)}, s32[3,1,32]{2,1,0:T(1,128)}, u32[]{:S(2)}) copy-start(s32[3,1,32]{2,1,0:T(1,128)} %copy-done.13) | copy-start | bytes 1156
  118.2 17.5 %copy-start.4 = (bf16[16,64,128]{2,1,0:T(8,128)(2,1)S(1)}, bf16[16,64,128]{2,1,0:T(8,128)(2,1)}, u32[]{:S(2)}) copy-start(bf16[16,64,128]{2,1,0:T(8,128)(2,1)} %refs_0_.3) | copy-start | bytes 786436
  172.3 21.2 %copy-start.7 = (bf16[1,8,64,128]{3,2,1,0:T(8,128)(2,1)S(1)}, bf16[1,8,64,128]{3,2,1,0:T(8,128)(2,1)}, u32[]{:S(2)}) copy-start(bf16[1,8,64,128]{3,2,1,0:T(8,128)(2,1)} %param.11) | copy-start | bytes 393220

commit v6 on v5

--- a/solution.py
+++ b/solution.py
@@ -17,6 +17,7 @@
 
 VM = pl.BlockSpec(memory_space=pltpu.VMEM)
 SM = pl.BlockSpec(memory_space=pltpu.SMEM)
+BIG = pltpu.CompilerParams(vmem_limit_bytes=58 * 1024 * 1024)
 PARAMS = pltpu.CompilerParams(vmem_limit_bytes=40 * 1024 * 1024)
 
 
@@ -30,39 +31,63 @@
     return pl.ds(pl.multiple_of(place[1] * slices, slices), slices)
 
 
-def project_kernel(place, e0, e1, *refs):
-    images, (m0, m1, out, prod, acc) = refs[:-5], refs[-5:]
-    n, slices = m0.shape[0], out.shape[1]
-    sides = ((e0, m0, place[1]), (e1, m1, 1 - place[1]))
-    for side, (entries, mat, a) in enumerate(sides):
+def project_sides(place, sides, image_of, out, prod, acc):
+    for side, (entries, mat, a, ready) in enumerate(sides):
+        n = mat.shape[0]
+        ready()
         for i in range(n):
-            v = entries[2, 0, i]
-            if len(images) == 2:
-                x = images[side][v, half(place, slices)]
-            else:
-                x = images[0][v * 2 + a]
+            x = image_of(side, entries[2, 0, i], a)
             prod[side * n + i] = lax.dot_general(x, mat[i], (((1,), (1,)), ((), ())), preferred_element_type=F32)
             acc[slot_row(entries, a, i)] = jnp.zeros(acc.shape[1:], F32)
     out[...] = jnp.zeros_like(out)
-    for side, (entries, _, a) in enumerate(sides):
-        for i in range(n):
+    for side, (entries, mat, a, _) in enumerate(sides):
+        for i in range(mat.shape[0]):
             row = slot_row(entries, a, i)
-            acc[row] = acc[row] + prod[side * n + i]
-    for entries, _, a in sides:
-        for i in range(n):
+            acc[row] = acc[row] + prod[side * mat.shape[0] + i]
+    for entries, mat, a, _ in sides:
+        for i in range(mat.shape[0]):
             row = slot_row(entries, a, i)
             out[row] = acc[row].astype(BF)
 
 
+def project_kernel(place, e0, e1, image, m0, m1, out, prod, acc):
+    sides = ((e0, m0, place[1], lambda: None), (e1, m1, 1 - place[1], lambda: None))
+    project_sides(place, sides, lambda side, v, a: image[v * 2 + a], out, prod, acc)
+
+
+def first_project_kernel(place, e0, e1, image_in, image1, mat_in, m1, out, prod, acc, image0, m0, sem):
+    slices = out.shape[1]
+    loads = [pltpu.make_async_copy(mat_in, m0, sem.at[0]), pltpu.make_async_copy(image_in, image0, sem.at[1])]
+    for load in loads:
+        load.start()
+
+    def loaded():
+        for load in loads:
+            load.wait()
+
+    images = (image1, image0)
+    sides = ((e1, m1, 1 - place[1], lambda: None), (e0, m0, place[1], loaded))
+    project_sides(place, sides, lambda side, v, a: images[side][v, half(place, slices)], out, prod, acc)
+
+
 def project(place, entries, images, mats, slices):
     n, width = mats[0].shape[0], mats[0].shape[2]
-    return pl.pallas_call(
-        project_kernel,
+    first = len(images) == 2
+    loose = pl.BlockSpec(memory_space=pl.ANY)
+    scratch = [pltpu.VMEM((2 * n, slices, width), F32), pltpu.VMEM((ROWS, slices, width), F32)]
+    if first:
+        scratch += [
+            pltpu.VMEM(images[0].shape, BF),
+            pltpu.VMEM(mats[0].shape, BF),
+            pltpu.SemaphoreType.DMA((2,)),
+        ]
+    return pl.pallas_call(
+        first_project_kernel if first else project_kernel,
         out_shape=jax.ShapeDtypeStruct((ROWS, slices, width), BF),
-        in_specs=[SM] * 3 + [VM] * (len(images) + 2),
-        out_specs=VM,
-        scratch_shapes=[pltpu.VMEM((2 * n, slices, width), F32), pltpu.VMEM((ROWS, slices, width), F32)],
-        compiler_params=PARAMS,
+        in_specs=[SM] * 3 + ([loose, VM, loose, VM] if first else [VM] * 3),
+        out_specs=VM,
+        scratch_shapes=scratch,
+        compiler_params=BIG if first else PARAMS,
     )(place, *entries, *images, *mats)
 
 
@@ -252,6 +277,7 @@
     place = jnp.stack(
         [lax.axis_index("zh"), lax.axis_index("c"), lax.axis_index("y") * own]
     ).astype(jnp.int32)
+    both_maps, sinos, wts = lax.optimization_barrier((both_maps, sinos, wts))
     maps = [far_send(both_maps, j) for j in range(4)]
     state = images
     for step in range(ITERS):

time: 271 us -> 267 us (0.985)
  blocking collectives: 187 us -> 199 us
  waiting for transfers between devices: 18.7 us -> 9.09 us
  starting transfers between devices: 41.6 us -> 36.5 us
  local copies, waits for them, and re-layouts: 5.86 us -> 1.75 us
    all_to_all x8 -> x9, blocking collectives: 158 us -> 171 us  [exchange(): return lax.all_to_all(v, axes, split_axis=0, concat_axis=0, tiled=True)]
    ppermute x3, waiting for transfers between devices: 12.1 us -> 7.83 us  [far_send(): lax.ppermute(v, 'zh', [(i, (i + j) % 4) for i in range(4)])]
    unnamed x32 -> x26, local copies, waits for them, and re-layouts: 5.86 us -> 1.75 us
    all_to_all x2 -> x1, starting transfers between devices: 7.46 us -> 3.75 us  [exchange(): return lax.all_to_all(v, axes, split_axis=0, concat_axis=0, tiled=True)]
    all_to_all x2 -> x1, waiting for transfers between devices: 3.42 us -> 0.01 us  [exchange(): return lax.all_to_all(v, axes, split_axis=0, concat_axis=0, tiled=True)]
  transfers between devices with their start and end apart: 11 -> 10, of which waited for: 6 -> 4; matrix products, arithmetic and copies ran while one was open for 0% -> 0% of each run, Pallas kernels for 0% -> 0%
where the time goes in v6:
time: 267 us; the launch traced here: 266 us
  blocking collectives  199 us (75%)
  starting transfers between devices  36.5 us (14%)
  Pallas kernels  18.9 us (7%)
  waiting for transfers between devices  9.09 us (3%)
    all_to_all x9, blocking collectives, exchange(): return lax.all_to_all(v, axes, split_axis=0, concat_axis=0, tiled=True)  171 us
    all_gather x2, blocking collectives, per_device(): lax.all_gather(residual(place, parts, sinos, wts), 'zh', axis=0, tiled=True)  28.5 us
    ppermute x6, starting transfers between devices, with_sibling(): return (v, lax.ppermute(v, 'c', [(0, 1), (1, 0)]))  19.7 us
    ppermute x3, starting transfers between devices, far_send(): lax.ppermute(v, 'zh', [(i, (i + j) % 4) for i in range(4)])  13 us
    pallas_call x2, Pallas kernels, project(): pl.pallas_call(first_project_kernel if first else project_kernel, out_sha...  8.27 us
    ppermute x3, waiting for transfers between devices, far_send(): lax.ppermute(v, 'zh', [(i, (i + j) % 4) for i in range(4)])  7.83 us
  transfers between devices with their start and end apart: 10, of which 4 were waited for; matrix products, arithmetic and copies ran while one was open for 0% of the time, Pallas kernels for 0%

profile of v6, /device:TPU:1, one launch (start us, length us, event | category | flops | bytes accessed | tf_op | source)
XLA Modules:
  0.0 266.4 jit_solution(3905902927124675763)
XLA Ops:
  0.0 8.8 %collective-permute-start.8 = (bf16[32,128,128]{2,1,0:T(8,128)(2,1)}, bf16[32,128,128]{2,1,0:T(8,128)(2,1)S(1)}, u32[]{:S(2)}, u32[]{:S(2)}) collective-permute-start(bf16[32,128,128]{2,1,0:T(8,128)(2,1)} %bitcast.15), channel_id=1, source_target_pairs={{0,8},{8,0},{1,9},{9,1},{2,10},{10,2},{3,11},{11,3},{4,12},{12,4},... | collective-permute-start | bytes 3145736 | tf_op jit(solution)/shard_map/ppermute | solution.py:266
  8.8 1.9 collective-permute-start.7
  10.7 2.4 collective-permute-start
  13.1 0.6 pad_add_fusion.1.place
  13.7 0.4 collective-permute-done.e1
  14.2 0.5 copy-done.10
  14.7 0.2 copy-done.4
  14.9 1.0 copy-done.1
  15.8 5.8 %shard_map.64 = bf16[256,32,128]{2,1,0:T(8,128)(2,1)} custom-call(s32[3]{0:T(128)} %pad_add_fusion.1.place, s32[3,1,32]{2,1,0:T(1,128)} %bitcast.27, s32[3,1,32]{2,1,0:T(1,128)} %copy-done.10, bf16[16,64,128]{2,1,0:T(8,128)(2,1)} %refs_0_.1, bf16[16,64,128]{2,1,0:T(8,128)(2,1)} %copy-done.4, bf16[32,128,128]{2,1,0:T(8,128)(2,1)} %bitcast.16, ...), custom_call_target="tpu_custom_call" | custom-call | tf_op jit(solution)/shard_map/pallas_call | solution.py:84
  21.6 0.0 copy-start.6
  21.6 0.0 copy-start.7
  21.6 0.0 copy-start.12
  21.7 3.7 %all-to-all-start = ((bf16[256,32,128]{2,1,0:T(8,128)(2,1)}), bf16[256,32,128]{2,1,0:T(8,128)(2,1)S(1)}, u32[]{:S(2)}, u32[]{:S(2)}) async-start(bf16[256,32,128]{2,1,0:T(8,128)(2,1)} %shard_map.64), calls=%async_computation | async-start | bytes 4194304 | tf_op jit(solution)/shard_map/all_to_all | solution.py:258
  25.4 2.2 collective-permute-start.2
  27.7 2.1 collective-permute-start.3
  29.8 2.2 collective-permute-start.1
  32.0 0.8 collective-permute-done.1
  32.8 6.9 %collective-permute-start.6 = (s32[2,2,64]{2,1,0:T(2,128)S(1)}, s32[2,2,64]{2,1,0:T(2,128)S(1)}, u32[]{:S(2)}, u32[]{:S(2)}) collective-permute-start(s32[2,2,64]{2,1,0:T(2,128)S(1)} %pad_add_fusion.m0), channel_id=1, source_target_pairs={{0,96},{32,0},{64,32},{96,64},{1,97},{33,1},{65,33},{97,65},{2,98}... | collective-permute-start | bytes 3080 | tf_op jit(solution)/shard_map/ppermute | solution.py:262
  39.7 1.9 collective-permute-start.5
  41.7 4.2 %collective-permute-start.4 = (s32[2,2,64]{2,1,0:T(2,128)S(1)}, s32[2,2,64]{2,1,0:T(2,128)S(1)}, u32[]{:S(2)}, u32[]{:S(2)}) collective-permute-start(s32[2,2,64]{2,1,0:T(2,128)S(1)} %pad_add_fusion.m0), channel_id=1, source_target_pairs={{0,32},{32,64},{64,96},{96,0},{1,33},{33,65},{65,97},{97,1},{2,34}... | collective-permute-start | bytes 3080 | tf_op jit(solution)/shard_map/ppermute | solution.py:262
  45.9 7.5 %collective-permute-done.5.m2 = s32[2,2,64]{2,1,0:T(2,128)S(1)} collective-permute-done((s32[2,2,64]{2,1,0:T(2,128)S(1)}, s32[2,2,64]{2,1,0:T(2,128)S(1)}, u32[]{:S(2)}, u32[]{:S(2)}) %collective-permute-start.5) | collective-permute-done | bytes 1056 | tf_op jit(solution)/shard_map/ppermute | solution.py:262
  53.4 0.4 collective-permute-done.4.m1
  53.8 1.1 shard_map.65
  54.9 16.4 %all_to_all.50.parts = bf16[64,32,128]{2,1,0:T(8,128)(2,1)S(1)} all-to-all(bf16[64,32,128]{2,1,0:T(8,128)(2,1)S(1)} %shard_map.65), channel_id=1, replica_groups=mesh['x'=4,'zh'=4,'zl'=2,'c'=2,'y'=8] {'zh'}, dimensions={0} | all-to-all | bytes 1048576 | tf_op jit(solution)/shard_map/all_to_all | solution.py:258
  71.3 0.7 shard_map.66
  71.9 14.0 %all_gather.6.res = bf16[64,32,128]{2,1,0:T(8,128)(2,1)S(1)} all-gather(bf16[16,32,128]{2,1,0:T(8,128)(2,1)S(1)} %shard_map.66), channel_id=1, replica_groups=mesh['x'=4,'zh'=4,'zl'=2,'c'=2,'y'=8] {'zh'}, dimensions={0}, use_global_device_ids=true | all-gather | bytes 655360 | tf_op jit(solution)/shard_map/all_gather | solution.py:287
  85.9 1.3 shard_map.67
  87.2 0.0 copy-start
  87.2 0.0 copy-start.9
  87.2 27.7 %all_to_all.51.reply = bf16[256,32,128]{2,1,0:T(8,128)(2,1)S(1)} all-to-all(bf16[256,32,128]{2,1,0:T(8,128)(2,1)S(1)} %shard_map.67), channel_id=1, replica_groups=mesh['x'=4,'zh'=4,'zl'=2,'c'=2,'y'=8] {'x','zl'}, dimensions={0} | all-to-all | bytes 4194304 | tf_op jit(solution)/shard_map/all_to_all | solution.py:258
  114.9 0.0 copy-start.3
  114.9 1.3 shard_map.68
  116.2 16.0 %all_to_all.52.got = bf16[32,32,128]{2,1,0:T(8,128)(2,1)S(1)} all-to-all(bf16[32,32,128]{2,1,0:T(8,128)(2,1)S(1)} %shard_map.68), channel_id=1, replica_groups=mesh['x'=4,'zh'=4,'zl'=2,'c'=2,'y'=8] {'y'}, dimensions={0} | all-to-all | bytes 524288 | tf_op jit(solution)/shard_map/all_to_all | solution.py:258
  132.2 0.6 shard_map.69
  132.8 11.7 %all_to_all.53.image = bf16[32,32,128]{2,1,0:T(8,128)(2,1)S(1)} all-to-all(bf16[32,32,128]{2,1,0:T(8,128)(2,1)S(1)} %get-tuple-element.17), channel_id=1, replica_groups=mesh['x'=4,'zh'=4,'zl'=2,'c'=2,'y'=8] {'y'}, dimensions={0} | all-to-all | bytes 524288 | tf_op jit(solution)/shard_map/all_to_all | solution.py:258
  144.5 2.5 shard_map.70
  147.1 20.7 %all_to_all.54.got = bf16[256,32,128]{2,1,0:T(8,128)(2,1)S(1)} all-to-all(bf16[256,32,128]{2,1,0:T(8,128)(2,1)S(1)} %shard_map.70), channel_id=1, replica_groups=mesh['x'=4,'zh'=4,'zl'=2,'c'=2,'y'=8] {'x','zl'}, dimensions={0} | all-to-all | bytes 4194304 | tf_op jit(solution)/shard_map/all_to_all | solution.py:258
  167.8 1.2 shard_map.71
  169.0 17.1 %all_to_all.55.parts = bf16[64,32,128]{2,1,0:T(8,128)(2,1)S(1)} all-to-all(bf16[64,32,128]{2,1,0:T(8,128)(2,1)S(1)} %shard_map.71), channel_id=1, replica_groups=mesh['x'=4,'zh'=4,'zl'=2,'c'=2,'y'=8] {'zh'}, dimensions={0} | all-to-all | bytes 1048576 | tf_op jit(solution)/shard_map/all_to_all | solution.py:258
  186.1 0.7 shard_map.72
  186.7 14.5 %all_gather.7.res = bf16[64,32,128]{2,1,0:T(8,128)(2,1)S(1)} all-gather(bf16[16,32,128]{2,1,0:T(8,128)(2,1)S(1)} %shard_map.72), channel_id=1, replica_groups=mesh['x'=4,'zh'=4,'zl'=2,'c'=2,'y'=8] {'zh'}, dimensions={0}, use_global_device_ids=true | all-gather | bytes 655360 | tf_op jit(solution)/shard_map/all_gather | solution.py:287
  201.2 1.3 shard_map.73
  202.5 21.9 %all_to_all.56.reply = bf16[256,32,128]{2,1,0:T(8,128)(2,1)S(1)} all-to-all(bf16[256,32,128]{2,1,0:T(8,128)(2,1)S(1)} %shard_map.73), channel_id=1, replica_groups=mesh['x'=4,'zh'=4,'zl'=2,'c'=2,'y'=8] {'x','zl'}, dimensions={0} | all-to-all | bytes 4194304 | tf_op jit(solution)/shard_map/all_to_all | solution.py:258
  224.3 1.3 shard_map.74
  225.6 11.7 %all_to_all.57.got = bf16[32,32,128]{2,1,0:T(8,128)(2,1)S(1)} all-to-all(bf16[32,32,128]{2,1,0:T(8,128)(2,1)S(1)} %shard_map.74), channel_id=1, replica_groups=mesh['x'=4,'zh'=4,'zl'=2,'c'=2,'y'=8] {'y'}, dimensions={0} | all-to-all | bytes 524288 | tf_op jit(solution)/shard_map/all_to_all | solution.py:258
  237.4 0.6 shard_map.75
  238.0 27.7 %all_to_all.58.got = bf16[32,32,128]{2,1,0:T(8,128)(2,1)S(1)} all-to-all(bf16[32,32,128]{2,1,0:T(8,128)(2,1)S(1)} %shard_map.75), channel_id=1, replica_groups=mesh['x'=4,'zh'=4,'zl'=2,'c'=2,'y'=8] {'y','c'}, dimensions={0} | all-to-all | bytes 524288 | tf_op jit(solution)/shard_map/all_to_all | solution.py:258
  265.6 0.7 shard_map.76
  (24 shorter events, 0.1 us)
Async XLA Ops:
  0.0 14.2 %collective-permute-start.8 = (bf16[32,128,128]{2,1,0:T(8,128)(2,1)}, bf16[32,128,128]{2,1,0:T(8,128)(2,1)S(1)}, u32[]{:S(2)}, u32[]{:S(2)}) collective-permute-start(bf16[32,128,128]{2,1,0:T(8,128)(2,1)} %bitcast.15), channel_id=1, source_target_pairs={{0,8},{8,0},{1,9},{9,1},{2,10},{10,2},{3,11},{11,3},{4,12},{12,4},... | collective-permute-start | bytes 3145736 | tf_op jit(solution)/shard_map/ppermute | solution.py:266
  8.8 5.4 %collective-permute-start.7 = (bf16[16,64,128]{2,1,0:T(8,128)(2,1)}, bf16[16,64,128]{2,1,0:T(8,128)(2,1)S(1)}, u32[]{:S(2)}, u32[]{:S(2)}) collective-permute-start(bf16[16,64,128]{2,1,0:T(8,128)(2,1)} %refs_0_.1), channel_id=1, source_target_pairs={{0,8},{8,0},{1,9},{9,1},{2,10},{10,2},{3,11},{11,3},{4,12},{12,4},... | collective-permute-start | bytes 786440 | tf_op jit(solution)/shard_map/ppermute | solution.py:266
  10.7 3.4 %collective-permute-start = (s32[3,1,32]{2,1,0:T(1,128)}, s32[3,1,32]{2,1,0:T(1,128)S(1)}, u32[]{:S(2)}, u32[]{:S(2)}) collective-permute-start(s32[3,1,32]{2,1,0:T(1,128)} %bitcast.26), channel_id=1, source_target_pairs={{0,8},{8,0},{1,9},{9,1},{2,10},{10,2},{3,11},{11,3},{4,12},{12,4},... | collective-permute-start | bytes 1160 | tf_op jit(solution)/shard_map/ppermute | solution.py:266
  14.1 0.5 copy-start.10
  14.1 0.7 copy-start.4
  14.8 1.0 copy-start.1
  21.6 3.8 %copy-start.6 = (bf16[1,8,64,128]{3,2,1,0:T(8,128)(2,1)S(1)}, bf16[1,8,64,128]{3,2,1,0:T(8,128)(2,1)}, u32[]{:S(2)}) copy-start(bf16[1,8,64,128]{3,2,1,0:T(8,128)(2,1)} %param.10) | copy-start | bytes 393220
  21.6 6.0 %copy-start.7 = (bf16[1,8,64,128]{3,2,1,0:T(8,128)(2,1)S(1)}, bf16[1,8,64,128]{3,2,1,0:T(8,128)(2,1)}, u32[]{:S(2)}) copy-start(bf16[1,8,64,128]{3,2,1,0:T(8,128)(2,1)} %param.11) | copy-start | bytes 393220
  21.6 8.1 %copy-start.12 = (s32[1,1,64,2]{2,3,1,0:T(2,128)S(1)}, s32[1,1,64,2]{2,3,1,0:T(2,128)}, u32[]{:S(2)}) copy-start(s32[1,1,64,2]{2,3,1,0:T(2,128)} %param.9) | copy-start | bytes 1540
  21.6 32.1 %copy-start.8 = (s32[3]{0:T(128)S(1)}, s32[3]{0:T(128)}, u32[]{:S(2)}) copy-start(s32[3]{0:T(128)} %pad_add_fusion.1.place) | copy-start | bytes 40
  21.7 32.1 %all-to-all-start = ((bf16[256,32,128]{2,1,0:T(8,128)(2,1)}), bf16[256,32,128]{2,1,0:T(8,128)(2,1)S(1)}, u32[]{:S(2)}, u32[]{:S(2)}) async-start(bf16[256,32,128]{2,1,0:T(8,128)(2,1)} %shard_map.64), calls=%async_computation | async-start | bytes 4194304 | tf_op jit(solution)/shard_map/all_to_all | solution.py:258
  25.4 7.4 %collective-permute-start.2 = (bf16[8,64,128]{2,1,0:T(8,128)(2,1)S(1)}, bf16[8,64,128]{2,1,0:T(8,128)(2,1)S(1)}, u32[]{:S(2)}, u32[]{:S(2)}) collective-permute-start(bf16[8,64,128]{2,1,0:T(8,128)(2,1)S(1)} %bitcast.20), channel_id=1, source_target_pairs={{0,8},{8,0},{1,9},{9,1},{2,10},{10,2},{3,11},{11,3},{4,12},{12,4},... | collective-permute-start | bytes 393224 | tf_op jit(solution)/shard_map/ppermute | solution.py:266
  27.7 5.2 %collective-permute-start.3 = (bf16[8,64,128]{2,1,0:T(8,128)(2,1)S(1)}, bf16[8,64,128]{2,1,0:T(8,128)(2,1)S(1)}, u32[]{:S(2)}, u32[]{:S(2)}) collective-permute-start(bf16[8,64,128]{2,1,0:T(8,128)(2,1)S(1)} %bitcast.23), channel_id=1, source_target_pairs={{0,8},{8,0},{1,9},{9,1},{2,10},{10,2},{3,11},{11,3},{4,12},{12,4},... | collective-permute-start | bytes 393224 | tf_op jit(solution)/shard_map/ppermute | solution.py:266
  29.8 3.0 %collective-permute-start.1 = (s32[2,64]{1,0:T(2,128)S(1)}, s32[2,64]{1,0:T(2,128)S(1)}, u32[]{:S(2)}, u32[]{:S(2)}) collective-permute-start(s32[2,64]{1,0:T(2,128)S(1)} %bitcast.31), channel_id=1, source_target_pairs={{0,8},{8,0},{1,9},{9,1},{2,10},{10,2},{3,11},{11,3},{4,12},{12,4},... | collective-permute-start | bytes 1544 | tf_op jit(solution)/shard_map/ppermute | solution.py:266
  32.8 13.1 %collective-permute-start.6 = (s32[2,2,64]{2,1,0:T(2,128)S(1)}, s32[2,2,64]{2,1,0:T(2,128)S(1)}, u32[]{:S(2)}, u32[]{:S(2)}) collective-permute-start(s32[2,2,64]{2,1,0:T(2,128)S(1)} %pad_add_fusion.m0), channel_id=1, source_target_pairs={{0,96},{32,0},{64,32},{96,64},{1,97},{33,1},{65,33},{97,65},{2,98}... | collective-permute-start | bytes 3080 | tf_op jit(solution)/shard_map/ppermute | solution.py:262
  39.7 13.6 %collective-permute-start.5 = (s32[2,2,64]{2,1,0:T(2,128)S(1)}, s32[2,2,64]{2,1,0:T(2,128)S(1)}, u32[]{:S(2)}, u32[]{:S(2)}) collective-permute-start(s32[2,2,64]{2,1,0:T(2,128)S(1)} %pad_add_fusion.m0), channel_id=1, source_target_pairs={{0,64},{32,96},{64,0},{96,32},{1,65},{33,97},{65,1},{97,33},{2,66}... | collective-permute-start | bytes 3080 | tf_op jit(solution)/shard_map/ppermute | solution.py:262
  41.7 12.1 %collective-permute-start.4 = (s32[2,2,64]{2,1,0:T(2,128)S(1)}, s32[2,2,64]{2,1,0:T(2,128)S(1)}, u32[]{:S(2)}, u32[]{:S(2)}) collective-permute-start(s32[2,2,64]{2,1,0:T(2,128)S(1)} %pad_add_fusion.m0), channel_id=1, source_target_pairs={{0,32},{32,64},{64,96},{96,0},{1,33},{33,65},{65,97},{97,1},{2,34}... | collective-permute-start | bytes 3080 | tf_op jit(solution)/shard_map/ppermute | solution.py:262
  87.2 27.7 %copy-start = (bf16[1,1,32,128,128]{4,3,2,1,0:T(8,128)(2,1)S(1)}, bf16[1,1,32,128,128]{4,3,2,1,0:T(8,128)(2,1)}, u32[]{:S(2)}) copy-start(bf16[1,1,32,128,128]{4,3,2,1,0:T(8,128)(2,1)} %param.7) | copy-start | bytes 3145732
  87.2 27.7 %copy-start.2 = (bf16[32,128,128]{2,1,0:T(8,128)(2,1)S(1)}, bf16[32,128,128]{2,1,0:T(8,128)(2,1)}, u32[]{:S(2)}) copy-start(bf16[32,128,128]{2,1,0:T(8,128)(2,1)} %copy-done.1) | copy-start | bytes 3145732
  87.2 27.7 %copy-start.9 = (s32[1,1,32,3]{2,1,3,0:T(1,128)S(1)}, s32[1,1,32,3]{2,1,3,0:T(1,128)}, u32[]{:S(2)}) copy-start(s32[1,1,32,3]{2,1,3,0:T(1,128)} %param.8) | copy-start | bytes 1156
  87.2 27.7 %copy-start.11 = (s32[3,1,32]{2,1,0:T(1,128)S(1)}, s32[3,1,32]{2,1,0:T(1,128)}, u32[]{:S(2)}) copy-start(s32[3,1,32]{2,1,0:T(1,128)} %copy-done.10) | copy-start | bytes 1156
  114.9 17.3 %copy-start.3 = (bf16[16,64,128]{2,1,0:T(8,128)(2,1)S(1)}, bf16[16,64,128]{2,1,0:T(8,128)(2,1)}, u32[]{:S(2)}) copy-start(bf16[16,64,128]{2,1,0:T(8,128)(2,1)} %refs_0_.1) | copy-start | bytes 786436
  114.9 17.3 %copy-start.5 = (bf16[16,64,128]{2,1,0:T(8,128)(2,1)S(1)}, bf16[16,64,128]{2,1,0:T(8,128)(2,1)}, u32[]{:S(2)}) copy-start(bf16[16,64,128]{2,1,0:T(8,128)(2,1)} %copy-done.4) | copy-start | bytes 786436

commit v7 on v6

--- a/solution.py
+++ b/solution.py
@@ -31,31 +31,32 @@
     return pl.ds(pl.multiple_of(place[1] * slices, slices), slices)
 
 
-def project_sides(place, sides, image_of, out, prod, acc):
+def project_sides(place, sides, image_of, out, prod, accs):
     for side, (entries, mat, a, ready) in enumerate(sides):
         n = mat.shape[0]
         ready()
         for i in range(n):
             x = image_of(side, entries[2, 0, i], a)
             prod[side * n + i] = lax.dot_general(x, mat[i], (((1,), (1,)), ((), ())), preferred_element_type=F32)
-            acc[slot_row(entries, a, i)] = jnp.zeros(acc.shape[1:], F32)
+            accs[side][slot_row(entries, a, i)] = jnp.zeros(accs[side].shape[1:], F32)
     out[...] = jnp.zeros_like(out)
-    for side, (entries, mat, a, _) in enumerate(sides):
-        for i in range(mat.shape[0]):
+    n = prod.shape[0] // 2
+    for i in range(n):
+        for side, (entries, _, a, _) in enumerate(sides):
+            acc, row = accs[side], slot_row(entries, a, i)
+            acc[row] = acc[row] + prod[side * n + i]
+    for i in range(n):
+        for side, (entries, _, a, _) in enumerate(sides):
             row = slot_row(entries, a, i)
-            acc[row] = acc[row] + prod[side * mat.shape[0] + i]
-    for entries, mat, a, _ in sides:
-        for i in range(mat.shape[0]):
-            row = slot_row(entries, a, i)
-            out[row] = acc[row].astype(BF)
-
-
-def project_kernel(place, e0, e1, image, m0, m1, out, prod, acc):
+            out[row] = accs[side][row].astype(BF)
+
+
+def project_kernel(place, e0, e1, image, m0, m1, out, prod, *accs):
     sides = ((e0, m0, place[1], lambda: None), (e1, m1, 1 - place[1], lambda: None))
-    project_sides(place, sides, lambda side, v, a: image[v * 2 + a], out, prod, acc)
-
-
-def first_project_kernel(place, e0, e1, image_in, image1, mat_in, m1, out, prod, acc, image0, m0, sem):
+    project_sides(place, sides, lambda side, v, a: image[v * 2 + a], out, prod, accs)
+
+
+def first_project_kernel(place, e0, e1, image_in, image1, mat_in, m1, out, prod, acc0, acc1, image0, m0, sem):
     slices = out.shape[1]
     loads = [pltpu.make_async_copy(mat_in, m0, sem.at[0]), pltpu.make_async_copy(image_in, image0, sem.at[1])]
     for load in loads:
@@ -67,14 +68,14 @@
 
     images = (image1, image0)
     sides = ((e1, m1, 1 - place[1], lambda: None), (e0, m0, place[1], loaded))
-    project_sides(place, sides, lambda side, v, a: images[side][v, half(place, slices)], out, prod, acc)
+    project_sides(place, sides, lambda side, v, a: images[side][v, half(place, slices)], out, prod, (acc0, acc1))
 
 
 def project(place, entries, images, mats, slices):
     n, width = mats[0].shape[0], mats[0].shape[2]
     first = len(images) == 2
     loose = pl.BlockSpec(memory_space=pl.ANY)
-    scratch = [pltpu.VMEM((2 * n, slices, width), F32), pltpu.VMEM((ROWS, slices, width), F32)]
+    scratch = [pltpu.VMEM((2 * n, slices, width), F32)] + [pltpu.VMEM((ROWS, slices, width), F32)] * 2
     if first:
         scratch += [
             pltpu.VMEM(images[0].shape, BF),
@@ -167,18 +168,21 @@
     )(place, *maps, res)
 
 
-def backproject_kernel(place, e0, e1, reply, m0, m1, out, prod, acc):
+def backproject_kernel(place, e0, e1, reply, m0, m1, out, prod, *accs):
     n = m0.shape[0]
     sides = ((e0, m0, place[1]), (e1, m1, 1 - place[1]))
     for side, (entries, mat, a) in enumerate(sides):
         for i in range(n):
             prod[side * n + i] = jnp.dot(reply[slot_row(entries, a, i)], mat[i], preferred_element_type=F32)
-    acc[...] = jnp.zeros_like(acc)
-    for side, (entries, _, a) in enumerate(sides):
-        for i in range(n):
-            v = entries[2, 0, i] * 2 + a
+    for acc in accs:
+        acc[...] = jnp.zeros_like(acc)
+    for i in range(n):
+        for side, (entries, _, _) in enumerate(sides):
+            acc, v = accs[side], entries[2, 0, i]
             acc[v] = acc[v] + prod[side * n + i]
-    out[...] = acc[...].astype(BF)
+    for side, (_, _, a) in enumerate(sides):
+        for v in range(accs[side].shape[0]):
+            out[v * 2 + a] = accs[side][v].astype(BF)
 
 
 def backproject(place, entries, reply, mats, vox_tiles):
@@ -188,7 +192,7 @@
         out_shape=jax.ShapeDtypeStruct((2 * vox_tiles, slices, width), BF),
         in_specs=[SM] * 3 + [VM] * 3,
         out_specs=VM,
-        scratch_shapes=[pltpu.VMEM((2 * n, slices, width), F32), pltpu.VMEM((2 * vox_tiles, slices, width), F32)],
+        scratch_shapes=[pltpu.VMEM((2 * n, slices, width), F32)] + [pltpu.VMEM((vox_tiles, slices, width), F32)] * 2,
         compiler_params=PARAMS,
     )(place, *entries, reply, *mats)
 

time: 267 us -> 267 us (level)
  no operation moved by 1% of the time
where the time goes in v7:
time: 267 us; the launch traced here: 266 us
  blocking collectives  199 us (75%)
  starting transfers between devices  36.5 us (14%)
  Pallas kernels  18.7 us (7%)
  waiting for transfers between devices  9.08 us (3%)
    all_to_all x9, blocking collectives, exchange(): return lax.all_to_all(v, axes, split_axis=0, concat_axis=0, tiled=True)  171 us
    all_gather x2, blocking collectives, per_device(): lax.all_gather(residual(place, parts, sinos, wts), 'zh', axis=0, tiled=True)  28.3 us
    ppermute x6, starting transfers between devices, with_sibling(): return (v, lax.ppermute(v, 'c', [(0, 1), (1, 0)]))  19.7 us
    ppermute x3, starting transfers between devices, far_send(): lax.ppermute(v, 'zh', [(i, (i + j) % 4) for i in range(4)])  13 us
    pallas_call x2, Pallas kernels, project(): pl.pallas_call(first_project_kernel if first else project_kernel, out_sha...  8.07 us
    ppermute x3, waiting for transfers between devices, far_send(): lax.ppermute(v, 'zh', [(i, (i + j) % 4) for i in range(4)])  7.83 us
  transfers between devices with their start and end apart: 10, of which 4 were waited for; matrix products, arithmetic and copies ran while one was open for 0% of the time, Pallas kernels for 0%

profile of v7, /device:TPU:1, one launch (start us, length us, event | category | flops | bytes accessed | tf_op | source)
XLA Modules:
  0.0 266.1 jit_solution(1753279523054941594)
XLA Ops:
  0.0 8.8 %collective-permute-start.8 = (bf16[32,128,128]{2,1,0:T(8,128)(2,1)}, bf16[32,128,128]{2,1,0:T(8,128)(2,1)S(1)}, u32[]{:S(2)}, u32[]{:S(2)}) collective-permute-start(bf16[32,128,128]{2,1,0:T(8,128)(2,1)} %bitcast.15), channel_id=1, source_target_pairs={{0,8},{8,0},{1,9},{9,1},{2,10},{10,2},{3,11},{11,3},{4,12},{12,4},... | collective-permute-start | bytes 3145736 | tf_op jit(solution)/shard_map/ppermute | solution.py:270
  8.8 1.9 collective-permute-start.7
  10.7 2.4 collective-permute-start
  13.1 0.6 pad_add_fusion.1.place
  13.7 0.4 collective-permute-done.e1
  14.2 0.5 copy-done.10
  14.7 0.2 copy-done.4
  14.9 1.0 copy-done.1
  15.8 5.8 %shard_map.64 = bf16[256,32,128]{2,1,0:T(8,128)(2,1)} custom-call(s32[3]{0:T(128)} %pad_add_fusion.1.place, s32[3,1,32]{2,1,0:T(1,128)} %bitcast.27, s32[3,1,32]{2,1,0:T(1,128)} %copy-done.10, bf16[16,64,128]{2,1,0:T(8,128)(2,1)} %refs_0_.1, bf16[16,64,128]{2,1,0:T(8,128)(2,1)} %copy-done.4, bf16[32,128,128]{2,1,0:T(8,128)(2,1)} %bitcast.16, ...), custom_call_target="tpu_custom_call" | custom-call | tf_op jit(solution)/shard_map/pallas_call | solution.py:85
  21.6 0.0 copy-start.6
  21.6 0.0 copy-start.7
  21.6 0.0 copy-start.12
  21.7 3.7 %all-to-all-start = ((bf16[256,32,128]{2,1,0:T(8,128)(2,1)}), bf16[256,32,128]{2,1,0:T(8,128)(2,1)S(1)}, u32[]{:S(2)}, u32[]{:S(2)}) async-start(bf16[256,32,128]{2,1,0:T(8,128)(2,1)} %shard_map.64), calls=%async_computation | async-start | bytes 4194304 | tf_op jit(solution)/shard_map/all_to_all | solution.py:262
  25.4 2.2 collective-permute-start.2
  27.7 2.1 collective-permute-start.3
  29.8 2.2 collective-permute-start.1
  32.0 0.8 collective-permute-done.1
  32.8 6.9 %collective-permute-start.6 = (s32[2,2,64]{2,1,0:T(2,128)S(1)}, s32[2,2,64]{2,1,0:T(2,128)S(1)}, u32[]{:S(2)}, u32[]{:S(2)}) collective-permute-start(s32[2,2,64]{2,1,0:T(2,128)S(1)} %pad_add_fusion.m0), channel_id=1, source_target_pairs={{0,96},{32,0},{64,32},{96,64},{1,97},{33,1},{65,33},{97,65},{2,98}... | collective-permute-start | bytes 3080 | tf_op jit(solution)/shard_map/ppermute | solution.py:266
  39.7 1.9 collective-permute-start.5
  41.7 4.2 %collective-permute-start.4 = (s32[2,2,64]{2,1,0:T(2,128)S(1)}, s32[2,2,64]{2,1,0:T(2,128)S(1)}, u32[]{:S(2)}, u32[]{:S(2)}) collective-permute-start(s32[2,2,64]{2,1,0:T(2,128)S(1)} %pad_add_fusion.m0), channel_id=1, source_target_pairs={{0,32},{32,64},{64,96},{96,0},{1,33},{33,65},{65,97},{97,1},{2,34}... | collective-permute-start | bytes 3080 | tf_op jit(solution)/shard_map/ppermute | solution.py:266
  45.9 7.4 %collective-permute-done.5.m2 = s32[2,2,64]{2,1,0:T(2,128)S(1)} collective-permute-done((s32[2,2,64]{2,1,0:T(2,128)S(1)}, s32[2,2,64]{2,1,0:T(2,128)S(1)}, u32[]{:S(2)}, u32[]{:S(2)}) %collective-permute-start.5) | collective-permute-done | bytes 1056 | tf_op jit(solution)/shard_map/ppermute | solution.py:266
  53.4 0.4 collective-permute-done.4.m1
  53.8 1.1 shard_map.65
  54.9 16.4 %all_to_all.50.parts = bf16[64,32,128]{2,1,0:T(8,128)(2,1)S(1)} all-to-all(bf16[64,32,128]{2,1,0:T(8,128)(2,1)S(1)} %shard_map.65), channel_id=1, replica_groups=mesh['x'=4,'zh'=4,'zl'=2,'c'=2,'y'=8] {'zh'}, dimensions={0} | all-to-all | bytes 1048576 | tf_op jit(solution)/shard_map/all_to_all | solution.py:262
  71.3 0.7 shard_map.66
  71.9 14.0 %all_gather.6.res = bf16[64,32,128]{2,1,0:T(8,128)(2,1)S(1)} all-gather(bf16[16,32,128]{2,1,0:T(8,128)(2,1)S(1)} %shard_map.66), channel_id=1, replica_groups=mesh['x'=4,'zh'=4,'zl'=2,'c'=2,'y'=8] {'zh'}, dimensions={0}, use_global_device_ids=true | all-gather | bytes 655360 | tf_op jit(solution)/shard_map/all_gather | solution.py:291
  85.9 1.3 shard_map.67
  87.2 0.0 copy-start
  87.2 0.0 copy-start.9
  87.2 27.6 %all_to_all.51.reply = bf16[256,32,128]{2,1,0:T(8,128)(2,1)S(1)} all-to-all(bf16[256,32,128]{2,1,0:T(8,128)(2,1)S(1)} %shard_map.67), channel_id=1, replica_groups=mesh['x'=4,'zh'=4,'zl'=2,'c'=2,'y'=8] {'x','zl'}, dimensions={0} | all-to-all | bytes 4194304 | tf_op jit(solution)/shard_map/all_to_all | solution.py:262
  114.9 0.0 copy-start.3
  114.9 1.3 shard_map.68
  116.2 15.9 %all_to_all.52.got = bf16[32,32,128]{2,1,0:T(8,128)(2,1)S(1)} all-to-all(bf16[32,32,128]{2,1,0:T(8,128)(2,1)S(1)} %shard_map.68), channel_id=1, replica_groups=mesh['x'=4,'zh'=4,'zl'=2,'c'=2,'y'=8] {'y'}, dimensions={0} | all-to-all | bytes 524288 | tf_op jit(solution)/shard_map/all_to_all | solution.py:262
  132.1 0.6 shard_map.69
  132.7 11.7 %all_to_all.53.image = bf16[32,32,128]{2,1,0:T(8,128)(2,1)S(1)} all-to-all(bf16[32,32,128]{2,1,0:T(8,128)(2,1)S(1)} %get-tuple-element.17), channel_id=1, replica_groups=mesh['x'=4,'zh'=4,'zl'=2,'c'=2,'y'=8] {'y'}, dimensions={0} | all-to-all | bytes 524288 | tf_op jit(solution)/shard_map/all_to_all | solution.py:262
  144.5 2.3 shard_map.70
  146.8 20.7 %all_to_all.54.got = bf16[256,32,128]{2,1,0:T(8,128)(2,1)S(1)} all-to-all(bf16[256,32,128]{2,1,0:T(8,128)(2,1)S(1)} %shard_map.70), channel_id=1, replica_groups=mesh['x'=4,'zh'=4,'zl'=2,'c'=2,'y'=8] {'x','zl'}, dimensions={0} | all-to-all | bytes 4194304 | tf_op jit(solution)/shard_map/all_to_all | solution.py:262
  167.5 1.2 shard_map.71
  168.7 17.2 %all_to_all.55.parts = bf16[64,32,128]{2,1,0:T(8,128)(2,1)S(1)} all-to-all(bf16[64,32,128]{2,1,0:T(8,128)(2,1)S(1)} %shard_map.71), channel_id=1, replica_groups=mesh['x'=4,'zh'=4,'zl'=2,'c'=2,'y'=8] {'zh'}, dimensions={0} | all-to-all | bytes 1048576 | tf_op jit(solution)/shard_map/all_to_all | solution.py:262
  185.9 0.7 shard_map.72
  186.5 14.3 %all_gather.7.res = bf16[64,32,128]{2,1,0:T(8,128)(2,1)S(1)} all-gather(bf16[16,32,128]{2,1,0:T(8,128)(2,1)S(1)} %shard_map.72), channel_id=1, replica_groups=mesh['x'=4,'zh'=4,'zl'=2,'c'=2,'y'=8] {'zh'}, dimensions={0}, use_global_device_ids=true | all-gather | bytes 655360 | tf_op jit(solution)/shard_map/all_gather | solution.py:291
  200.9 1.3 shard_map.73
  202.1 22.0 %all_to_all.56.reply = bf16[256,32,128]{2,1,0:T(8,128)(2,1)S(1)} all-to-all(bf16[256,32,128]{2,1,0:T(8,128)(2,1)S(1)} %shard_map.73), channel_id=1, replica_groups=mesh['x'=4,'zh'=4,'zl'=2,'c'=2,'y'=8] {'x','zl'}, dimensions={0} | all-to-all | bytes 4194304 | tf_op jit(solution)/shard_map/all_to_all | solution.py:262
  224.1 1.3 shard_map.74
  225.4 11.7 %all_to_all.57.got = bf16[32,32,128]{2,1,0:T(8,128)(2,1)S(1)} all-to-all(bf16[32,32,128]{2,1,0:T(8,128)(2,1)S(1)} %shard_map.74), channel_id=1, replica_groups=mesh['x'=4,'zh'=4,'zl'=2,'c'=2,'y'=8] {'y'}, dimensions={0} | all-to-all | bytes 524288 | tf_op jit(solution)/shard_map/all_to_all | solution.py:262
  237.2 0.6 shard_map.75
  237.7 27.7 %all_to_all.58.got = bf16[32,32,128]{2,1,0:T(8,128)(2,1)S(1)} all-to-all(bf16[32,32,128]{2,1,0:T(8,128)(2,1)S(1)} %shard_map.75), channel_id=1, replica_groups=mesh['x'=4,'zh'=4,'zl'=2,'c'=2,'y'=8] {'y','c'}, dimensions={0} | all-to-all | bytes 524288 | tf_op jit(solution)/shard_map/all_to_all | solution.py:262
  265.4 0.7 shard_map.76
  (24 shorter events, 0.1 us)
Async XLA Ops:
  0.0 14.2 %collective-permute-start.8 = (bf16[32,128,128]{2,1,0:T(8,128)(2,1)}, bf16[32,128,128]{2,1,0:T(8,128)(2,1)S(1)}, u32[]{:S(2)}, u32[]{:S(2)}) collective-permute-start(bf16[32,128,128]{2,1,0:T(8,128)(2,1)} %bitcast.15), channel_id=1, source_target_pairs={{0,8},{8,0},{1,9},{9,1},{2,10},{10,2},{3,11},{11,3},{4,12},{12,4},... | collective-permute-start | bytes 3145736 | tf_op jit(solution)/shard_map/ppermute | solution.py:270
  8.8 5.4 %collective-permute-start.7 = (bf16[16,64,128]{2,1,0:T(8,128)(2,1)}, bf16[16,64,128]{2,1,0:T(8,128)(2,1)S(1)}, u32[]{:S(2)}, u32[]{:S(2)}) collective-permute-start(bf16[16,64,128]{2,1,0:T(8,128)(2,1)} %refs_0_.1), channel_id=1, source_target_pairs={{0,8},{8,0},{1,9},{9,1},{2,10},{10,2},{3,11},{11,3},{4,12},{12,4},... | collective-permute-start | bytes 786440 | tf_op jit(solution)/shard_map/ppermute | solution.py:270
  10.7 3.4 %collective-permute-start = (s32[3,1,32]{2,1,0:T(1,128)}, s32[3,1,32]{2,1,0:T(1,128)S(1)}, u32[]{:S(2)}, u32[]{:S(2)}) collective-permute-start(s32[3,1,32]{2,1,0:T(1,128)} %bitcast.26), channel_id=1, source_target_pairs={{0,8},{8,0},{1,9},{9,1},{2,10},{10,2},{3,11},{11,3},{4,12},{12,4},... | collective-permute-start | bytes 1160 | tf_op jit(solution)/shard_map/ppermute | solution.py:270
  14.1 0.5 copy-start.10
  14.1 0.7 copy-start.4
  14.8 1.0 copy-start.1
  21.6 3.8 %copy-start.6 = (bf16[1,8,64,128]{3,2,1,0:T(8,128)(2,1)S(1)}, bf16[1,8,64,128]{3,2,1,0:T(8,128)(2,1)}, u32[]{:S(2)}) copy-start(bf16[1,8,64,128]{3,2,1,0:T(8,128)(2,1)} %param.10) | copy-start | bytes 393220
  21.6 6.1 %copy-start.7 = (bf16[1,8,64,128]{3,2,1,0:T(8,128)(2,1)S(1)}, bf16[1,8,64,128]{3,2,1,0:T(8,128)(2,1)}, u32[]{:S(2)}) copy-start(bf16[1,8,64,128]{3,2,1,0:T(8,128)(2,1)} %param.11) | copy-start | bytes 393220
  21.6 8.1 %copy-start.12 = (s32[1,1,64,2]{2,3,1,0:T(2,128)S(1)}, s32[1,1,64,2]{2,3,1,0:T(2,128)}, u32[]{:S(2)}) copy-start(s32[1,1,64,2]{2,3,1,0:T(2,128)} %param.9) | copy-start | bytes 1540
  21.6 32.1 %copy-start.8 = (s32[3]{0:T(128)S(1)}, s32[3]{0:T(128)}, u32[]{:S(2)}) copy-start(s32[3]{0:T(128)} %pad_add_fusion.1.place) | copy-start | bytes 40
  21.7 32.1 %all-to-all-start = ((bf16[256,32,128]{2,1,0:T(8,128)(2,1)}), bf16[256,32,128]{2,1,0:T(8,128)(2,1)S(1)}, u32[]{:S(2)}, u32[]{:S(2)}) async-start(bf16[256,32,128]{2,1,0:T(8,128)(2,1)} %shard_map.64), calls=%async_computation | async-start | bytes 4194304 | tf_op jit(solution)/shard_map/all_to_all | solution.py:262
  25.4 7.4 %collective-permute-start.2 = (bf16[8,64,128]{2,1,0:T(8,128)(2,1)S(1)}, bf16[8,64,128]{2,1,0:T(8,128)(2,1)S(1)}, u32[]{:S(2)}, u32[]{:S(2)}) collective-permute-start(bf16[8,64,128]{2,1,0:T(8,128)(2,1)S(1)} %bitcast.20), channel_id=1, source_target_pairs={{0,8},{8,0},{1,9},{9,1},{2,10},{10,2},{3,11},{11,3},{4,12},{12,4},... | collective-permute-start | bytes 393224 | tf_op jit(solution)/shard_map/ppermute | solution.py:270
  27.7 5.2 %collective-permute-start.3 = (bf16[8,64,128]{2,1,0:T(8,128)(2,1)S(1)}, bf16[8,64,128]{2,1,0:T(8,128)(2,1)S(1)}, u32[]{:S(2)}, u32[]{:S(2)}) collective-permute-start(bf16[8,64,128]{2,1,0:T(8,128)(2,1)S(1)} %bitcast.23), channel_id=1, source_target_pairs={{0,8},{8,0},{1,9},{9,1},{2,10},{10,2},{3,11},{11,3},{4,12},{12,4},... | collective-permute-start | bytes 393224 | tf_op jit(solution)/shard_map/ppermute | solution.py:270
  29.8 3.1 %collective-permute-start.1 = (s32[2,64]{1,0:T(2,128)S(1)}, s32[2,64]{1,0:T(2,128)S(1)}, u32[]{:S(2)}, u32[]{:S(2)}) collective-permute-start(s32[2,64]{1,0:T(2,128)S(1)} %bitcast.31), channel_id=1, source_target_pairs={{0,8},{8,0},{1,9},{9,1},{2,10},{10,2},{3,11},{11,3},{4,12},{12,4},... | collective-permute-start | bytes 1544 | tf_op jit(solution)/shard_map/ppermute | solution.py:270
  32.8 13.1 %collective-permute-start.6 = (s32[2,2,64]{2,1,0:T(2,128)S(1)}, s32[2,2,64]{2,1,0:T(2,128)S(1)}, u32[]{:S(2)}, u32[]{:S(2)}) collective-permute-start(s32[2,2,64]{2,1,0:T(2,128)S(1)} %pad_add_fusion.m0), channel_id=1, source_target_pairs={{0,96},{32,0},{64,32},{96,64},{1,97},{33,1},{65,33},{97,65},{2,98}... | collective-permute-start | bytes 3080 | tf_op jit(solution)/shard_map/ppermute | solution.py:266
  39.7 13.6 %collective-permute-start.5 = (s32[2,2,64]{2,1,0:T(2,128)S(1)}, s32[2,2,64]{2,1,0:T(2,128)S(1)}, u32[]{:S(2)}, u32[]{:S(2)}) collective-permute-start(s32[2,2,64]{2,1,0:T(2,128)S(1)} %pad_add_fusion.m0), channel_id=1, source_target_pairs={{0,64},{32,96},{64,0},{96,32},{1,65},{33,97},{65,1},{97,33},{2,66}... | collective-permute-start | bytes 3080 | tf_op jit(solution)/shard_map/ppermute | solution.py:266
  41.7 12.1 %collective-permute-start.4 = (s32[2,2,64]{2,1,0:T(2,128)S(1)}, s32[2,2,64]{2,1,0:T(2,128)S(1)}, u32[]{:S(2)}, u32[]{:S(2)}) collective-permute-start(s32[2,2,64]{2,1,0:T(2,128)S(1)} %pad_add_fusion.m0), channel_id=1, source_target_pairs={{0,32},{32,64},{64,96},{96,0},{1,33},{33,65},{65,97},{97,1},{2,34}... | collective-permute-start | bytes 3080 | tf_op jit(solution)/shard_map/ppermute | solution.py:266
  87.2 27.7 %copy-start = (bf16[1,1,32,128,128]{4,3,2,1,0:T(8,128)(2,1)S(1)}, bf16[1,1,32,128,128]{4,3,2,1,0:T(8,128)(2,1)}, u32[]{:S(2)}) copy-start(bf16[1,1,32,128,128]{4,3,2,1,0:T(8,128)(2,1)} %param.7) | copy-start | bytes 3145732
  87.2 27.7 %copy-start.2 = (bf16[32,128,128]{2,1,0:T(8,128)(2,1)S(1)}, bf16[32,128,128]{2,1,0:T(8,128)(2,1)}, u32[]{:S(2)}) copy-start(bf16[32,128,128]{2,1,0:T(8,128)(2,1)} %copy-done.1) | copy-start | bytes 3145732
  87.2 27.7 %copy-start.9 = (s32[1,1,32,3]{2,1,3,0:T(1,128)S(1)}, s32[1,1,32,3]{2,1,3,0:T(1,128)}, u32[]{:S(2)}) copy-start(s32[1,1,32,3]{2,1,3,0:T(1,128)} %param.8) | copy-start | bytes 1156
  87.2 27.7 %copy-start.11 = (s32[3,1,32]{2,1,0:T(1,128)S(1)}, s32[3,1,32]{2,1,0:T(1,128)}, u32[]{:S(2)}) copy-start(s32[3,1,32]{2,1,0:T(1,128)} %copy-done.10) | copy-start | bytes 1156
  114.9 17.3 %copy-start.3 = (bf16[16,64,128]{2,1,0:T(8,128)(2,1)S(1)}, bf16[16,64,128]{2,1,0:T(8,128)(2,1)}, u32[]{:S(2)}) copy-start(bf16[16,64,128]{2,1,0:T(8,128)(2,1)} %refs_0_.1) | copy-start | bytes 786436
  114.9 17.3 %copy-start.5 = (bf16[16,64,128]{2,1,0:T(8,128)(2,1)S(1)}, bf16[16,64,128]{2,1,0:T(8,128)(2,1)}, u32[]{:S(2)}) copy-start(bf16[16,64,128]{2,1,0:T(8,128)(2,1)} %copy-done.4) | copy-start | bytes 786436
